TPU v7x, 32 devices: a whole 2x2x4 slice. The times are simulated.
32 devices in a mesh: seq: 8 (over z, y), head: 4 (over x, core).
Axes of the slice: x: 2, y: 2, z: 4, core: 2. Of those that a mesh axis runs over, the one named last changes fastest.
Arguments:
- tiles: bfloat16 [6, 4096, 768], P(None, ('seq', 'head')), may hold values from -6 to 6
- coords: int32 [6, 4096, 2], P(None, ('seq', 'head')), may hold values from 0 to 255
- lengths: int32 [6], replicated, may hold values from 1024 to 4096, as said below
- padding_mask: int32 [6, 4096], replicated, may hold values from 0 to 1, as said below
- ln1_gain: float32 [768], replicated, may hold values from 0.1 to 1.9
- ln1_bias: float32 [768], replicated, may hold values from -4 to 4
- query_key_value_weight: bfloat16 [768, 3, 768], P(None, None, 'head'), may hold values from -0.21875 to 0.21875
- qv_bias: float32 [2, 768], P(None, 'head'), may hold values from -6 to 6
- attention_output_weight: bfloat16 [768, 768], P('head'), may hold values from -4 to 4
- attention_output_bias: float32 [768], replicated, may hold values from -4 to 4
- ln2_gain: float32 [768], replicated, may hold values from 0.1 to 1.9
- ln2_bias: float32 [768], replicated, may hold values from -4 to 4
- mlp_entry_matrix: bfloat16 [768, 3072], P(None, 'head'), may hold values from -0.21875 to 0.21875
- mlp_entry_offset: float32 [3072], P('head'), may hold values from -6 to 6
- feed_output_weight: bfloat16 [3072, 768], P('head'), may hold values from -0.109375 to 0.109375
- feed_output_bias: float32 [768], replicated, may hold values from -4 to 4
- cotangent: bfloat16 [6, 4096, 768], P(None, ('seq', 'head')), may hold values from -6 to 6
Outputs:
- output: bfloat16 [6, 4096, 768], P(None, ('seq', 'head'))
- tiles_grad: bfloat16 [6, 4096, 768], P(None, ('seq', 'head'))
- ln1_gain_grad: float32 [768], replicated
- ln1_bias_grad: float32 [768], replicated
- w_qkv_grad: float32 [768, 3, 768], P('seq', None, 'head')
- qv_bias_grad: float32 [2, 768], P(None, 'head')
- w_out_grad: float32 [768, 768], P('head', 'seq')
- out_bias_grad: float32 [768], replicated
- ln2_gain_grad: float32 [768], replicated
- ln2_bias_grad: float32 [768], replicated
- w_fc1_grad: float32 [768, 3072], P('seq', 'head')
- fc1_bias_grad: float32 [3072], P('head')
- w_fc2_grad: float32 [3072, 768], P('head', 'seq')
- fc2_bias_grad: float32 [768], replicated
Inputs may be any that keep to these rules, and one draw needn't show every extreme that they name: `lengths`: one slide, drawn from the seed, uses all 4096 tiles; each other slide uses 4096 // 4 or more. `padding_mask`: the first 16 tiles of every slide are marked 1.
All inputs are finite; a program needn't handle non-finite values.
Results may differ from a plain program's by a relative error of at most 0.02.
Values may be sent and summed in bfloat16 or wider, within the bound.
No kernel may reach another device: no remote copies, remote signals or barrier semaphores. Data moves between devices by JAX's collectives and lax.ppermute only.
A program may use at most 384 MiB of HBM per device.

v0:
```python
from functools import partial
import math

import jax
import jax.numpy as jnp
from jax import lax
from jax.sharding import PartitionSpec as P

HEADS = 16
FF = 3072
SEG2 = 5792
RATIO = 16


NEG = -10000.0
FLOOR = -1e30
EPS = 1e-05


def partner(x, axis, stride):
    return lax.ppermute(x, axis, [(i, i ^ 1 << stride) for i in range(lax.axis_size(axis))])


def layer_norm(value, gain, shift):
    mean = jnp.mean(value, axis=-1, keepdims=True)
    centered = value - mean
    var = jnp.mean(centered * centered, axis=-1, keepdims=True)
    return centered * lax.rsqrt(var + EPS) * gain + shift


def position_table(coords, width):
    quarter = width // 4
    freq = jnp.exp(-jnp.log(10000.0) * jnp.arange(quarter, dtype=jnp.float32) / quarter)
    col_angle = coords[..., 0:1].astype(jnp.float32) * freq
    row_angle = coords[..., 1:2].astype(jnp.float32) * freq
    return jnp.concatenate(
        [jnp.sin(col_angle), jnp.cos(col_angle), jnp.sin(row_angle), jnp.cos(row_angle)], axis=-1
    )


def mask_shape(value, chosen):
    return (1, 1, chosen.shape[0]) + (1,) * (value.ndim - 4) + (chosen.shape[1], 1)


def pick(value, chosen):
    rate = chosen.shape[0]
    split = value.reshape((value.shape[0], value.shape[1] // rate, rate) + value.shape[2:])
    return jnp.sum(
        jnp.where(chosen.reshape(mask_shape(value, chosen)), split, jnp.zeros((), value.dtype)),
        axis=2,
    )


def spread(value, chosen):
    rate = chosen.shape[0]
    full = jnp.where(
        chosen.reshape(mask_shape(value, chosen)),
        jnp.expand_dims(value, 2),
        jnp.zeros((), value.dtype),
    )
    return full.reshape((value.shape[0], value.shape[1] * rate) + value.shape[2:])


def scores_of(query, keys, bias, pair, scale):
    raw = jnp.einsum("qhe,khe->hqk", query, keys, preferred_element_type=jnp.float32)
    return raw * scale + jnp.transpose(bias)[:, None, :] + pair


def attend_forward(query, keys, values, bias, pair, scale):
    scores = scores_of(query, keys, bias, pair, scale)
    total = jax.nn.logsumexp(scores, axis=-1)
    probs = jnp.exp(scores - total[..., None]).astype(jnp.bfloat16)
    result = jnp.einsum("hqk,khe->qhe", probs, values, preferred_element_type=jnp.float32)
    return (result, jnp.transpose(total)[..., None])


def attend_backward(query, keys, values, bias, pair, total, grad_out, grad_total, scale):
    scores = scores_of(query, keys, bias, pair, scale)
    probs = jnp.exp(scores - jnp.transpose(total[..., 0])[..., None])
    grad_probs = jnp.einsum("qhe,khe->hqk", grad_out, values, preferred_element_type=jnp.float32)
    delta = jnp.sum(probs * grad_probs, axis=-1) - jnp.transpose(grad_total[..., 0])
    grad_scores = (probs * (grad_probs - delta[..., None])).astype(jnp.bfloat16)
    grad_query = (
        jnp.einsum("hqk,khe->qhe", grad_scores, keys, preferred_element_type=jnp.float32) * scale
    )
    grad_keys = (
        jnp.einsum("hqk,qhe->khe", grad_scores, query, preferred_element_type=jnp.float32) * scale
    )
    grad_values = jnp.einsum(
        "hqk,qhe->khe", probs.astype(jnp.bfloat16), grad_out, preferred_element_type=jnp.float32
    )
    return (grad_query, grad_keys, grad_values)


def forward_slide(args, pair, scale):
    q_one, kv_one, bias_one = args
    return attend_forward(q_one, kv_one[:, 0], kv_one[:, 1], bias_one, pair, scale)


def backward_slide(args, pair, scale):
    q_one, kv_one, bias_one, total_one, grad_one, grad_total_one = args
    return attend_backward(
        q_one,
        kv_one[:, 0],
        kv_one[:, 1],
        bias_one,
        pair,
        total_one,
        grad_one,
        grad_total_one,
        scale,
    )


def on_device(
    tiles,
    coords,
    lengths,
    padding_mask,
    ln1_gain,
    ln1_bias,
    query_key_value_weight,
    qv_bias,
    attention_output_weight,
    attention_output_bias,
    ln2_gain,
    ln2_bias,
    mlp_entry_matrix,
    mlp_entry_offset,
    feed_output_weight,
    feed_output_bias,
    cotangent,
):
    slides, rows, width = tiles.shape
    head_count = lax.axis_size("head")
    local_width = query_key_value_weight.shape[2]
    local_heads = local_width * HEADS // width
    head_dim = width // HEADS
    hidden_local = mlp_entry_matrix.shape[1]
    scale = 1.0 / math.sqrt(head_dim)
    seg_rows = rows * head_count
    total_len = padding_mask.shape[1]
    seq_index = lax.axis_index("seq")
    head_index = lax.axis_index("head")
    dilations = (RATIO // 8, RATIO // 4, RATIO // 2, RATIO)
    reaches = (SEG2, total_len, total_len, total_len)
    positions = jnp.arange(total_len, dtype=jnp.int32)
    valid = (positions[None, :] < lengths[:, None]) & (padding_mask == 1)
    own_valid = lax.dynamic_slice_in_dim(valid, seq_index * seg_rows, seg_rows, 1)
    mate_valid = lax.dynamic_slice_in_dim(valid, (seq_index ^ 1) * seg_rows, seg_rows, 1)
    near_valid = jnp.concatenate([own_valid, mate_valid], axis=1)
    near_bias = jnp.broadcast_to(
        jnp.where(near_valid, 0.0, NEG)[..., None], (slides, 2 * seg_rows, local_heads)
    )
    global_heads = head_index * local_heads + jnp.arange(local_heads, dtype=jnp.int32)
    chosens = []
    far_biases = []
    selects = []
    pair_masks = []
    for dilation, reach in zip(dilations, reaches):
        chosen = (
            jnp.arange(dilation, dtype=jnp.int32)[:, None] == (global_heads % dilation)[None, :]
        )
        chosens.append(chosen)
        far_valid = jnp.any(
            valid.reshape(slides, total_len // dilation, dilation)[..., None] & chosen[None, None],
            axis=2,
        )
        far_biases.append(jnp.where(far_valid, 0.0, NEG))
        selects.append(
            (
                (jnp.arange(seg_rows, dtype=jnp.int32) % dilation)[:, None]
                == (global_heads % dilation)[None, :]
            )[None, :, :, None]
        )
        query_places = seq_index * seg_rows + dilation * jnp.arange(
            seg_rows // dilation, dtype=jnp.int32
        )
        key_places = dilation * jnp.arange(total_len // dilation, dtype=jnp.int32)
        pair_masks.append(
            jnp.where((query_places // reach)[:, None] == (key_places // reach)[None, :], 0.0, NEG)
        )
    base = tiles.astype(jnp.float32) + position_table(coords, width)
    first_normalized = layer_norm(base, ln1_gain, ln1_bias).astype(jnp.bfloat16)
    initial_tokens, cotangent_rows = (
        lax.all_gather(first_normalized, "head", axis=1, tiled=True),
        lax.all_gather(cotangent, "head", axis=1, tiled=True),
    )
    packed_projection_matrix = query_key_value_weight.reshape(width, 3 * local_width)
    triple_bias = jnp.concatenate([qv_bias[0], jnp.zeros_like(qv_bias[0]), qv_bias[1]])
    query_key_value = (
        jnp.einsum(
            "hmq,qn->hmn",
            initial_tokens,
            packed_projection_matrix,
            preferred_element_type=jnp.float32,
        )
        + triple_bias
    ).astype(jnp.bfloat16)
    query_key_value = query_key_value.reshape(slides, seg_rows, 3, local_heads, head_dim)
    query = query_key_value[:, :, 0]
    key_value = query_key_value[:, :, 1:3]
    mate_kv = partner(key_value, "seq", 0)
    near_kv = jnp.concatenate([key_value, mate_kv], axis=1)

    def collect(piece):
        return tuple((pick(piece, chosens[index]) for index in range(4)))

    far_kvs = collect(lax.all_gather(key_value, "seq", axis=1, tiled=True))
    far_queries = [pick(query, chosen) for chosen in chosens]
    near_out, near_total = lax.map(
        partial(forward_slide, pair=0.0, scale=scale), (query, near_kv, near_bias)
    )
    far_results = []
    for index in range(4):
        far_results.append(
            lax.map(
                partial(forward_slide, pair=pair_masks[index], scale=scale),
                (far_queries[index], far_kvs[index], far_biases[index]),
            )
        )
    outs_full = [near_out] + [spread(far_results[index][0], chosens[index]) for index in range(4)]
    totals_full = [near_total] + [
        jnp.where(selects[index], spread(far_results[index][1], chosens[index]), FLOOR)
        for index in range(4)
    ]
    stacked = jnp.stack(totals_full)
    highest = jnp.max(stacked, axis=0)
    raised = jnp.exp(stacked - highest)
    weights = raised / jnp.sum(raised, axis=0)
    combined_output = weights[0] * outs_full[0]
    for index in range(1, 5):
        combined_output = combined_output + weights[index] * outs_full[index]
    combined_lowered = combined_output.reshape(slides, seg_rows, local_width).astype(jnp.bfloat16)
    attention_piece = jnp.einsum(
        "mua,ah->muh", combined_lowered, attention_output_weight, preferred_element_type=jnp.float32
    )
    attn_rows = lax.psum_scatter(
        attention_piece.astype(jnp.bfloat16), "head", scatter_dimension=1, tiled=True
    ).astype(jnp.float32)
    mid = base + (attn_rows + attention_output_bias)
    later_layernormed = layer_norm(mid, ln2_gain, ln2_bias).astype(jnp.bfloat16)
    later_tokens = lax.all_gather(later_layernormed, "head", axis=1, tiled=True)
    before_nonlinearity = (
        jnp.einsum(
            "awq,qd->awd", later_tokens, mlp_entry_matrix, preferred_element_type=jnp.float32
        )
        + mlp_entry_offset
    )
    hidden_activation = jax.nn.gelu(before_nonlinearity, approximate=False).astype(jnp.bfloat16)
    feedforward_piece = jnp.einsum(
        "nrv,vk->nrk", hidden_activation, feed_output_weight, preferred_element_type=jnp.float32
    )
    mlp_rows_sum = lax.psum_scatter(
        feedforward_piece.astype(jnp.bfloat16), "head", scatter_dimension=1, tiled=True
    ).astype(jnp.float32)
    output = mid + (mlp_rows_sum + feed_output_bias)
    cot_float = cotangent.astype(jnp.float32)
    grad_fc2_bias = jnp.sum(cot_float, axis=(0, 1))
    hidden_gradient = jnp.einsum(
        "tvq,cq->tvc", cotangent_rows, feed_output_weight, preferred_element_type=jnp.float32
    )
    feed_output_weight_gradient = jnp.einsum(
        "gar,gai->ri", hidden_activation, cotangent_rows, preferred_element_type=jnp.float32
    )
    gelu_pull = jax.vjp(lambda v: jax.nn.gelu(v, approximate=False), before_nonlinearity)[1]
    preactivation_gradient = gelu_pull(hidden_gradient)[0].astype(jnp.bfloat16)
    feed_input_weight_gradient = jnp.einsum(
        "vxr,vxm->rm", later_tokens, preactivation_gradient, preferred_element_type=jnp.float32
    )
    grad_fc1_bias = jnp.sum(preactivation_gradient.astype(jnp.float32), axis=(0, 1))
    second_backward = jnp.einsum(
        "ivo,go->ivg", preactivation_gradient, mlp_entry_matrix, preferred_element_type=jnp.float32
    )
    back2_rows = lax.psum_scatter(
        second_backward.astype(jnp.bfloat16), "head", scatter_dimension=1, tiled=True
    ).astype(jnp.float32)
    norm2_pull = jax.vjp(layer_norm, mid, ln2_gain, ln2_bias)[1]
    grad_mid_norm, grad_ln2_gain, grad_ln2_bias = norm2_pull(back2_rows)
    grad_mid = cot_float + grad_mid_norm
    grad_attn = grad_mid.astype(jnp.bfloat16)
    grad_out_bias = jnp.sum(grad_attn.astype(jnp.float32), axis=(0, 1))
    attention_rows_gradient = lax.all_gather(grad_attn, "head", axis=1, tiled=True)
    grad_w_out = jnp.einsum(
        "fub,fui->bi", combined_lowered, attention_rows_gradient, preferred_element_type=jnp.float32
    )
    grad_merged = jnp.einsum(
        "tpq,jq->tpj",
        attention_rows_gradient,
        attention_output_weight,
        preferred_element_type=jnp.float32,
    )
    grad_merged = grad_merged.reshape(slides, seg_rows, local_heads, head_dim)
    grad_parts = [weights[index] * grad_merged for index in range(5)]
    gaps = [
        weights[index]
        * jnp.sum(grad_merged * (outs_full[index] - combined_output), axis=-1, keepdims=True)
        for index in range(5)
    ]
    grad_near = grad_parts[0].astype(jnp.bfloat16)
    near_dq, near_dk, near_dv = lax.map(
        partial(backward_slide, pair=0.0, scale=scale),
        (query, near_kv, near_bias, near_total, grad_near, gaps[0]),
    )
    own_grad = jnp.stack([near_dk[:, :seg_rows], near_dv[:, :seg_rows]], axis=2)
    mate_grad = jnp.stack([near_dk[:, seg_rows:], near_dv[:, seg_rows:]], axis=2)
    returned = partner(mate_grad.astype(jnp.bfloat16), "seq", 0).astype(mate_grad.dtype)
    far_grads = []
    grad_query = near_dq
    for index in range(4):
        grad_far = pick(grad_parts[index + 1], chosens[index]).astype(jnp.bfloat16)
        grad_far_total = pick(gaps[index + 1], chosens[index])
        far_dq, far_dk, far_dv = lax.map(
            partial(backward_slide, pair=pair_masks[index], scale=scale),
            (
                far_queries[index],
                far_kvs[index],
                far_biases[index],
                far_results[index][1],
                grad_far,
                grad_far_total,
            ),
        )
        far_grads.append(jnp.stack([far_dk, far_dv], axis=2))
        grad_query = grad_query + spread(far_dq, chosens[index])
    far_back = (
        lax.psum_scatter(
            far_grads[0].astype(jnp.bfloat16), "seq", scatter_dimension=1, tiled=True
        ).astype(jnp.float32),
        lax.psum_scatter(
            far_grads[1].astype(jnp.bfloat16), "seq", scatter_dimension=1, tiled=True
        ).astype(jnp.float32),
        lax.psum_scatter(
            far_grads[2].astype(jnp.bfloat16), "seq", scatter_dimension=1, tiled=True
        ).astype(jnp.float32),
        lax.psum_scatter(
            far_grads[3].astype(jnp.bfloat16), "seq", scatter_dimension=1, tiled=True
        ).astype(jnp.float32),
    )
    grad_kv = own_grad + returned
    for index in range(4):
        grad_kv = grad_kv + spread(far_back[index], chosens[index])
    query_key_value_gradient = jnp.concatenate([grad_query[:, :, None], grad_kv], axis=2).astype(
        jnp.bfloat16
    )
    query_key_value_gradient = query_key_value_gradient.reshape(slides, seg_rows, 3 * local_width)
    grad_w_qkv = jnp.einsum(
        "ymt,yma->ta", initial_tokens, query_key_value_gradient, preferred_element_type=jnp.float32
    ).reshape(width, 3, local_width)
    bias_sums = jnp.sum(query_key_value_gradient.astype(jnp.float32), axis=(0, 1)).reshape(
        3, local_width
    )
    grad_qv = jnp.stack([bias_sums[0], bias_sums[2]])
    first_backward = jnp.einsum(
        "kgw,aw->kga",
        query_key_value_gradient,
        packed_projection_matrix,
        preferred_element_type=jnp.float32,
    )
    back1_rows = lax.psum_scatter(
        first_backward.astype(jnp.bfloat16), "head", scatter_dimension=1, tiled=True
    ).astype(jnp.float32)
    norm1_pull = jax.vjp(layer_norm, base, ln1_gain, ln1_bias)[1]
    grad_base_norm, grad_ln1_gain, grad_ln1_bias = norm1_pull(back1_rows)
    tiles_grad = (grad_mid + grad_base_norm).astype(jnp.bfloat16)
    w_qkv_grad, w_out_grad, w_fc1_grad, w_fc2_grad = (
        lax.psum_scatter(
            grad_w_qkv.astype(jnp.bfloat16), "seq", scatter_dimension=0, tiled=True
        ).astype(jnp.float32),
        lax.psum_scatter(
            grad_w_out.astype(jnp.bfloat16), "seq", scatter_dimension=1, tiled=True
        ).astype(jnp.float32),
        lax.psum_scatter(
            feed_input_weight_gradient.astype(jnp.bfloat16), "seq", scatter_dimension=0, tiled=True
        ).astype(jnp.float32),
        lax.psum_scatter(
            feed_output_weight_gradient.astype(jnp.bfloat16), "seq", scatter_dimension=1, tiled=True
        ).astype(jnp.float32),
    )
    shared = jnp.stack(
        [grad_ln1_gain, grad_ln1_bias, grad_out_bias, grad_ln2_gain, grad_ln2_bias, grad_fc2_bias]
    )
    qv_full = lax.dynamic_update_slice_in_dim(
        jnp.zeros((2, width), jnp.float32), grad_qv, head_index * local_width, 1
    )
    fc1_full = lax.dynamic_update_slice_in_dim(
        jnp.zeros((FF,), jnp.float32), grad_fc1_bias, head_index * hidden_local, 0
    )
    shared_sum, qv_sum, fc1_sum = lax.psum((shared, qv_full, fc1_full), ("seq", "head"))
    qv_bias_grad = lax.dynamic_slice_in_dim(qv_sum, head_index * local_width, local_width, 1)
    fc1_bias_grad = lax.dynamic_slice_in_dim(fc1_sum, head_index * hidden_local, hidden_local, 0)
    return (
        output.astype(jnp.bfloat16),
        tiles_grad,
        shared_sum[0],
        shared_sum[1],
        w_qkv_grad,
        qv_bias_grad,
        w_out_grad,
        shared_sum[2],
        shared_sum[3],
        shared_sum[4],
        w_fc1_grad,
        fc1_bias_grad,
        w_fc2_grad,
        shared_sum[5],
    )


def solution(mesh):
    placed = (
        P(None, ("seq", "head"), None),
        P(None, ("seq", "head"), None),
        P(),
        P(),
        P(),
        P(),
        P(None, None, "head"),
        P(None, "head"),
        P("head", None),
        P(),
        P(),
        P(),
        P(None, "head"),
        P("head"),
        P("head", None),
        P(),
        P(None, ("seq", "head"), None),
    )
    return jax.shard_map(
        on_device,
        mesh=mesh,
        in_specs=placed,
        out_specs=(
            P(None, ("seq", "head"), None),
            P(None, ("seq", "head"), None),
            P(),
            P(),
            P("seq", None, "head"),
            P(None, "head"),
            P("head", "seq"),
            P(),
            P(),
            P(),
            P("seq", "head"),
            P("head"),
            P("head", "seq"),
            P(),
        ),
        check_vma=False,
    )
```

profile of v0, /device:TPU:0, one launch (start us, length us, event | category | flops | bytes accessed | tf_op | source)
XLA Modules:
  0.0 2483.6 jit_solution(17398075650967164261)
XLA Ops:
  18.3 40.1 %all-gather.6.cloned.1.call-done = bf16[6,512,768]{2,1,0:T(8,128)(2,1)} async-done(((bf16[6,128,768]{2,1,0:T(8,128)(2,1)}), bf16[6,512,768]{2,1,0:T(8,128)(2,1)}) %all-gather.6.cloned.1.call-update) | async-done | bytes 4718608 | tf_op jit(solution)/shard_map/all_gather | solution.py:186
  165.6 116.6 %collective-permute-done = bf16[6,512,2,4,48]{1,4,3,2,0:T(8,128)(2,1)} collective-permute-done((bf16[6,512,2,4,48]{1,4,3,2,0:T(8,128)(2,1)S(1)}, bf16[6,512,2,4,48]{1,4,3,2,0:T(8,128)(2,1)}, u32[]{:S(2)}, u32[]{:S(2)}) %collective-permute-start) | collective-permute-done | bytes 2359328 | tf_op jit(solution)/shard_map/ppermute | solution.py:21
  287.7 56.6 %while.148 = (s32[]{:T(128)}, f32[6,512,4,48]{1,3,2,0:T(8,128)S(1)}, f32[6,512,4,1]{1,2,3,0:T(4,128)}, bf16[6,1024,2,4,48]{1,4,3,2,0:T(8,128)(2,1)}, bf16[6,512,4,48]{1,3,2,0:T(8,128)(2,1)}, /*index=5*/f32[6,1024,4]{1,2,0:T(4,128)}) while((s32[]{:T(128)}, f32[6,512,4,48]{1,3,2,0:T(8,128)S(1)}, f32[6,512,4,1]{1,2,3,0:T(4,128)}, ...), condition=%wide.region_5.6_spmd.clone, body=%wide.region_2.5_spmd.sunk.clone | while | flops 425738240 | bytes 28296272 | solution.py:211
  345.8 134.8 %all-gather.8.cloned.1.call-done = bf16[6,4096,2,4,48]{1,4,3,2,0:T(8,128)(2,1)} async-done(((bf16[6,512,2,4,48]{1,4,3,2,0:T(8,128)(2,1)}), bf16[6,4096,2,4,48]{1,4,3,2,0:T(8,128)(2,1)}) %all-gather.8.cloned.1.call-update) | async-done | bytes 18874384 | tf_op jit(solution)/shard_map/all_gather | solution.py:209
  480.6 42.6 %copy.478 = bf16[6,4096,2,4,48]{4,1,3,2,0:T(8,128)(2,1)} copy(bf16[6,4096,2,4,48]{1,4,3,2,0:T(8,128)(2,1)} %all-gather.8.cloned.1.call-done) | data formatting | bytes 37748736 | tf_op jit(solution)/shard_map/all_gather | solution.py:209
  523.2 40.5 %select_reduce_fusion = bf16[6,256,2,4,48]{4,1,3,2,0:T(8,128)(2,1)} fusion(pred[16,4]{0,1:T(4,128)(4,1)} %copy-done.110, bf16[6,4096,2,4,48]{4,1,3,2,0:T(8,128)(2,1)} %copy.478), kind=kLoop, calls=%fused_computation.306 | loop fusion | flops 18284544 | bytes 20054080 | tf_op jit(solution)/shard_map/reduce_sum | solution.py:48
  563.7 41.6 %fusion.201 = bf16[6,512,2,4,48]{4,1,3,2,0:T(8,128)(2,1)} fusion(bf16[6,4096,2,4,48]{4,1,3,2,0:T(8,128)(2,1)} %copy.478, pred[8,4]{0,1:T(4,128)(4,1)} %copy-done.112), kind=kLoop, calls=%fused_computation.305 | loop fusion | flops 17694720 | bytes 21233696 | tf_op jit(solution)/shard_map/reduce_sum | solution.py:48
  605.3 88.3 %select_reduce_fusion.1 = bf16[6,1024,2,4,48]{4,1,3,2,0:T(8,128)(2,1)} fusion(bf16[6,1024,4,2,4,48]{5,2,1,4,3,0:T(4,128)(2,1)} %bitcast.1075, pred[4,4]{0,1:T(4,128)(4,1)S(1)} %copy-done.120), kind=kLoop, calls=%fused_computation.307 | loop fusion | flops 16515072 | bytes 23592976 | tf_op jit(solution)/shard_map/reduce_sum | solution.py:48
  705.6 27.4 %while.151 = (s32[]{:T(128)}, f32[6,128,4,48]{1,3,2,0:T(8,128)S(1)}, f32[6,128,4,1]{1,2,3,0:T(4,128)S(1)}, bf16[6,1024,2,4,48]{1,4,3,2,0:T(8,128)(2,1)}, bf16[6,...) while((s32[]{:T(128)}, f32[6,128,4,48]{1,3,2,0:T(8,128)S(1)}, ...), condition=%wide.region_19.20_spmd.clone.clone, body=%wide.region_16.19_spmd.clone.sunk.clone | while | flops 105123840 | bytes 9925733 | solution.py:217
  743.8 26.0 %while.152 = (s32[]{:T(128)}, f32[6,64,4,48]{1,3,2,0:T(8,128)}, f32[6,64,4,1]{1,2,3,0:T(4,128)}, bf16[6,512,2,4,48]{1,4,3,2,0:T(8,128)(2,1)S(1)}, bf16[6,64,4,48...) while((s32[]{:T(128)}, f32[6,64,4,48]{1,3,2,0:T(8,128)}, ...), condition=%wide.region_26.27_spmd.clone.clone, body=%wide.region_23.26_spmd.clone.sunk.clone | while | flops 26281984 | bytes 3204957 | solution.py:217
  780.2 22.3 while.153
  805.8 170.9 %fusion.200 = bf16[6,2048,2,4,48]{4,1,3,2,0:T(8,128)(2,1)} fusion(bf16[6,2048,2,2,4,48]{5,2,1,4,3,0:T(2,128)(2,1)} %bitcast.1076, pred[2,4]{0,1:T(4,128)(4,1)S(1)} %copy-done.123), kind=kLoop, calls=%fused_computation.303 | loop fusion | flops 14155776 | bytes 28311560 | tf_op jit(solution)/shard_map/reduce_sum | solution.py:48
  976.8 22.5 copy.481
  999.4 56.1 %while.150 = (s32[]{:T(128)}, f32[6,256,4,48]{1,3,2,0:T(8,128)S(1)}, f32[6,256,4,1]{1,2,3,0:T(4,128)S(1)}, bf16[6,2048,2,4,48]{1,4,3,2,0:T(8,128)(2,1)}, bf16[6,...) while((s32[]{:T(128)}, f32[6,256,4,48]{1,3,2,0:T(8,128)S(1)}, ...), condition=%wide.region_12.13_spmd.clone.clone, body=%wide.region_9.12_spmd.clone.sunk.clone | while | flops 433070080 | bytes 38790756 | solution.py:217
  1125.9 47.9 %reduce-scatter.18.cloned.1.call-done = bf16[6,128,768]{2,1,0:T(8,128)(2,1)} async-done(((bf16[6,512,768]{2,1,0:T(8,128)(2,1)}), bf16[6,128,768]{2,1,0:T(8,128)(2,1)}) %reduce-scatter.18.cloned.1.call-update) | async-done | bytes 1179664 | tf_op jit(solution)/shard_map/reduce_scatter | solution.py:238
  1179.7 37.0 %all-gather.10.cloned.1.call-done = bf16[6,512,768]{2,1,0:T(8,128)(2,1)} async-done(((bf16[6,128,768]{2,1,0:T(8,128)(2,1)}), bf16[6,512,768]{2,1,0:T(8,128)(2,1)}) %all-gather.10.cloned.1.call-update) | async-done | bytes 4718608 | tf_op jit(solution)/shard_map/all_gather | solution.py:243
  1229.3 22.7 multiply_convert_fusion.5
  1278.0 47.5 %reduce-scatter.22.cloned.1.call-done = bf16[6,128,768]{2,1,0:T(8,128)(2,1)} async-done(((bf16[6,512,768]{2,1,0:T(8,128)(2,1)}), bf16[6,128,768]{2,1,0:T(8,128)(2,1)}) %reduce-scatter.22.cloned.1.call-update) | async-done | bytes 1179664 | tf_op jit(solution)/shard_map/reduce_scatter | solution.py:275
  1419.7 41.4 %while.156 = (s32[]{:T(128)}, f32[6,64,4,48]{1,3,2,0:T(8,128)S(1)}, bf16[6,512,4,48]{1,3,2,0:T(8,128)(2,1)}, bf16[6,512,4,48]{1,3,2,0:T(8,128)(2,1)}, bf16[6,512...) while((s32[]{:T(128)}, f32[6,64,4,48]{1,3,2,0:T(8,128)S(1)}, ...), condition=%wide.region_63.64_spmd.clone.clone, body=%wide.region_61.63_spmd.clone.sunk.clone | while | flops 64401408 | bytes 6690701 | solution.py:313
  1467.3 30.0 %while.157 = (s32[]{:T(128)}, f32[6,32,4,48]{3,1,2,0:T(8,128)S(1)}, bf16[6,256,4,48]{1,3,2,0:T(8,128)(2,1)S(1)}, bf16[6,256,4,48]{1,3,2,0:T(8,128)(2,1)S(1)}, bf...) while((s32[]{:T(128)}, f32[6,32,4,48]{3,1,2,0:T(8,128)S(1)}, ...), condition=%wide.region_69.70_spmd.clone.clone, body=%wide.region_67.69_spmd.clone.sunk.clone | while | flops 16128002 | bytes 2348301 | solution.py:313
  1505.4 16.7 fusion.213
  1545.8 61.0 %while.155 = (s32[]{:T(128)}, f32[6,128,4,48]{1,3,2,0:T(8,128)}, bf16[6,1024,4,48]{1,3,2,0:T(8,128)(2,1)S(1)}, bf16[6,1024,4,48]{1,3,2,0:T(8,128)(2,1)}, bf16[6,...) while((s32[]{:T(128)}, f32[6,128,4,48]{1,3,2,0:T(8,128)}, ...), condition=%wide.region_57.58_spmd.clone.clone, body=%wide.region_55.57_spmd.clone.sunk.clone | while | flops 257384448 | bytes 21471364 | solution.py:313
  1613.6 34.4 %fusion.215 = bf16[6,256,4,48]{3,1,2,0:T(8,128)(2,1)} fusion(f32[6,256,2,4,48]{4,3,2,1,0:T(4,128)} %reshape.1430, pred[2,4]{0,1:T(4,128)(4,1)S(1)} %copy-done.124, f32[6,256,2,4]{2,1,3,0:T(8,128)} %copy.509), kind=kLoop, calls=%fused_computation.345 | loop fusion | flops 1474560 | bytes 2998280 | tf_op jit(solution)/shard_map/reduce_sum | solution.py:48
  1661.7 20.1 copy.558
  1681.8 17.9 reshape.1443
  1700.4 191.1 %while.154 = (s32[]{:T(128)}, f32[6,256,4,48]{1,3,2,0:T(8,128)S(1)}, bf16[6,2048,4,48]{1,3,2,0:T(8,128)(2,1)}, bf16[6,2048,4,48]{1,3,2,0:T(8,128)(2,1)}, bf16[6,...) while((s32[]{:T(128)}, f32[6,256,4,48]{1,3,2,0:T(8,128)S(1)}, ...), condition=%wide.region_51.52_spmd.clone.clone, body=%wide.region_49.51_spmd.clone.sunk.clone | while | flops 1029095424 | bytes 143601840 | solution.py:313
  1920.4 112.0 %while.149 = (s32[]{:T(128)}, f32[6,512,4,48]{1,3,2,0:T(8,128)S(1)}, f32[6,1024,4,48]{1,3,2,0:T(8,128)}, f32[6,1024,4,48]{1,3,2,0:T(8,128)}, bf16[6,1024,2,4,48]...) while((s32[]{:T(128)}, f32[6,512,4,48]{1,3,2,0:T(8,128)S(1)}, ...), condition=%wide.region_45.46_spmd.clone, body=%wide.region_43.45_spmd.sunk.clone | while | flops 1038385152 | bytes 68586616 | solution.py:301
  2232.4 29.4 %reduce-scatter.38.cloned.1.call-done = bf16[96,192]{1,0:T(8,128)(2,1)} async-done(((bf16[768,192]{1,0:T(8,128)(2,1)}), bf16[96,192]{1,0:T(8,128)(2,1)}) %reduce-scatter.38.cloned.1.call-update) | async-done | bytes 36880
  2263.8 65.1 %reduce-scatter.28.cloned.1.call-done = bf16[96,3,192]{2,0,1:T(8,128)(2,1)} async-done(((bf16[768,3,192]{2,0,1:T(8,128)(2,1)}), bf16[96,3,192]{2,0,1:T(8,128)(2,1)}) %reduce-scatter.28.cloned.1.call-update) | async-done | bytes 110608 | tf_op jit(solution)/shard_map/reduce_scatter | solution.py:367
  2330.6 47.8 %reduce-scatter.26.cloned.1.call-done = bf16[6,128,768]{2,1,0:T(8,128)(2,1)} async-done(((bf16[6,512,768]{2,1,0:T(8,128)(2,1)}), bf16[6,128,768]{2,1,0:T(8,128)(2,1)}) %reduce-scatter.26.cloned.1.call-update) | async-done | bytes 1179664 | tf_op jit(solution)/shard_map/reduce_scatter | solution.py:360
  2384.9 43.7 %reduce-scatter.20.cloned.1.call-done = bf16[6,128,768]{2,1,0:T(8,128)(2,1)} async-done(((bf16[6,512,768]{2,1,0:T(8,128)(2,1)}), bf16[6,128,768]{2,1,0:T(8,128)(2,1)}) %reduce-scatter.20.cloned.1.call-update) | async-done | bytes 1179664 | tf_op jit(solution)/shard_map/reduce_scatter | solution.py:254
  2434.5 40.4 %all-reduce.1 = (f32[6,768]{1,0:T(8,128)S(1)}, f32[2,768]{1,0:T(2,128)S(1)}, f32[3072]{0:T(1024)S(1)}) all-reduce(f32[6,768]{1,0:T(8,128)S(1)} %stack.144, f32[2,768]{1,0:T(2,128)} %copy-done.109, f32[3072]{0:T(1024)} %copy-done.102), channel_id=1, replica_groups=mesh['seq'=8,'head'=4] {'seq','head'}, use_global_device_ids=true, to_apply=%region_83.84 | all-reduce | flops 9216 | bytes 73728 | tf_op jit(solution)/shard_map/psum | solution.py:389
  (1195 shorter events, 1294.4 us)
Async XLA Ops:
  7.2 1209.5 %copy-start = (bf16[768,768]{1,0:T(8,128)(2,1)S(1)}, bf16[768,768]{1,0:T(8,128)(2,1)}, u32[]{:S(2)}) copy-start(bf16[768,768]{1,0:T(8,128)(2,1)} %param.49) | copy-start | bytes 3538948
  7.2 51.2 %all-gather.6.cloned.1.call-start = ((), (), s32[]{:S(2)}) async-start(), calls=%async_computation.11 | async-start | bytes 5898240 | tf_op jit(solution)/shard_map/all_gather | solution.py:186
  18.1 462.5 %all-gather.8.cloned.1.call-start = ((), (), s32[]{:S(2)}) async-start(), calls=%async_computation.12 | async-start | bytes 21233664 | tf_op jit(solution)/shard_map/all_gather | solution.py:209
  67.4 1106.4 %reduce-scatter.18.cloned.1.call-start = ((), (), s32[]{:S(2)}) async-start(), calls=%async_computation.13 | async-start | bytes 5898240 | tf_op jit(solution)/shard_map/reduce_scatter | solution.py:238
  121.0 161.1 %collective-permute-start = (bf16[6,512,2,4,48]{1,4,3,2,0:T(8,128)(2,1)S(1)}, bf16[6,512,2,4,48]{1,4,3,2,0:T(8,128)(2,1)}, u32[]{:S(2)}, u32[]{:S(2)}) collective-permute-start(bf16[6,512,2,4,48]{1,4,3,2,0:T(8,128)(2,1)S(1)} %copy-done.11), channel_id=1, source_target_pairs={{0,4},{4,0},{8,12},{12,8},{16,20},{20,16},{24,28},{28,24},{1,5},{5... | collective-permute-start | bytes 7077896 | tf_op jit(solution)/shard_map/ppermute | solution.py:21
  165.6 121.2 %copy-start.72 = (f32[6,1024]{1,0:T(8,128)S(1)}, f32[6,1024]{1,0:T(8,128)}, u32[]{:S(2)}) copy-start(f32[6,1024]{1,0:T(8,128)} %add_select_fusion) | copy-start | bytes 73732
  344.3 178.9 %copy-start.12 = (f32[6,512,4,48]{1,3,2,0:T(8,128)}, f32[6,512,4,48]{1,3,2,0:T(8,128)S(1)}, u32[]{:S(2)}) copy-start(f32[6,512,4,48]{1,3,2,0:T(8,128)S(1)} %get-tuple-element.494) | copy-start | bytes 7077892
  802.5 174.2 %copy-start.75 = (s32[256]{0:T(256)}, s32[256]{0:T(256)S(1)}, u32[]{:S(2)}) copy-start(s32[256]{0:T(256)S(1)} %get-tuple-element.2684) | copy-start | bytes 3076
  1125.9 90.8 %all-gather.10.cloned.1.call-start = ((), (), s32[]{:S(2)}) async-start(), calls=%async_computation.14 | async-start | bytes 5898240 | tf_op jit(solution)/shard_map/all_gather | solution.py:243
  1175.5 155.3 %copy-start.62 = (f32[6,128]{1,0:T(8,128)}, f32[6,128]{1,0:T(8,128)S(1)}, u32[]{:S(2)}) copy-start(f32[6,128]{1,0:T(8,128)S(1)} %broadcast_multiply_fusion) | copy-start | bytes 9220
  1176.9 154.0 %copy-start.79 = (f32[6,128]{1,0:T(8,128)}, f32[6,128]{1,0:T(8,128)S(1)}, u32[]{:S(2)}) copy-start(f32[6,128]{1,0:T(8,128)S(1)} %fusion.263) | copy-start | bytes 9220
  1179.0 76.6 %all-gather.12.cloned.1.call-start = ((), (), s32[]{:S(2)}) async-start(), calls=%async_computation.16 | async-start | bytes 5898240 | tf_op jit(solution)/shard_map/all_gather | solution.py:187
  1179.6 145.9 %reduce-scatter.22.cloned.1.call-start = ((), (), s32[]{:S(2)}) async-start(), calls=%async_computation.17 | async-start | bytes 5898240 | tf_op jit(solution)/shard_map/reduce_scatter | solution.py:275
  1277.6 94.4 %all-gather.14.cloned.1.call-start = ((), (), s32[]{:S(2)}) async-start(), calls=%async_computation.18 | async-start | bytes 5898240 | tf_op jit(solution)/shard_map/all_gather | solution.py:283
  1334.4 765.7 %all-reduce.4.cloned.1.call-start = ((), (), s32[]{:S(2)}) async-start(), calls=%async_computation.27 | async-start | bytes 6291456
  1505.3 610.9 %reduce-scatter.36.cloned.1.call-start = ((), (), s32[]{:S(2)}) async-start(), calls=%async_computation.25 | async-start | bytes 2654208
  1544.9 595.0 %reduce-scatter.34.cloned.1.call-start = ((), (), s32[]{:S(2)}) async-start(), calls=%async_computation.24 | async-start | bytes 5308416
  1699.7 467.9 %reduce-scatter.24.cloned.1.call-start = ((), (), s32[]{:S(2)}) async-start(), calls=%async_computation.19 | async-start | bytes 10616832 | tf_op jit(solution)/shard_map/reduce_scatter | solution.py:327
  1900.2 327.2 %reduce-scatter.30.cloned.1.call-start = ((), (), s32[]{:S(2)}) async-start(), calls=%async_computation.22 | async-start | bytes 1327104 | tf_op jit(solution)/shard_map/reduce_scatter | solution.py:373
  1908.9 320.1 %reduce-scatter.32.cloned.1.call-start = ((), (), s32[]{:S(2)}) async-start(), calls=%async_computation.23 | async-start | bytes 1327104 | tf_op jit(solution)/shard_map/reduce_scatter | solution.py:376
  1919.0 342.8 %reduce-scatter.38.cloned.1.call-start = ((), (), s32[]{:S(2)}) async-start(), calls=%async_computation.26 | async-start | bytes 442368
  2040.5 149.8 %collective-permute-start.1 = (bf16[6,512,2,4,48]{1,4,3,2,0:T(8,128)(2,1)}, bf16[6,512,2,4,48]{1,4,3,2,0:T(8,128)(2,1)}, u32[]{:S(2)}, u32[]{:S(2)}) collective-permute-start(bf16[6,512,2,4,48]{1,4,3,2,0:T(8,128)(2,1)} %pad_maximum_fusion.3), channel_id=1, source_target_pairs={{0,4},{4,0},{8,12},{12,8},{16,20},{20,16},{24,28},{28,24},{1,5},{5... | collective-permute-start | bytes 7077896 | tf_op jit(solution)/shard_map/ppermute | solution.py:21
  2090.9 238.0 %reduce-scatter.28.cloned.1.call-start = ((), (), s32[]{:S(2)}) async-start(), calls=%async_computation.21 | async-start | bytes 1327104 | tf_op jit(solution)/shard_map/reduce_scatter | solution.py:367
  2209.7 168.6 %reduce-scatter.26.cloned.1.call-start = ((), (), s32[]{:S(2)}) async-start(), calls=%async_computation.20 | async-start | bytes 5898240 | tf_op jit(solution)/shard_map/reduce_scatter | solution.py:360
  2217.4 211.2 %reduce-scatter.20.cloned.1.call-start = ((), (), s32[]{:S(2)}) async-start(), calls=%async_computation.15 | async-start | bytes 5898240 | tf_op jit(solution)/shard_map/reduce_scatter | solution.py:254
  2226.5 151.8 %copy-start.6 = (f32[6,128,768]{2,1,0:T(8,128)S(1)}, f32[6,128,768]{2,1,0:T(8,128)}, u32[]{:S(2)}) copy-start(f32[6,128,768]{2,1,0:T(8,128)} %copy-done.4) | copy-start | bytes 7077892
  2226.5 151.8 %copy-start.70 = (f32[6,128]{1,0:T(8,128)S(1)}, f32[6,128]{1,0:T(8,128)}, u32[]{:S(2)}) copy-start(f32[6,128]{1,0:T(8,128)} %copy-done.69) | copy-start | bytes 9220
  2263.8 66.8 %copy-start.109 = (f32[2,768]{1,0:T(2,128)}, f32[2,768]{1,0:T(2,128)S(1)}, u32[]{:S(2)}) copy-start(f32[2,768]{1,0:T(2,128)S(1)} %dynamic_update_slice.93) | copy-start | bytes 18436
  2330.6 98.0 %copy-start.63 = (f32[6,128]{1,0:T(8,128)S(1)}, f32[6,128]{1,0:T(8,128)}, u32[]{:S(2)}) copy-start(f32[6,128]{1,0:T(8,128)} %copy-done.62) | copy-start | bytes 9220
  2330.6 98.0 %copy-start.78 = (f32[768]{0:T(1024)S(1)}, f32[768]{0:T(1024)}, u32[]{:S(2)}) copy-start(f32[768]{0:T(1024)} %param.47) | copy-start | bytes 9220
  2330.6 98.0 %copy-start.80 = (f32[6,128]{1,0:T(8,128)S(1)}, f32[6,128]{1,0:T(8,128)}, u32[]{:S(2)}) copy-start(f32[6,128]{1,0:T(8,128)} %copy-done.79) | copy-start | bytes 9220
  2384.3 92.6 %copy-start.1 = (bf16[768,768]{1,0:T(8,128)(2,1)S(1)}, bf16[768,768]{1,0:T(8,128)(2,1)}, u32[]{:S(2)}) copy-start(bf16[768,768]{1,0:T(8,128)(2,1)} %param.49) | copy-start | bytes 3538948
  (138 other events, 1415.5 us)
Sparse Core Ops, SparseCore 0:
  18.2 40.1 all-gather.5
  67.5 413.0 all-gather.7
  1126.0 47.7 reduce-scatter.17
  1179.2 37.4 all-gather.9
  1218.2 37.4 all-gather.11
  1277.7 47.8 reduce-scatter.21
  1334.5 37.4 all-gather.13
  1505.4 128.8 all-reduce.3
  1638.2 67.8 reduce-scatter.35
  1710.0 94.2 reduce-scatter.33
  1900.3 163.8 reduce-scatter.23
  2067.8 63.4 reduce-scatter.29
  2135.0 62.9 reduce-scatter.31
  2201.5 60.3 reduce-scatter.37
  2266.0 62.8 reduce-scatter.27
  2331.5 46.8 reduce-scatter.25
  2380.7 47.8 reduce-scatter.19
where the time goes:
time: 2510 us; the launch traced here: 2480 us
  other arithmetic  704 us (28%)
  local copies, waits for them, and re-layouts  638 us (25%)
  waiting for transfers between devices  624 us (25%)
  matrix products  452 us (18%)
  blocking collectives  40.4 us (2%)
    reduce_sum x16, other arithmetic, pick(): jnp.sum(jnp.where(chosen.reshape(mask_shape(value, chosen)), split, jnp.z...  443 us
    broadcast_in_dim x45, local copies, waits for them, and re-layouts, spread(): jnp.where(chosen.reshape(mask_shape(value, chosen)), jnp.expand_dims(valu...  172 us
    unnamed x306, local copies, waits for them, and re-layouts  161 us
    all_gather x1, waiting for transfers between devices, on_device(): far_kvs = collect(lax.all_gather(key_value, 'seq', axis=1, tiled=True))  135 us
    dot_general x60, matrix products, scores_of(): jnp.einsum('qhe,khe->hqk', query, keys, preferred_element_type=jnp.float32)  127 us
    ppermute x2, waiting for transfers between devices, partner(): lax.ppermute(x, axis, [(i, i ^ 1 << stride) for i in range(lax.axis_size(...  117 us
    convert_element_type x30, other arithmetic, attend_backward(): grad_scores = (probs * (grad_probs - delta[..., None])).astype(jnp.bfloat16)  68.7 us
    reduce_scatter x1, waiting for transfers between devices, on_device(): lax.psum_scatter(grad_w_qkv.astype(jnp.bfloat16), 'seq', scatter_dimensio...  65.1 us
  transfers between devices with their start and end apart: 19, of which 12 were waited for; matrix products, arithmetic and copies ran while one was open for 38% of the time, Pallas kernels for 0%

commit v1 on v0

--- a/solution.py
+++ b/solution.py
@@ -3,7 +3,11 @@
 
 import jax
 import jax.numpy as jnp
+import ml_dtypes
+import numpy as np
 from jax import lax
+from jax.experimental import pallas as pl
+from jax.experimental.pallas import tpu as pltpu
 from jax.sharding import PartitionSpec as P
 
 HEADS = 16
@@ -407,7 +411,1451 @@
     )
 
 
+HEAD_DIM = 48
+TRIPLE = 144
+META = 32
+AUG = 128
+OUT_ROWS = 64
+ACC_ROWS = 56
+SLOT_ORDER = (0, 2, 1, 3)
+LOG2E = math.log2(math.e)
+COST = 2.5
+FIRST_COLUMNS = 1024
+BF = jnp.bfloat16
+F32 = jnp.float32
+
+
+def dot(a, b):
+    return lax.dot_general(a, b, (((1,), (0,)), ((), ())), preferred_element_type=F32)
+
+
+def dot_nt(a, b):
+    return lax.dot_general(a, b, (((1,), (1,)), ((), ())), preferred_element_type=F32)
+
+
+def split3(value):
+    high = value.astype(BF)
+    rest = value - high.astype(F32)
+    middle = rest.astype(BF)
+    low = (rest - middle.astype(F32)).astype(BF)
+    return high, middle, low
+
+
+def split3_constant(value):
+    pieces = []
+    rest = np.float32(value)
+    for _ in range(3):
+        piece = np.float32(rest.astype(ml_dtypes.bfloat16))
+        pieces.append(float(piece))
+        rest = np.float32(rest - piece)
+    return pieces
+
+
+def joined(rows):
+    wide = rows.astype(F32)
+    return wide[0:1] + wide[1:2] + wide[2:3]
+
+
+def rows_of(shape, first, pieces):
+    row = lax.broadcasted_iota(jnp.int32, shape, 0)
+    out = jnp.zeros(shape, F32)
+    for index, piece in enumerate(pieces):
+        out = jnp.where(row == first + index, piece, out)
+    return out
+
+
+def rows_between(shape, first, count):
+    row = lax.broadcasted_iota(jnp.int32, shape, 0)
+    return jnp.where((row >= first) & (row < first + count), 1.0, 0.0)
+
+
+def query_rows(query, meta, factor):
+    wide = query.astype(F32) * factor
+    high = wide.astype(BF)
+    low = (wide - high.astype(F32)).astype(BF)
+    return jnp.concatenate([high, low, meta], 0)
+
+
+def key_rows(keys, meta):
+    return jnp.concatenate([keys, keys, meta], 0)
+
+
+def ones_below(value, count):
+    width = value.shape[-1]
+    return jnp.concatenate([value, rows_between((16, width), 0, count).astype(BF)], 0)
+
+
+def plain64(value):
+    return jnp.concatenate([value, jnp.zeros((16, value.shape[-1]), value.dtype)], 0)
+
+
+def padded_turn(value):
+    height, width = value.shape
+    missing = -height % 128
+    full = jnp.concatenate([value, jnp.zeros((missing, width), value.dtype)], 0)
+    return full.T
+
+
+def turned_out(value):
+    height = value.shape[0]
+    return jnp.concatenate([value, jnp.zeros((height, 64), F32)], 1).T[0:HEAD_DIM]
+
+
+def bias_rows(valid):
+    shape = (META, valid.shape[-1])
+    return rows_of(shape, 0, [(1.0 - valid) * part for part in split3_constant(NEG * LOG2E)])
+
+
+def near_key_meta(valid):
+    shape = (META, valid.shape[-1])
+    return (bias_rows(valid) + rows_between(shape, 15, 3)).astype(BF)
+
+
+def far_levels(place, width, half):
+    head = 4 * (2 * place[2] + place[3]) + place[0]
+    lane = lax.broadcasted_iota(jnp.int32, (1, width), 1)
+    spot = (2 * (lane & (half - 1)) + (place[0] & 1)) & 15
+    return jnp.where(
+        spot == (head & 15),
+        4,
+        jnp.where((spot & 7) == (head & 7), 3, jnp.where((spot & 3) == (head & 3), 2, 1)),
+    )
+
+
+def far_tables(level):
+    pieces = {0: [], 1: []}
+    for extra in (0, 1):
+        for part in range(3):
+            for kind in range(1, 5):
+                row = jnp.zeros(level.shape, F32)
+                for there in range(1, 5):
+                    amount = split3_constant(math.log2(min(kind, there) + extra))[part]
+                    row = jnp.where(level == there, amount, row)
+                pieces[extra].append(row)
+    shape = (META, level.shape[-1])
+    return rows_of(shape, 3, pieces[0]) + rows_between(shape, 15, 3) + rows_of(shape, 18, pieces[1])
+
+
+def far_queries(level):
+    shape = (META, level.shape[-1])
+    chosen = [jnp.where(level == kind, 1.0, 0.0) for kind in range(1, 5)] * 3
+    ones = rows_between(shape, 0, 3)
+    return (ones + rows_of(shape, 18, chosen)).astype(BF), (ones + rows_of(shape, 3, chosen)).astype(BF)
+
+
+def softmax_out(keys, values, queries, stage):
+    top = None
+    for index, key in enumerate(keys):
+        scores = dot(key(), queries[index])
+        stage[index] = scores
+        peak = jnp.max(scores, axis=0, keepdims=True)
+        top = peak if top is None else jnp.maximum(top, peak)
+    acc = None
+    for index, value in enumerate(values):
+        probs = jnp.exp2(stage[index] - top).astype(BF)
+        part = dot(value(), probs)
+        acc = part if acc is None else acc + part
+    total = acc[HEAD_DIM : HEAD_DIM + 1]
+    return acc[0:HEAD_DIM] * (1.0 / total), top + jnp.log2(total)
+
+
+def moments(value):
+    mean = jnp.mean(value, axis=-1, keepdims=True)
+    centered = value - mean
+    var = jnp.mean(centered * centered, axis=-1, keepdims=True)
+    rate = lax.rsqrt(var + EPS)
+    return centered * rate, rate
+
+
+def norm_back(xhat, rate, gain, upstream):
+    a = upstream * gain
+    return rate * (
+        a - jnp.mean(a, axis=-1, keepdims=True) - xhat * jnp.mean(a * xhat, axis=-1, keepdims=True)
+    )
+
+
+def parity_order(rows, back):
+    first = lax.broadcasted_iota(jnp.int32, (rows, rows), 1 if back else 0)
+    second = lax.broadcasted_iota(jnp.int32, (rows, rows), 0 if back else 1)
+    half = rows // 2
+    source = jnp.where(first < half, 2 * first, 2 * (first - half) + 1)
+    return (source == second).astype(F32).astype(BF)
+
+
+def entry_kernel(
+    place, tiles_a, tiles_b, coords_a, coords_b, cot_a, cot_b, table, base, cot_out, own, other
+):
+    rows = tiles_a.shape[1]
+    half = rows // 2
+    order = parity_order(rows, False)
+    lane = lax.broadcasted_iota(jnp.int32, (rows, 256), 1).astype(F32)
+    sides = ((tiles_a, coords_a, cot_a, own), (tiles_b, coords_b, cot_b, other))
+    for side, (tiles, coords, cot, out) in enumerate(sides):
+        spots = dot(order, coords[0].astype(F32).astype(BF))
+        parts = []
+        for axis in range(2):
+            hot = (spots[:, axis : axis + 1] == lane).astype(F32).astype(BF)
+            parts.append(dot(hot, table[0]) + dot(hot, table[1]) + dot(hot, table[2]))
+        value = dot(order, tiles[0]) + jnp.concatenate(parts, 1)
+        base[side, 0] = value
+        xhat = moments(value)[0].astype(BF)
+        out[0, 0] = xhat[:half]
+        out[0, 1] = xhat[half:]
+        cot_out[side, 0] = dot(order, cot[0]).astype(BF)
+
+
+def join_kernel(place, first, second, out):
+    here = first.shape[2]
+    out[:, :, :here] = first[...]
+    out[:, :, here:] = second[...]
+
+
+def widen_kernel(place, first, second, stay, send):
+    half = first.shape[2] // 2
+    stay[...] = jnp.concatenate([first[:, :, :half], second[:, :, :half]], -1)
+    send[...] = jnp.concatenate([first[:, :, half:], second[:, :, half:]], -1)
+
+
+def narrow_kernel(place, first, second, stay, send):
+    here = first.shape[2]
+    columns = first.shape[-1] // 2
+    for ref, part in ((first, slice(0, here)), (second, slice(here, 2 * here))):
+        stay[:, :, part] = ref[..., :columns]
+        send[:, :, part] = ref[..., columns:]
+
+
+def fold_kernel(place, first, second, stay, send):
+    half = first.shape[2] // 2
+    total = (first[...].astype(F32) + second[...].astype(F32)).astype(BF)
+    stay[...] = total[:, :, :half]
+    send[...] = total[:, :, half:]
+
+
+def z_fold_kernel(place, first, second, stay, send, total, *, bit):
+    half = first.shape[0] // 2
+    total[...] = (first[...].astype(F32) + second[...].astype(F32)).astype(BF)
+    side = place[0] // 2 if bit else place[0] % 2
+    stay[...] = total[pl.ds(pl.multiple_of(side * half, 32), half)]
+    send[...] = total[pl.ds(pl.multiple_of((1 - side) * half, 32), half)]
+
+
+def weights_out_kernel(place, first, second, fc1, fc2, out):
+    total = first[...].astype(F32) + second[...].astype(F32)
+    width = fc1.shape[1]
+    rows = total.shape[0]
+    fc1[...] = total[:, :width]
+    out[...] = padded_turn(total[:, width:FIRST_COLUMNS])[: out.shape[0], :rows]
+    fc2[...] = padded_turn(total[:, FIRST_COLUMNS:])[:, :rows]
+
+
+def qkv_out_kernel(place, first, second, out):
+    total = first[...].astype(F32) + second[...].astype(F32)
+    for head in range(4):
+        for part in range(3):
+            at = (head * 3 + part) * HEAD_DIM
+            out[:, part, head * HEAD_DIM : (head + 1) * HEAD_DIM] = total[:, at : at + HEAD_DIM]
+
+
+def small_start_kernel(place, sums_a, sums_b, fc1_a, fc1_b, ln_sum, bias_sum, stay, send, last):
+    width = sums_a.shape[1]
+    common = [sums_a[index : index + 1] + sums_b[index : index + 1] for index in range(4)]
+    common += [ln_sum[0:1], ln_sum[1:2]]
+    slots = [fc1_a[slot, 0:1] + fc1_b[slot, 0:1] for slot in range(4)]
+    stay[...] = rows_of((8, width), 0, common + slots[0:2])
+    send[...] = rows_of((8, width), 0, common + slots[2:4])
+    missing = width - bias_sum.shape[1]
+    last[...] = jnp.concatenate([bias_sum[...], jnp.zeros((8, missing), F32)], 1)
+
+
+def small_middle_kernel(place, first, second, stay, send):
+    total = first[...] + second[...]
+    row = lax.broadcasted_iota(jnp.int32, total.shape, 0)
+    stay[...] = jnp.where(row == 7, 0.0, total)
+    send[...] = jnp.where(row == 6, total[7:8], jnp.where(row == 7, 0.0, total))
+
+
+def small_last_kernel(place, first, second, last, out):
+    total = first[...] + second[...]
+    row = lax.broadcasted_iota(jnp.int32, total.shape, 0)
+    out[...] = jnp.where(row == 7, last[...], total)
+
+
+def add_kernel(place, first, second, out):
+    out[...] = first[...] + second[...]
+
+
+def normed_of(xhat, gains):
+    return (xhat.astype(F32) * gains[0:1] + gains[1:2]).astype(BF)
+
+
+def qkv_kernel(place, first, second, weight, bias, gains, near, s0, s1, s2, s3):
+    width = first.shape[2]
+    for parity in range(2):
+        for part, ref in enumerate((first, second)):
+            made = dot_nt(weight[...], normed_of(ref[0, parity], gains)) + bias[...]
+            made = made.astype(BF)
+            for head in range(4):
+                near[0, head, parity, :, part * width : (part + 1) * width] = made[
+                    head * TRIPLE : (head + 1) * TRIPLE
+                ]
+    for slot, ref in enumerate((s0, s1, s2, s3)):
+        head = place[0] ^ slot
+        ref[0] = near[0, head, head & 1]
+
+
+def near_forward_kernel(place, qkv, valid, out, key_aug, value_aug, stage, *, slide, factor):
+    width = qkv.shape[-1]
+    own = lax.rem(pl.program_id(0), 2)
+    queries = []
+    ones = rows_between((META, width), 0, 3).astype(BF)
+    for role in range(2):
+        parity = own if role == 0 else 1 - own
+        block = qkv[0, 0, parity]
+        there = valid[place[1] * 3 + slide, pl.ds(place[0] * 2 + parity, 1)]
+        key_aug[role] = key_rows(block[48:96], near_key_meta(there)).T
+        value_aug[role] = ones_below(block[96:144], 1)
+        queries.append(query_rows(block[0:48], ones, factor))
+    for role, used in ((0, (1,)), (1, (0, 1))):
+        result, total = softmax_out(
+            [lambda r=r: key_aug[r] for r in used],
+            [lambda r=r: value_aug[r] for r in used],
+            [queries[role]] * len(used),
+            stage,
+        )
+        out[0, role] = jnp.concatenate([result, rows_of((8, width), 0, [total])], 0)
+
+
+def far_forward_kernel(
+    place, b0, b1, b2, b3, valid, o0, o1, o2, o3, key_aug, value_aug, q_same, q_other, stage, out,
+    *, first_slide, half, factor,
+):
+    width = b0.shape[-1]
+    slide = first_slide + pl.program_id(0)
+    level = far_levels(place, width, half)
+    tail = far_tables(level)
+    same, other = far_queries(level)
+    for slot, block in enumerate((b0, b1, b2, b3)):
+        row = (place[0] ^ slot) * 2 + (place[0] & 1)
+        there = valid[place[1] * 3 + slide, pl.ds(row, 1)]
+        key_aug[slot] = key_rows(block[0, 48:96], (tail + bias_rows(there)).astype(BF)).T
+        value_aug[slot] = ones_below(block[0, 96:144], 1)
+        q_same[slot] = query_rows(block[0, 0:48], same, factor)
+        q_other[slot] = query_rows(block[0, 0:48], other, factor)
+
+    def step(slot, carry):
+        places = [lax.rem(slot + shift, 4) for shift in range(4)]
+        result, total = softmax_out(
+            [lambda p=p: key_aug[p] for p in places],
+            [lambda p=p: value_aug[p] for p in places],
+            [q_same[slot], q_other[slot], q_other[slot], q_other[slot]],
+            stage,
+        )
+        ending = rows_of((16, width), 0, [part.astype(F32) for part in split3(total)])
+        out[slot] = jnp.concatenate([result, ending], 0).astype(BF)
+        return carry
+
+    lax.fori_loop(0, 4, step, 0)
+    for slot, ref in enumerate((o0, o1, o2, o3)):
+        ref[0] = out[slot]
+
+
+def merge_kernel(place, *refs):
+    count = refs[-2].shape[0]
+    nears = refs[:count]
+    f0, f1, f2, f3, kept, stay, send, far = refs[count:]
+    width = kept.shape[-1]
+    for slide, near in enumerate(nears):
+        for slot, ref in enumerate((f0, f1, f2, f3)):
+            far[place[0] ^ slot] = ref[slide]
+        by_parity = [[], []]
+        for head in range(4):
+            own = head & 1
+            there = far[head]
+            far_total = joined(there[48:51])
+            near_total = near[head, 0, 48:49]
+            top = jnp.maximum(far_total, near_total)
+            total = top + jnp.log2(jnp.exp2(far_total - top) + jnp.exp2(near_total - top))
+            both = there[0:48].astype(F32) * jnp.exp2(far_total - total) + near[
+                head, 0, 0:48
+            ] * jnp.exp2(near_total - total)
+            kept[slide, head, own] = jnp.concatenate([both, rows_of((8, width), 0, [total])], 0)
+            kept[slide, head, 1 - own] = near[head, 1]
+            by_parity[own].append(both)
+            by_parity[1 - own].append(near[head, 1, 0:48])
+        for parity in range(2):
+            turned = padded_turn(jnp.concatenate(by_parity[parity], 0))[:, 0:192].astype(BF)
+            for block in range(4):
+                rows = slice(block * width // 8, (block + 1) * width // 8)
+                stay[slide, parity, block] = turned[rows]
+                rows = slice((block + 4) * width // 8, (block + 5) * width // 8)
+                send[slide, parity, block] = turned[rows]
+
+
+def gradient_rows_kernel(place, first, second, kept, *refs):
+    near, s0, s1, s2, s3 = refs[-5:]
+    half = first.shape[2]
+    width = kept.shape[-1]
+    for parity in range(2):
+        turned = jnp.concatenate(
+            [
+                jnp.concatenate([ref[0, parity], jnp.zeros((half, 64), BF)], 1).T
+                for ref in (first, second)
+            ],
+            1,
+        )
+        for head in range(4):
+            part = turned[head * 48 : (head + 1) * 48]
+            inner = jnp.sum(part.astype(F32) * kept[0, head, parity, 0:48], axis=0, keepdims=True)
+            total = kept[0, head, parity, 48:49]
+            rows = [piece.astype(F32) for piece in split3(total) + split3(inner)]
+            ending = rows_of((16, width), 0, rows).astype(BF)
+            near[0, head, parity] = jnp.concatenate([part, ending], 0)
+    for slot, ref in enumerate((s0, s1, s2, s3)):
+        head = place[0] ^ slot
+        ref[0] = near[0, head, head & 1]
+
+
+def negated_total(grad_block, base):
+    tail = grad_block[48:64].astype(F32)
+    row = lax.broadcasted_iota(jnp.int32, base.shape, 0)
+    out = base.astype(F32)
+    for index in range(3):
+        out = jnp.where(row == 15 + index, -tail[index : index + 1], out)
+    return out.astype(BF)
+
+
+def gradient_aug(grad_block):
+    width = grad_block.shape[-1]
+    tail = grad_block[48:64].astype(F32)
+    rows = rows_of((16, width), 0, [-tail[index : index + 1] for index in (3, 4, 5)])
+    return jnp.concatenate([grad_block[0:48], rows.astype(BF)], 0)
+
+
+def pair_block(key_aug, value_aug, queries, grads):
+    probs = jnp.exp2(dot(key_aug, queries))
+    slopes = (probs * dot(value_aug, grads)).astype(BF)
+    return probs.astype(BF), slopes
+
+
+def near_backward_kernel(
+    place, qkv, valid, grad, out, key_aug, key_t, value_aug, q_aug, g_aug, q_nat, g_nat,
+    *, slide, factor, scale,
+):
+    width = qkv.shape[-1]
+    own = lax.rem(pl.program_id(0), 2)
+    ones = rows_between((META, width), 0, 3)
+    for role in range(2):
+        parity = own if role == 0 else 1 - own
+        block = qkv[0, 0, parity]
+        given = grad[0, 0, parity]
+        there = valid[place[1] * 3 + slide, pl.ds(place[0] * 2 + parity, 1)]
+        key_aug[role] = key_rows(block[48:96], near_key_meta(there)).T
+        key_t[role] = plain64(block[48:96])
+        value_aug[role] = padded_turn(ones_below(block[96:144], 3))[:, 0:64]
+        q_aug[role] = query_rows(block[0:48], negated_total(given, ones), factor)
+        g_aug[role] = gradient_aug(given)
+        q_nat[role] = padded_turn(plain64(block[0:48]))[:, 0:64]
+        g_nat[role] = padded_turn(plain64(given[0:48]))[:, 0:64]
+    dq = [None, None]
+    for key_role, users in ((0, (1,)), (1, (0, 1))):
+        dk = None
+        dv = None
+        for role in users:
+            probs, slopes = pair_block(
+                key_aug[key_role], value_aug[key_role], q_aug[role], g_aug[role]
+            )
+            add_v = dot(probs, g_nat[role])
+            add_k = dot(slopes, q_nat[role])
+            add_q = dot(key_t[key_role], slopes)
+            dv = add_v if dv is None else dv + add_v
+            dk = add_k if dk is None else dk + add_k
+            dq[role] = add_q if dq[role] is None else dq[role] + add_q
+        parity = own if key_role == 0 else 1 - own
+        out[0, parity, 48:96] = (turned_out(dk) * scale).astype(BF)
+        out[0, parity, 96:144] = turned_out(dv).astype(BF)
+    for role in range(2):
+        parity = own if role == 0 else 1 - own
+        out[0, parity, 0:48] = (dq[role][0:48] * scale).astype(BF)
+
+
+def far_backward_kernel(
+    place, b0, b1, b2, b3, g0, g1, g2, g3, valid, o0, o1, o2, o3,
+    key_aug, key_t, value_aug, q_same, q_other, g_aug, q_nat, g_nat, dq, out,
+    *, first_slide, half, factor, scale,
+):
+    width = b0.shape[-1]
+    slide = first_slide + pl.program_id(0)
+    level = far_levels(place, width, half)
+    tail = far_tables(level)
+    same, other = far_queries(level)
+    for slot, (block, given) in enumerate(((b0, g0), (b1, g1), (b2, g2), (b3, g3))):
+        grad = given[0]
+        row = (place[0] ^ slot) * 2 + (place[0] & 1)
+        there = valid[place[1] * 3 + slide, pl.ds(row, 1)]
+        key_aug[slot] = key_rows(block[0, 48:96], (tail + bias_rows(there)).astype(BF)).T
+        key_t[slot] = plain64(block[0, 48:96])
+        value_aug[slot] = padded_turn(ones_below(block[0, 96:144], 3))[:, 0:64]
+        q_same[slot] = query_rows(block[0, 0:48], negated_total(grad, same), factor)
+        q_other[slot] = query_rows(block[0, 0:48], negated_total(grad, other), factor)
+        g_aug[slot] = gradient_aug(grad)
+        q_nat[slot] = padded_turn(plain64(block[0, 0:48]))[:, 0:64]
+        g_nat[slot] = padded_turn(plain64(grad[0:48]))[:, 0:64]
+    dq[...] = jnp.zeros_like(dq)
+
+    def step(slot, carry):
+        dk = None
+        dv = None
+        for shift in range(4):
+            there = lax.rem(slot + shift, 4)
+            queries = q_same[there] if shift == 0 else q_other[there]
+            probs, slopes = pair_block(key_aug[slot], value_aug[slot], queries, g_aug[there])
+            add_v = dot(probs, g_nat[there])
+            add_k = dot(slopes, q_nat[there])
+            dv = add_v if dv is None else dv + add_v
+            dk = add_k if dk is None else dk + add_k
+            dq[there] += dot(key_t[slot], slopes)
+        out[slot, 48:96] = (turned_out(dk) * scale).astype(BF)
+        out[slot, 96:144] = turned_out(dv).astype(BF)
+        return carry
+
+    lax.fori_loop(0, 4, step, 0)
+    for slot, ref in enumerate((o0, o1, o2, o3)):
+        ref[0] = out[slot]
+        ref[0, 0:48] = (dq[slot, 0:48] * scale).astype(BF)
+
+
+def qkv_backward_kernel(place, *refs, count, begins, ends):
+    refs = list(refs)
+    nears = [refs.pop(0) for _ in range(count)]
+    f0, f1, f2, f3, first, second, weight, gains = [refs.pop(0) for _ in range(8)]
+    before = [] if begins else [refs.pop(0) for _ in range(3)]
+    wgrads = [refs.pop(0) for _ in range(2 if ends else 1)]
+    bias_sum, ln_sum, stay, send, far = refs[:5]
+    acc = refs[5] if ends else wgrads[0]
+    if begins:
+        for ref in (acc, bias_sum, ln_sum):
+            ref[...] = jnp.zeros_like(ref)
+    else:
+        for ref, old in zip((acc, bias_sum, ln_sum), before):
+            ref[...] = old[...]
+    half = first.shape[2]
+    piece_rows = half // 4
+    gain_row = jnp.zeros((1, gains.shape[1]), F32)
+    bias_row = jnp.zeros((1, gains.shape[1]), F32)
+    ones = jnp.ones((8, 2 * half), BF)
+    for slide, near in enumerate(nears):
+        for slot, ref in enumerate((f0, f1, f2, f3)):
+            far[place[0] ^ slot] = ref[slide]
+        for parity in range(2):
+            pieces = []
+            for head in range(4):
+                piece = near[head, parity]
+                if head & 1 == parity:
+                    piece = (piece.astype(F32) + far[head].astype(F32)).astype(BF)
+                pieces.append(piece)
+            total = jnp.concatenate(pieces, 0)
+            bias_sum[...] += dot_nt(ones, total)
+            turned = padded_turn(total)[:, 0 : total.shape[0]]
+            for part, ref, out in ((0, first, stay), (1, second, send)):
+                xhat = ref[slide, parity]
+                here = slice(part * half, (part + 1) * half)
+                acc[...] += dot(total[:, here], normed_of(xhat, gains))
+                back = dot(turned[here], weight[...])
+                low = back.astype(BF)
+                for block in range(4):
+                    out[slide, parity, block] = low[block * piece_rows : (block + 1) * piece_rows]
+                gain_row = gain_row + jnp.sum(back * xhat.astype(F32), axis=0, keepdims=True)
+                bias_row = bias_row + jnp.sum(back, axis=0, keepdims=True)
+    ln_sum[...] += rows_of(ln_sum.shape, 0, [gain_row, bias_row])
+    if ends:
+        missing = wgrads[0].shape[1] - acc.shape[0]
+        full = jnp.concatenate([acc[...], jnp.zeros((missing, acc.shape[1]), F32)], 0)
+        turned = full.T.astype(BF)
+        rows = turned.shape[0] // 8
+        for index in range(8):
+            part = turned[index * rows : (index + 1) * rows]
+            where = slice(index // 2 * rows, (index // 2 + 1) * rows)
+
+            @pl.when(place[1] == index % 2)
+            def _():
+                wgrads[0][where] = part
+
+            @pl.when(place[1] != index % 2)
+            def _():
+                wgrads[1][where] = part
+
+
+def exit_kernel(place, first, second, base, grad_mid, out_rows, gains, *refs):
+    tiles_grad, output = refs[-2:]
+    rows = base.shape[2]
+    half = rows // 2
+    xhat, rate = moments(base[0, 0])
+    side = pl.program_id(0)
+    upstream = jnp.concatenate(
+        [jnp.where(side == 0, first[0, part], second[0, part]) for part in range(2)], 0
+    ).astype(F32)
+    grad = grad_mid[0, 0] + norm_back(xhat, rate, gains[0:1], upstream)
+    undo = parity_order(rows, True)
+    tiles_grad[0] = dot(undo, grad.astype(BF)).astype(BF)
+    output[0] = dot(undo, out_rows[0, 0]).astype(BF)
+
+
+def mlp_kernel(
+    place, base, own, other, cot, w1, w2, wo0, wo1, wo2, wo3, offset, small,
+    output, grad_mid, grad_own, grad_other, hidden_out, g_pre_out, normed_t, cot_t, attn_t,
+    merged_out, sums, fc1_sum,
+    w_out, mid, merged, normed, ff, back,
+):
+    step = pl.program_id(0)
+    rows, width = mid.shape
+    part = 256
+    half = part // 4
+
+    def cot_at(first):
+        slide = first // part
+        return jnp.concatenate([cot[0, slide], cot[1, slide]], 0)
+
+    @pl.when(step == 0)
+    def _():
+        for index, ref in enumerate((wo0, wo1, wo2, wo3)):
+            w_out[index * 192 : (index + 1) * 192] = ref[0]
+        for first in range(0, rows, part):
+            here = pl.ds(first, part)
+            slide = first // part
+            for side, ref in enumerate((own, other)):
+                for parity in range(2):
+                    at = first + (2 * side + parity) * half
+                    merged[at : at + half] = ref[slide, parity]
+            value = jnp.concatenate([base[0, slide], base[1, slide]], 0)
+            value = value + (dot(merged[here], w_out[...]) + small[0:1])
+            mid[here] = value
+            xhat, _ = moments(value)
+            low = (xhat * small[1:2] + small[2:3]).astype(BF)
+            normed[here] = low
+            normed_t[:, first : first + part] = low.T
+            cot_t[:, first : first + part] = cot_at(first).T
+        for index, slot in enumerate(SLOT_ORDER):
+            merged_out[slot] = merged[:, index * 192 : (index + 1) * 192]
+
+    shift = joined(offset[0, 0:3])
+    fc1 = jnp.zeros((1, width), F32)
+    for first in range(0, rows, part):
+        here = pl.ds(first, part)
+        pre = dot(normed[here], w1[0]) + shift
+        cdf = 0.5 * (1.0 + lax.erf(pre * math.sqrt(0.5)))
+        hidden = (pre * cdf).astype(BF)
+        slope = cdf + pre * (jnp.exp(-0.5 * pre * pre) * (1.0 / math.sqrt(2.0 * math.pi)))
+        g_pre = (dot_nt(cot_at(first), w2[0]) * slope).astype(BF)
+        hidden_out[0, here] = hidden
+        g_pre_out[0, here] = g_pre
+        add_ff = dot(hidden, w2[0])
+        add_back = dot_nt(g_pre, w1[0])
+
+        @pl.when(step == 0)
+        def _():
+            ff[here] = add_ff
+            back[here] = add_back
+
+        @pl.when(step != 0)
+        def _():
+            ff[here] += add_ff
+            back[here] += add_back
+
+        fc1 = fc1 + jnp.sum(g_pre.astype(F32), axis=0, keepdims=True)
+    fc1_sum[0] = jnp.broadcast_to(fc1, (8, width))
+
+    @pl.when(step == pl.num_programs(0) - 1)
+    def _():
+        totals = [jnp.zeros((1, width), F32)] * 4
+        for first in range(0, rows, part):
+            here = pl.ds(first, part)
+            slide = first // part
+            value = mid[here]
+            result = (value + (ff[here] + small[3:4])).astype(BF)
+            xhat, rate = moments(value)
+            upstream = back[here]
+            cot_wide = cot_at(first).astype(F32)
+            grad = cot_wide + norm_back(xhat, rate, small[1:2], upstream)
+            low = grad.astype(BF)
+            back_rows = dot_nt(low, w_out[...]).astype(BF)
+            for side, ref in enumerate((grad_own, grad_other)):
+                output[side, slide] = result[2 * side * half : 2 * (side + 1) * half]
+                grad_mid[side, slide] = grad[2 * side * half : 2 * (side + 1) * half]
+                for parity in range(2):
+                    at = (2 * side + parity) * half
+                    ref[slide, parity, 0] = back_rows[at : at + half]
+            attn_t[:, first : first + part] = low.T
+            wide = low.astype(F32)
+            for index, piece in enumerate((wide, upstream * xhat, upstream, cot_wide)):
+                totals[index] = totals[index] + jnp.sum(piece, axis=0, keepdims=True)
+        sums[...] = rows_of((8, width), 0, totals)
+
+
+def weight_grad_kernel(place, *refs, partner):
+    groups = [refs[0:6], refs[6:12]]
+    outs = refs[12 + 2 * partner :]
+    width = refs[0].shape[0]
+    piece = width // 8
+    slot = pl.program_id(0)
+
+    def rows(index):
+        return slice(index // 2 * piece, (index // 2 + 1) * piece)
+
+    def over(index, other):
+        return sum(dot(group[index][...], group[other][0]) for group in groups)
+
+    second = over(1, 4)
+    for index in range(8):
+        side = (index % 2) ^ place[1]
+        part = second[index * piece : (index + 1) * piece]
+        if not partner:
+            outs[1][0, side, rows(index)] = part.astype(BF)
+            continue
+        part = (part + refs[13][0, side, rows(index)].astype(F32)).astype(BF)
+        for here, ref in enumerate(outs[2:]):
+
+            @pl.when(slot == here)
+            def _():
+                ref[side, rows(index)] = part
+
+    rest = over(2, 5)
+    missing = FIRST_COLUMNS - width - rest.shape[1]
+    rest = jnp.concatenate([rest, jnp.zeros((width, missing), F32)], 1)
+    for first, value in ((0, over(0, 3)), (width, rest)):
+        columns = slice(first, first + value.shape[1])
+        for index in range(8):
+            part = value[index * piece : (index + 1) * piece]
+            if not partner:
+                outs[0][(index % 2) ^ place[1], 0, rows(index), columns] = part.astype(BF)
+                continue
+            for side, ref in enumerate(outs[:2]):
+
+                @pl.when((index % 2) ^ place[1] == side)
+                def _():
+                    there = part + refs[12][side, 0, rows(index), columns].astype(F32)
+                    ref[0, rows(index), columns] = there.astype(BF)
+
+
+def side_fold_kernel(place, first, second, stay, send):
+    total = (first[...].astype(F32) + second[...].astype(F32)).astype(BF)
+    stay[...] = total[0]
+    send[...] = total[1]
+
+
+def z_fold_both_kernel(place, first, second, third, fourth, stay, send, total):
+    columns = first.shape[1]
+    half = first.shape[0] // 2
+    total[:, :columns] = (first[...].astype(F32) + second[...].astype(F32)).astype(BF)
+    total[:, columns:] = (third[...].astype(F32) + fourth[...].astype(F32)).astype(BF)
+    side = place[0] // 2
+    stay[...] = total[pl.ds(pl.multiple_of(side * half, 32), half)]
+    send[...] = total[pl.ds(pl.multiple_of((1 - side) * half, 32), half)]
+
+
+def hold_kernel(place, w1, w2, wo, offset, out):
+    width = w1.shape[1]
+    out[0:width] = w1[...]
+    out[width : 2 * width] = w2[...]
+    out[2 * width : 2 * width + wo.shape[0]] = wo[...]
+    rows = [part.astype(F32) for part in split3(offset[...])]
+    out[2 * width + wo.shape[0] :] = rows_of((16, width), 0, rows).astype(BF)
+
+
+def whole(shape):
+    return pl.BlockSpec(tuple(shape), lambda *_: (0,) * len(shape))
+
+
+def shaped(shape, dtype):
+    return jax.ShapeDtypeStruct(tuple(shape), dtype)
+
+
+def run(name, body, place, ins, outs, grid=(1,), scratch=(), tokens=(), aliases=None, mib=48, us=5):
+    arrays = [pair[0] for pair in ins]
+    in_specs = [whole(a.shape) if s is None else s for a, s in ins]
+    in_specs += [pl.BlockSpec(memory_space=pl.ANY)] * len(tokens)
+    out_specs = [whole(o.shape) if s is None else s for o, s in outs]
+    given, extra = len(ins), len(tokens)
+
+    def kernel(place_ref, *refs):
+        body(place_ref, *refs[:given], *refs[given + extra :])
+
+    return pl.pallas_call(
+        kernel,
+        grid_spec=pltpu.PrefetchScalarGridSpec(
+            num_scalar_prefetch=1,
+            grid=grid,
+            in_specs=in_specs,
+            out_specs=out_specs,
+            scratch_shapes=list(scratch),
+        ),
+        out_shape=[o for o, _ in outs],
+        input_output_aliases={k + 1: v for k, v in (aliases or {}).items()},
+        compiler_params=pltpu.CompilerParams(vmem_limit_bytes=mib * 1024 * 1024),
+        cost_estimate=pl.CostEstimate(
+            flops=int(COST * us * 1.1e9), transcendentals=0, bytes_accessed=int(COST * us * 3.6e6)
+        ),
+        name=name,
+    )(place, *arrays, *tokens)
+
+
+def swap(value, axis, bit):
+    return lax.ppermute(value, axis, [(i, i ^ bit) for i in range(lax.axis_size(axis))])
+
+
+def paired(body, given):
+    def kernel(place, *refs):
+        near, away = refs[given : given + 2]
+        slots = (near.at[0], near.at[1], away.at[0], away.at[1])
+        body(place, *refs[:given], *slots, *refs[given + 2 :])
+
+    return kernel
+
+
+def pair_kernel(place, near, away, out):
+    out[0] = near[1]
+    out[1] = away[1]
+
+
+def nested(
+    tiles,
+    coords,
+    lengths,
+    padding_mask,
+    ln1_gain,
+    ln1_bias,
+    query_key_value_weight,
+    qv_bias,
+    attention_output_weight,
+    attention_output_bias,
+    ln2_gain,
+    ln2_bias,
+    mlp_entry_matrix,
+    mlp_entry_offset,
+    feed_output_weight,
+    feed_output_bias,
+    cotangent,
+):
+    slides, rows, width = tiles.shape
+    group = slides // 2
+    half = rows // 2
+    lanes = 8 * half
+    mine = lanes // 2
+    local = query_key_value_weight.shape[2]
+    scale = 1.0 / math.sqrt(HEAD_DIM)
+    factor = scale * LOG2E
+    seq_index = lax.axis_index("seq")
+    head_index = lax.axis_index("head")
+    z, y = seq_index // 2, seq_index % 2
+    x, core = head_index // 2, head_index % 2
+    place = jnp.stack([z, y, x, core]).astype(jnp.int32)
+    parts = ((0, 1), (1, group - 1))
+    token = []
+
+    def step(name, body, ins, outs, **options):
+        made = run(name, body, place, ins, outs, tokens=list(token), **options)
+        token[:] = [made[-1]]
+        return made
+
+    def vm(*shape, dtype=BF):
+        return pltpu.VMEM(shape, dtype)
+
+    def bf(*shape):
+        return shaped(shape, BF)
+
+    def f32(*shape):
+        return shaped(shape, F32)
+
+    def plain(*arrays):
+        return [(array, None) for array in arrays]
+
+    def lead_block(*shape):
+        return pl.BlockSpec((1,) + shape, lambda k, p: (k,) + (0,) * len(shape))
+
+    def over_z(pieces):
+        return [(pieces[0], None)] + [(swap(pieces[k], "seq", 2 * k), None) for k in (1, 2, 3)]
+
+    def over_z_first(pair):
+        return pair[0], swap(pair[1], "seq", 4)
+
+    def over_z_second(pair):
+        near, away = pair
+        send = step("pair", pair_kernel, plain(near, away), [(shaped(near.shape, BF), None)], us=0.5)[0]
+        got = swap(send, "seq", 2)
+        return [(near, 0), (got, 0), (away, 0), (got, 1)]
+
+    def by_slide(slots):
+        out = []
+        for array, index in slots:
+            shape = array.shape[-2:]
+            if index is None:
+                out.append((array, lead_block(*shape)))
+            else:
+                out.append((array, pl.BlockSpec((None, 1) + shape, lambda k, p, i=index: (i, k, 0, 0))))
+        return out
+
+    def all_slides(slots):
+        out = []
+        for array, index in slots:
+            if index is None:
+                out.append((array, None))
+            else:
+                shape = array.shape[1:]
+                out.append((array, pl.BlockSpec((None,) + shape, lambda k, p, i=index: (i, 0, 0, 0))))
+        return out
+
+    total_len = padding_mask.shape[1]
+    positions = jnp.arange(total_len, dtype=jnp.int32)
+    valid = (positions[None, :] < lengths[:, None]) & (padding_mask == 1)
+    valid = valid.astype(BF).reshape(slides * 4, total_len // 4)
+    spot = jnp.arange(total_len // 4, dtype=jnp.int32)
+    lane = spot % lanes
+    chip = lane // half
+    there = (
+        (y ^ (chip & 1)) * lanes
+        + (x ^ ((chip >> 1) & 1)) * (lanes // 2)
+        + (core ^ (chip >> 2)) * rows
+        + 2 * (lane % half)
+        + spot // lanes
+    )
+    taken = (spot[:, None] == there[None, :]).astype(BF)
+    valid = jnp.einsum("rp,pl->rl", valid, taken, preferred_element_type=F32)
+    valid = valid.reshape(slides, 8, lanes)
+
+    weight = query_key_value_weight.reshape(width, 3, 4, HEAD_DIM).transpose(2, 1, 3, 0)
+    weight = weight.reshape(3 * local, width)
+    triple = jnp.stack([qv_bias[0], jnp.zeros_like(qv_bias[0]), qv_bias[1]])
+    triple = triple.reshape(3, 4, HEAD_DIM).transpose(1, 0, 2).reshape(3 * local, 1)
+    gains = jnp.concatenate([jnp.stack([ln1_gain, ln1_bias]), jnp.zeros((6, width), F32)], 0)
+    small = jnp.concatenate(
+        [
+            jnp.stack([attention_output_bias, ln2_gain, ln2_bias, feed_output_bias]),
+            jnp.zeros((4, width), F32),
+        ],
+        0,
+    )
+    quarter = width // 4
+    freq = jnp.exp(-jnp.log(10000.0) * jnp.arange(quarter, dtype=F32) / quarter)
+    angle = jnp.arange(256, dtype=F32)[:, None] * freq
+    table = jnp.stack(split3(jnp.concatenate([jnp.sin(angle), jnp.cos(angle)], axis=-1)))
+
+    bases, cots, blocks = [], [], []
+    pending = []
+    for first, count in parts:
+
+        def at_side(side, depth, first=first):
+            return pl.BlockSpec(
+                (1, rows, depth), lambda k, p: ((p[1] ^ side) * group + first + k, 0, 0)
+            )
+
+        both = pl.BlockSpec((2, 1, rows, width), lambda k, p: (0, k, 0, 0))
+        piece = pl.BlockSpec((1, 2, half, width), lambda k, p: (k, 0, 0, 0))
+        pair = (2, count, rows, width)
+        ins = []
+        for array, depth in ((tiles, width), (coords, 2), (cotangent, width)):
+            ins += [(array, at_side(0, depth)), (array, at_side(1, depth))]
+        base, cot, own, other = step(
+            "entry",
+            entry_kernel,
+            ins + plain(table),
+            [
+                (f32(*pair), both),
+                (bf(*pair), both),
+                (bf(count, 2, half, width), piece),
+                (bf(count, 2, half, width), piece),
+            ],
+            grid=(count,),
+            us=2.2 * count,
+        )
+        bases.append(base)
+        cots.append(cot)
+        shape = (count, 2, 1, half, width)
+        pending.append((own.reshape(shape), swap(other, "seq", 1).reshape(shape)))
+
+    def join(first, second):
+        shape = first.shape[:2] + (2 * first.shape[2],) + first.shape[3:]
+        return step("join", join_kernel, plain(first, second), [(shaped(shape, BF), None)], us=1)[0]
+
+    pending = [join(*pair) for pair in pending]
+    pending = [(block, swap(block, "head", 2)) for block in pending]
+
+    qkvs, far_blocks = [None, None], [None, None]
+    near_outs, near_grads = [None] * group, [None] * group
+
+    def project(g):
+        first, count = parts[g]
+        outs = step(
+            "qkv",
+            qkv_kernel,
+            [(blocks[g][0], lead_block(2, mine, width)), (blocks[g][1], lead_block(2, mine, width))]
+            + plain(weight, triple, gains),
+            [(bf(count, 4, 2, TRIPLE, lanes), lead_block(4, 2, TRIPLE, lanes))]
+            + [(bf(count, TRIPLE, lanes), lead_block(TRIPLE, lanes))] * 4,
+            grid=(count,),
+            us=2.2 * count,
+        )
+        qkvs[g] = outs[0]
+        far_blocks[g] = over_z(outs[1:])
+
+    def spread_columns(g):
+        block = join(*pending[g])
+        shape = (parts[g][1], 2, mine, width)
+        blocks.append((block.reshape(shape), swap(block, "head", 1).reshape(shape)))
+
+    def head_block(k, height):
+        return pl.BlockSpec((1, 1, 2, height, lanes), lambda i, p: (k, i, 0, 0, 0))
+
+    def each_head(height):
+        return pl.BlockSpec((1, 2, height, lanes), lambda i, p: (i, 0, 0, 0))
+
+    def near_forward(g, k):
+        slide = parts[g][0] + k
+        near_outs[slide] = step(
+            "near_forward",
+            partial(near_forward_kernel, slide=slide, factor=factor),
+            [(qkvs[g], head_block(k, TRIPLE)), (valid, None)],
+            [(f32(4, 2, ACC_ROWS, lanes), each_head(ACC_ROWS))],
+            grid=(4,),
+            scratch=[vm(2, lanes, AUG), vm(2, OUT_ROWS, lanes), vm(2, lanes, lanes, dtype=F32)],
+            us=6.6,
+        )[0]
+
+    far_outs, kept, merged = [None, None], [None, None], [None, None]
+
+    def far_kernel(name, body, g, ins, height, scratch, two_steps, us, **options):
+        first, count = parts[g]
+        body = partial(body, first_slide=first, half=half, factor=factor, **options)
+        if two_steps:
+            body = paired(body, len(ins))
+            block = pl.BlockSpec((2, 1, height, lanes), lambda k, p: (0, k, 0, 0))
+            outs = [(bf(2, count, height, lanes), block)] * 2
+        else:
+            outs = [(bf(count, height, lanes), lead_block(height, lanes))] * 4
+        outs = step(name, body, ins, outs, grid=(count,), scratch=scratch, us=us * count)
+        return over_z_first(outs) if two_steps else over_z(outs)
+
+    def far_forward(g, two_steps):
+        far_outs[g] = far_kernel(
+            "far_forward",
+            far_forward_kernel,
+            g,
+            by_slide(far_blocks[g]) + plain(valid),
+            OUT_ROWS,
+            [
+                vm(4, lanes, AUG),
+                vm(4, OUT_ROWS, lanes),
+                vm(4, AUG, lanes),
+                vm(4, AUG, lanes),
+                vm(4, lanes, lanes, dtype=F32),
+                vm(4, OUT_ROWS, lanes),
+            ],
+            two_steps,
+            8,
+        )
+
+    def merge(g):
+        first, count = parts[g]
+        turned = bf(count, 2, 4, half, local)
+        kept[g], stay, send = step(
+            "merge",
+            merge_kernel,
+            plain(*near_outs[first : first + count]) + all_slides(far_outs[g]),
+            [(f32(count, 4, 2, ACC_ROWS, lanes), None), (turned, None), (turned, None)],
+            scratch=[vm(4, OUT_ROWS, lanes)],
+            us=count,
+        )
+        merged[g] = (stay, swap(send, "head", 1))
+
+    def widen(g, axis, bit):
+        pieces = [(a, None) for a in merged[g]]
+        count, _, blocks_here, _, columns = merged[g][0].shape
+        shape = bf(count, 2, blocks_here // 2, half, 2 * columns)
+        stay, send = step("widen", widen_kernel, pieces, [(shape, None)] * 2, us=1)
+        merged[g] = (stay, swap(send, axis, bit))
+
+    spread_columns(0)
+    project(0)
+    near_forward(0, 0)
+    spread_columns(1)
+    packed = step(
+        "hold",
+        hold_kernel,
+        plain(
+            mlp_entry_matrix,
+            feed_output_weight,
+            attention_output_weight,
+            mlp_entry_offset[None],
+        ),
+        [(bf(2 * width + local + 16, width), None)],
+        us=2,
+    )[0]
+    packed = lax.all_gather(packed, "head")
+    project(1)
+    far_forward(0, True)
+    near_forward(1, 0)
+    far_outs[0] = over_z_second(far_outs[0])
+    near_forward(1, 1)
+    merge(0)
+    far_forward(1, False)
+    widen(0, "head", 2)
+
+    def last_widen(g):
+        first, second = merged[g]
+        count = first.shape[0]
+        shape = bf(count, 2, 1, half, width)
+        stay, send = step("widen", widen_kernel, plain(first, second), [(shape, None)] * 2, us=1)
+        shape = (count, 2, half, width)
+        merged[g] = (stay.reshape(shape), swap(send, "seq", 1).reshape(shape))
+
+    last_widen(0)
+    merge(1)
+    widen(1, "head", 2)
+
+    def head_of(i, p):
+        return (p[2] ^ (i % 2)) * 2 + (p[3] ^ (i // 2))
+
+    def weight_spec(height, index, slot=None):
+        if slot is None:
+            return pl.BlockSpec((1, height, width), lambda i, p: (head_of(i, p), index, 0))
+        return pl.BlockSpec((1, height, width), lambda i, p: (head_of(slot, p), index, 0))
+
+    def slot_block(*shape):
+        return pl.BlockSpec((1,) + shape, lambda i, p: (i,) + (0,) * len(shape))
+
+    owned, given, grads = [None, None], [None, None], [None, None]
+
+    def feed_forward(g):
+        count = parts[g][1]
+        here = 2 * count * rows
+        pair = (2, count, rows, width)
+        turned = bf(width, here)
+        piece = bf(count, 2, 1, half, width)
+        outs = step(
+            "mlp",
+            mlp_kernel,
+            plain(bases[g], *merged[g], cots[g])
+            + [(packed, weight_spec(width, 0)), (packed, weight_spec(width, 1))]
+            + [(packed, weight_spec(local, 2 * width // local, slot)) for slot in SLOT_ORDER]
+            + [(packed, weight_spec(16, (2 * width + local) // 16)), (small, None)],
+            [
+                (bf(*pair), None),
+                (f32(*pair), None),
+                (piece, None),
+                (piece, None),
+                (bf(4, here, width), slot_block(here, width)),
+                (bf(4, here, width), slot_block(here, width)),
+                (turned, None),
+                (turned, None),
+                (turned, None),
+                (bf(4, here, local), None),
+                (f32(8, width), None),
+                (f32(4, 8, width), slot_block(8, width)),
+            ],
+            grid=(4,),
+            scratch=[
+                vm(width, width),
+                vm(here, width, dtype=F32),
+                vm(here, width),
+                vm(here, width),
+                vm(here, width, dtype=F32),
+                vm(here, width, dtype=F32),
+            ],
+            mib=60,
+            us=5 + 10 * count,
+        )
+        output, grad_mid, own, other, hidden, g_pre, normed_t, cot_t, attn_t, slots, sums, fc1 = outs
+        owned[g] = (output, grad_mid, sums, fc1)
+        grads[g] = (normed_t, cot_t, attn_t, g_pre, hidden, slots)
+        given[g] = (own, swap(other, "seq", 1))
+
+    def narrow(g, axis, bit):
+        first, second = given[g]
+        count, _, blocks_here, _, columns = first.shape
+        shape = bf(count, 2, 2 * blocks_here, half, columns // 2)
+        stay, send = step("narrow", narrow_kernel, plain(first, second), [(shape, None)] * 2, us=1)
+        given[g] = (stay, swap(send, axis, bit))
+
+    feed_forward(0)
+    last_widen(1)
+    feed_forward(1)
+
+    tall = width // 2
+    sent = [
+        (bf(2, 2, tall, FIRST_COLUMNS), pl.BlockSpec((2, 1, tall, FIRST_COLUMNS), lambda i, p: (0, i, 0, 0))),
+        (bf(2, 2, tall, width), pl.BlockSpec((1, 2, tall, width), lambda i, p: (i, 0, 0, 0))),
+    ]
+    kept_w = [(bf(2, tall, FIRST_COLUMNS), slot_block(tall, FIRST_COLUMNS))] * 2
+    kept_w += [(bf(2, tall, width), None)] * 2
+
+    def weight_grads(first, partner):
+        def at(*shape):
+            return pl.BlockSpec((1,) + shape, lambda i, p: (i + first, 0, 0))
+
+        ins = []
+        for (_, count), (normed_t, cot_t, attn_t, g_pre, hidden, slots) in zip(parts, grads):
+            here = 2 * count * rows
+            ins += plain(normed_t, cot_t, attn_t)
+            ins += [(g_pre, at(here, width)), (hidden, at(here, width)), (slots, at(here, local))]
+        return step(
+            "weight_grads",
+            partial(weight_grad_kernel, partner=len(partner) // 2),
+            ins + [(value, spec) for value, (_, spec) in zip(partner, sent)],
+            kept_w if partner else sent,
+            grid=(2,),
+            mib=56,
+            us=12,
+        )
+
+    def split_fold(pair, axis, bit):
+        shape = pair[0].shape[1:]
+        stay, send = step(
+            "split_fold", side_fold_kernel, plain(*pair), [(shaped(shape, BF), None)] * 2, us=2
+        )
+        return stay, swap(send, axis, bit)
+
+    grad_rows, far_grads, far_backs = [None, None], [None, None], [None, None]
+    backs, sums_so_far = [None, None], []
+
+    def rows_of_gradients(g):
+        first, count = parts[g]
+        pieces = [value.reshape(count, 2, mine, local) for value in given[g]]
+        slot = pl.BlockSpec((1, OUT_ROWS, lanes), lambda k, p: (first + k, 0, 0))
+        any_spec = pl.BlockSpec(memory_space=pl.ANY)
+        before = [(array, any_spec) for array in far_grads[0] or []]
+        outs = step(
+            "gradient_rows",
+            gradient_rows_kernel,
+            [(value, lead_block(2, mine, local)) for value in pieces]
+            + [(kept[g], lead_block(4, 2, ACC_ROWS, lanes))]
+            + before,
+            [(bf(count, 4, 2, OUT_ROWS, lanes), lead_block(4, 2, OUT_ROWS, lanes))]
+            + [(bf(group, OUT_ROWS, lanes), slot)] * 4,
+            grid=(count,),
+            aliases={3 + k: 1 + k for k in range(4)} if before else None,
+            us=count,
+        )
+        grad_rows[g] = outs[0]
+        far_grads[0] = outs[1:] if first == 0 else over_z(outs[1:])
+
+    def near_backward(g, k):
+        slide = parts[g][0] + k
+        near_grads[slide] = step(
+            "near_backward",
+            partial(near_backward_kernel, slide=slide, factor=factor, scale=scale),
+            [(qkvs[g], head_block(k, TRIPLE)), (valid, None), (grad_rows[g], head_block(k, OUT_ROWS))],
+            [(bf(4, 2, TRIPLE, lanes), each_head(TRIPLE))],
+            grid=(4,),
+            scratch=[
+                vm(2, lanes, AUG),
+                vm(2, OUT_ROWS, lanes),
+                vm(2, lanes, OUT_ROWS),
+                vm(2, AUG, lanes),
+                vm(2, OUT_ROWS, lanes),
+                vm(2, lanes, OUT_ROWS),
+                vm(2, lanes, OUT_ROWS),
+            ],
+            us=9.7,
+        )[0]
+
+    def far_backward(g, two_steps):
+        first = parts[g][0]
+        grads_here = [
+            (array, pl.BlockSpec((1, OUT_ROWS, lanes), lambda k, p: (first + k, 0, 0)))
+            for array, _ in far_grads[0]
+        ]
+        far_backs[g] = far_kernel(
+            "far_backward",
+            far_backward_kernel,
+            g,
+            by_slide(far_blocks[g]) + grads_here + plain(valid),
+            TRIPLE,
+            [
+                vm(4, lanes, AUG),
+                vm(4, OUT_ROWS, lanes),
+                vm(4, lanes, OUT_ROWS),
+                vm(4, AUG, lanes),
+                vm(4, AUG, lanes),
+                vm(4, OUT_ROWS, lanes),
+                vm(4, lanes, OUT_ROWS),
+                vm(4, lanes, OUT_ROWS),
+                vm(4, OUT_ROWS, lanes, dtype=F32),
+                vm(4, TRIPLE, lanes),
+            ],
+            two_steps,
+            12,
+            scale=scale,
+        )
+
+    def project_back(g, ends):
+        first, count = parts[g]
+        begins = not ends
+        if ends:
+            wgrads = [(bf(width // 2, 3 * local + 64), None)] * 2
+        else:
+            wgrads = [(f32(3 * local, width), None)]
+        back = bf(count, 2, 4, half, width)
+        outs = step(
+            "qkv_backward",
+            partial(qkv_backward_kernel, count=count, begins=begins, ends=ends),
+            plain(*near_grads[first : first + count])
+            + all_slides(far_backs[g])
+            + plain(*blocks[g], weight, gains, *sums_so_far),
+            wgrads + [(f32(8, 3 * local), None), (f32(8, width), None), (back, None), (back, None)],
+            scratch=[vm(4, TRIPLE, lanes)] + ([vm(3 * local, width, dtype=F32)] if ends else []),
+            us=2 + 4 * count,
+        )
+        sums_so_far[:] = outs[:-2]
+        backs[g] = (outs[-2], swap(outs[-1], "head", 1))
+
+    def fold_back(g, axis, bit):
+        first, second = backs[g]
+        count, _, blocks_here, _, _ = first.shape
+        shape = bf(count, 2, blocks_here // 2, half, width)
+        stay, send = step("fold", fold_kernel, plain(first, second), [(shape, None)] * 2, us=1)
+        backs[g] = (stay, swap(send, axis, bit))
+
+    results = []
+
+    def leave(g):
+        first, count = parts[g]
+        output, grad_mid = owned[g][:2]
+        pieces = [value.reshape(count, 2, half, width) for value in backs[g]]
+        piece = pl.BlockSpec((1, 2, half, width), lambda s, k, p: (k, 0, 0, 0))
+        row = pl.BlockSpec((1, 1, rows, width), lambda s, k, p: (s, k, 0, 0))
+        out = pl.BlockSpec((1, rows, width), lambda s, k, p: ((p[1] ^ s) * group + first + k, 0, 0))
+        any_spec = pl.BlockSpec(memory_space=pl.ANY)
+        results[:] = step(
+            "leave",
+            exit_kernel,
+            [(value, piece) for value in pieces]
+            + [(bases[g], row), (grad_mid, row), (output, row), (gains, None)]
+            + [(value, any_spec) for value in results],
+            [(bf(*tiles.shape), out)] * 2,
+            grid=(2, count),
+            aliases={6: 0, 7: 1} if results else None,
+            us=1 + 1.3 * count,
+        )
+
+    def z_fold(pair, bit):
+        first, second = pair
+        shape = bf(first.shape[0] // 2, first.shape[1])
+        stay, send = step(
+            "z_fold",
+            partial(z_fold_kernel, bit=bit),
+            plain(first, second),
+            [(shape, None)] * 2,
+            scratch=[vm(*first.shape)],
+            us=1,
+        )
+        return stay, swap(send, "seq", 4 if bit else 2)
+
+    def small_step(name, body, pair, extra=()):
+        return step(name, body, plain(*pair, *extra), [(f32(8, width), None)], us=0.5)[0]
+
+    narrow(0, "head", 2)
+    sent_w = weight_grads(2, [])
+    narrow(0, "head", 1)
+    narrow(1, "head", 2)
+    rows_of_gradients(0)
+    near_backward(0, 0)
+    narrow(1, "head", 1)
+    outs = weight_grads(0, [swap(value, "head", 1) for value in sent_w])
+    first_w = (outs[0], swap(outs[1], "seq", 1))
+    second_w = (outs[2], swap(outs[3], "head", 2))
+    rows_of_gradients(1)
+    near_backward(1, 0)
+    far_backward(1, False)
+    second_w = split_fold(second_w, "seq", 1)
+    first_w = split_fold(first_w, "head", 2)
+    far_backward(0, True)
+    near_backward(1, 1)
+    far_backs[0] = over_z_second(far_backs[0])
+    stay, send = step(
+        "z_fold_both",
+        z_fold_both_kernel,
+        plain(*first_w, *second_w),
+        [(bf(tall // 2, FIRST_COLUMNS + width), None)] * 2,
+        scratch=[vm(tall, FIRST_COLUMNS + width)],
+        us=2,
+    )
+    folded = (stay, swap(send, "seq", 4))
+    project_back(1, False)
+    fold_back(1, "head", 2)
+    project_back(0, True)
+    stay, send, bias_sum, ln_sum = sums_so_far
+    grad_in = (stay, swap(send, "seq", 1))
+    stay, send, last = step(
+        "small_start",
+        small_start_kernel,
+        plain(*[owned[g][2] for g in range(2)], *[owned[g][3] for g in range(2)], ln_sum, bias_sum),
+        [(f32(8, width), None)] * 3,
+        us=0.5,
+    )
+    common = (stay, swap(send, "head", 1))
+    fold_back(0, "head", 2)
+    stay, send = step("small_middle", small_middle_kernel, plain(*common), [(f32(8, width), None)] * 2, us=0.5)
+    common = (stay, swap(send, "head", 2))
+    fold_back(1, "seq", 1)
+    grad_in = z_fold(grad_in, True)
+    common = small_step("small_last", small_last_kernel, common, [last])
+    common = (common, swap(common, "seq", 1))
+    fold_back(0, "seq", 1)
+    folded = z_fold(folded, False)
+    common = small_step("add", add_kernel, common)
+    common = (common, swap(common, "seq", 4))
+    leave(1)
+    grad_in = z_fold(grad_in, False)
+    common = small_step("add", add_kernel, common)
+    common = (common, swap(common, "seq", 2))
+    leave(0)
+    w_fc1_grad, w_fc2_grad, w_out_grad = step(
+        "weights_out",
+        weights_out_kernel,
+        plain(*folded),
+        [
+            (f32(width // 8, width), None),
+            (f32(width, width // 8), None),
+            (f32(local, width // 8), None),
+        ],
+        us=1.5,
+    )
+    w_qkv_grad = step(
+        "qkv_out", qkv_out_kernel, plain(*grad_in), [(f32(width // 8, 3, local), None)], us=1.5
+    )[0]
+    common = small_step("add", add_kernel, common)
+    per_head = common[7, : 3 * local].reshape(4, 3, HEAD_DIM).transpose(1, 0, 2).reshape(3, local)
+    tiles_grad, output = results
+    return (
+        output,
+        tiles_grad,
+        common[4],
+        common[5],
+        w_qkv_grad,
+        jnp.stack([per_head[0], per_head[2]]),
+        w_out_grad,
+        common[0],
+        common[1],
+        common[2],
+        w_fc1_grad,
+        common[6],
+        w_fc2_grad,
+        common[3],
+    )
+
+
+def nests(mesh, tiles, padding_mask):
+    sizes = (mesh.shape["seq"], mesh.shape["head"], tiles.shape[0])
+    return sizes == (8, 4, 6) and padding_mask.shape[1] <= SEG2
+
+
 def solution(mesh):
+    def program(*args):
+        one_span = nests(mesh, args[0], args[3])
+        return spread_out(mesh, nested if one_span else on_device)(*args)
+
+    return program
+
+
+def spread_out(mesh, body):
     placed = (
         P(None, ("seq", "head"), None),
         P(None, ("seq", "head"), None),
@@ -428,7 +1876,7 @@
         P(None, ("seq", "head"), None),
     )
     return jax.shard_map(
-        on_device,
+        body,
         mesh=mesh,
         in_specs=placed,
         out_specs=(

time: 2510 us -> 457 us (0.18)
  other arithmetic: 704 us -> 2.2 us
  local copies, waits for them, and re-layouts: 638 us -> 31.6 us
  waiting for transfers between devices: 624 us -> 107 us
  matrix products: 452 us -> 0.81 us
  Pallas kernels: 0 us -> 233 us
  starting transfers between devices: 4.78 us -> 62.8 us
  blocking collectives: 40.4 us -> 0 us
    reduce_sum x58 -> x0, other arithmetic: 500 us -> none  [the longest x16 443 us: pick(): jnp.sum(jnp.where(chosen.reshape(mask_shape(value, chosen)), split, jnp.z...]
    dot_general x222 -> x1, matrix products: 452 us -> 0.81 us  [nested(): valid = jnp.einsum('rp,pl->rl', valid, taken, preferred_element_type=F32)]
    reduce_scatter x8 -> x0, waiting for transfers between devices: 252 us -> none  [the longest x1 65.1 us: on_device(): lax.psum_scatter(grad_w_qkv.astype(jnp.bfloat16), 'seq', scatter_dimensio...]
    pallas_call x0 -> x59, Pallas kernels: none -> 233 us  [run(): pl.pallas_call(kernel, grid_spec=pltpu.PrefetchScalarGridSpec(num_scalar_...]
    all_gather x5 -> x1, waiting for transfers between devices: 225 us -> 0.01 us  [nested(): packed = lax.all_gather(packed, 'head')]
    broadcast_in_dim x49 -> x3, local copies, waits for them, and re-layouts: 173 us -> 0.01 us  [the longest x1 0.01 us: nested(): mlp_entry_offset[None]]
    unnamed x306 -> x201, local copies, waits for them, and re-layouts: 161 us -> 28.3 us
    convert_element_type x40 -> x2, other arithmetic: 113 us -> 0.24 us  [the longest x1 0.14 us: split3(): middle = rest.astype(BF)]
  transfers between devices with their start and end apart: 19 -> 60, of which waited for: 12 -> 20; matrix products, arithmetic and copies ran while one was open for 38% -> 1% of each run, Pallas kernels for 0% -> 47%
where the time goes in v1:
time: 457 us; the launch traced here: 453 us
  Pallas kernels  233 us (51%)
  waiting for transfers between devices  107 us (23%)
  starting transfers between devices  62.8 us (14%)
  local copies, waits for them, and re-layouts  31.6 us (7%)
  between operations  15.8 us (3%)
    pallas_call x59, Pallas kernels, run(): pl.pallas_call(kernel, grid_spec=pltpu.PrefetchScalarGridSpec(num_scalar_...  233 us
    ppermute x59, waiting for transfers between devices, swap(): lax.ppermute(value, axis, [(i, i ^ bit) for i in range(lax.axis_size(axis...  107 us
    ppermute x59, starting transfers between devices, swap(): lax.ppermute(value, axis, [(i, i ^ bit) for i in range(lax.axis_size(axis...  62.8 us
    unnamed x201, local copies, waits for them, and re-layouts  28.3 us
  transfers between devices with their start and end apart: 60, of which 20 were waited for; matrix products, arithmetic and copies ran while one was open for 1% of the time, Pallas kernels for 47%

profile of v1, /device:TPU:0, one launch (start us, length us, event | category | flops | bytes accessed | tf_op | source)
XLA Modules:
  0.0 453.3 jit_solution(14084881732999388688)
XLA Ops:
  17.3 4.4 entry.3
  25.5 7.7 %collective-permute-done.2 = bf16[2,2,64,768]{3,2,1,0:T(8,128)(2,1)S(1)} collective-permute-done((bf16[2,2,64,768]{3,2,1,0:T(8,128)(2,1)S(1)}, bf16[2,2,64,768]{3,2,1,0:T(8,128)(2,1)S(1)}, u32[]{:S(2)}, u32[]{:S(2)}) %collective-permute-start.2) | collective-permute-done | bytes 393248 | tf_op jit(solution)/shard_map/ppermute | solution.py:1202
  40.9 6.6 %near_forward.3.refs_2_.refs_0_ = f32[4,2,56,512]{3,2,1,0:T(8,128)S(1)} custom-call(s32[4]{0:T(128)S(1)} %pad_add_fusion.place_ref, bf16[1,4,2,144,512]{4,3,2,1,0:T(8,128)(2,1)S(1)} %get-tuple-element.153.refs_0_, f32[6,8,512]{2,1,0:T(8,128)S(1)} %reshape.328.refs_1_.refs_4_.refs_8_, bf16[1,144,512]{2,1,0:T(8,128)(2,1)S(1)} %get-tuple-element.155.refs_2_), custom_call_target="tpu_custom_call" | custom-call | flops 18150000640 | bytes 59400000 | tf_op jit(solution)/shard_map/near_forward/pallas_call | solution.py:1182
  48.6 9.0 %collective-permute-done.7.refs_1_ = bf16[2,2,2,64,768]{4,3,2,1,0:T(8,128)(2,1)S(1)} collective-permute-done((bf16[2,2,2,64,768]{4,3,2,1,0:T(8,128)(2,1)}, bf16[2,2,2,64,768]{4,3,2,1,0:T(8,128)(2,1)S(1)}, u32[]{:S(2)}, u32[]{:S(2)}) %collective-permute-start.7) | collective-permute-done | bytes 786464 | tf_op jit(solution)/shard_map/ppermute | solution.py:1202
  60.6 3.9 collective-permute-start.6
  65.2 4.0 qkv.3
  69.1 3.7 collective-permute-start.14
  73.2 11.2 %collective-permute-done.5.refs_2_ = bf16[1,144,512]{2,1,0:T(8,128)(2,1)S(1)} collective-permute-done((bf16[1,144,512]{2,1,0:T(8,128)(2,1)S(1)}, bf16[1,144,512]{2,1,0:T(8,128)(2,1)S(1)}, u32[]{:S(2)}, u32[]{:S(2)}) %collective-permute-start.5) | collective-permute-done | bytes 147488 | tf_op jit(solution)/shard_map/ppermute | solution.py:1202
  84.4 7.7 %far_forward.2 = (bf16[2,1,64,512]{3,2,1,0:T(8,128)(2,1)S(1)}, bf16[2,1,64,512]{3,2,1,0:T(8,128)(2,1)S(1)}) custom-call(s32[4]{0:T(128)S(1)} %pad_add_fusion.place_ref, bf16[1,144,512]{2,1,0:T(8,128)(2,1)S(1)} %get-tuple-element.156.refs_0_, bf16[1,144,512]{2,1,0:T(8,128)(2,1)S(1)} %collective-permute-done.4.refs_1_, ...), custom_call_target="tpu_custom_call" | custom-call | flops 22000001024 | bytes 72000000 | tf_op jit(solution)/shard_map/far_forward/pallas_call | solution.py:1182
  95.3 6.6 %near_forward.4.refs_2_.refs_0_ = f32[4,2,56,512]{3,2,1,0:T(8,128)S(1)} custom-call(s32[4]{0:T(128)S(1)} %pad_add_fusion.place_ref, bf16[2,4,2,144,512]{4,3,2,1,0:T(8,128)(2,1)S(1)} %copy-done.65, f32[6,8,512]{2,1,0:T(8,128)S(1)} %reshape.328.refs_1_.refs_4_.refs_8_, bf16[2,1,64,512]{3,2,1,0:T(8,128)(2,1)S(1)} %get-tuple-element.161.refs_2_), custom_call_target="tpu_custom_call" | custom-call | flops 18150000640 | bytes 59400000 | tf_op jit(solution)/shard_map/near_forward/pallas_call | solution.py:1182
  104.4 6.6 %near_forward.5.refs_5_.refs_1_ = f32[4,2,56,512]{3,2,1,0:T(8,128)S(1)} custom-call(s32[4]{0:T(128)S(1)} %pad_add_fusion.place_ref, bf16[2,4,2,144,512]{4,3,2,1,0:T(8,128)(2,1)S(1)} %copy-done.65, f32[6,8,512]{2,1,0:T(8,128)S(1)} %reshape.328.refs_1_.refs_4_.refs_8_, bf16[2,1,64,512]{3,2,1,0:T(8,128)(2,1)S(1)} %pair.2.refs_2_), custom_call_target="tpu_custom_call" | custom-call | flops 18150000640 | bytes 59400000 | tf_op jit(solution)/shard_map/near_forward/pallas_call | solution.py:1182
  115.1 15.1 %far_forward.3 = (bf16[2,64,512]{2,1,0:T(8,128)(2,1)S(1)}, bf16[2,64,512]{2,1,0:T(8,128)(2,1)S(1)}, bf16[2,64,512]{2,1,0:T(8,128)(2,1)S(1)}, bf16[2,64,512]{2,1,0:T(8,128)(2,1)S(1)}) custom-call(s32[4]{0:T(128)S(1)} %pad_add_fusion.place_ref, bf16[2,144,512]{2,1,0:T(8,128)(2,1)S(1)} %get-tuple-element.165.refs_0_, ...), custom_call_target="tpu_custom_call" | custom-call | flops 44000002048 | bytes 144000000 | tf_op jit(solution)/shard_map/far_forward/pallas_call | solution.py:1182
  139.5 5.4 %collective-permute-done.17.refs_3_ = bf16[2,64,512]{2,1,0:T(8,128)(2,1)S(1)} collective-permute-done((bf16[2,64,512]{2,1,0:T(8,128)(2,1)S(1)}, bf16[2,64,512]{2,1,0:T(8,128)(2,1)S(1)}, u32[]{:S(2)}, u32[]{:S(2)}) %collective-permute-start.17) | collective-permute-done | bytes 131104 | tf_op jit(solution)/shard_map/ppermute | solution.py:1202
  151.6 3.8 collective-permute-done.16
  156.0 14.5 %mlp.2 = (bf16[2,1,128,768]{3,2,1,0:T(8,128)(2,1)}, f32[2,1,128,768]{3,2,1,0:T(8,128)}, bf16[1,2,1,64,768]{4,3,2,1,0:T(8,128)(2,1)}, bf16[1,2,1,64,768]{4,3,2,1,...) custom-call(s32[4]{0:T(128)} %copy-done.1, ...), custom_call_target="tpu_custom_call" | custom-call | flops 41250000896 | bytes 135000000 | tf_op jit(solution)/shard_map/mlp/pallas_call | solution.py:1182
  174.8 10.0 %collective-permute-done.23 = bf16[2,2,1,64,768]{4,3,1,0,2:T(8,128)(2,1)S(1)} collective-permute-done((bf16[2,2,1,64,768]{4,3,1,0,2:T(8,128)(2,1)S(1)}, bf16[2,2,1,64,768]{4,3,1,0,2:T(8,128)(2,1)S(1)}, u32[]{:S(2)}, u32[]{:S(2)}) %collective-permute-start.23) | collective-permute-done | bytes 393248 | tf_op jit(solution)/shard_map/ppermute | solution.py:1202
  185.6 24.3 %mlp.3 = (bf16[2,2,128,768]{3,2,1,0:T(8,128)(2,1)}, f32[2,2,128,768]{3,2,1,0:T(8,128)}, bf16[2,2,1,64,768]{4,3,2,1,0:T(8,128)(2,1)}, bf16[2,2,1,64,768]{4,3,2,1,...) custom-call(s32[4]{0:T(128)} %copy-done.1, ...), custom_call_target="tpu_custom_call" | custom-call | flops 68750000128 | bytes 225000000 | tf_op jit(solution)/shard_map/mlp/pallas_call | solution.py:1182
  213.6 10.4 %weight_grads.2 = (bf16[2,2,384,1024]{3,2,1,0:T(8,128)(2,1)}, bf16[2,2,384,768]{3,2,1,0:T(8,128)(2,1)}) custom-call(s32[4]{0:T(128)} %copy-done.1, bf16[768,256]{1,0:T(8,128)(2,1)} %get-tuple-element.191.refs_0_, bf16[768,256]{1,0:T(8,128)(2,1)} %get-tuple-element.192.refs_1_, bf16[768,256]{1,0:T(8,128)(2,1)} %get-tuple-element.193.refs_2_, ...), custom_call_target="tpu_custom_call" | custom-call | flops 32999999488 | bytes 108000000 | tf_op jit(solution)/shard_map/weight_grads/pallas_call | solution.py:1182
  233.2 9.7 %near_backward.3.refs_2_.refs_0_ = bf16[4,2,144,512]{3,2,1,0:T(8,128)(2,1)S(1)} custom-call(s32[4]{0:T(128)S(1)} %copy-done.4, bf16[1,4,2,144,512]{4,3,2,1,0:T(8,128)(2,1)S(1)} %copy-done.60, f32[6,8,512]{2,1,0:T(8,128)S(1)} %reshape.328.refs_1_.refs_4_.refs_8_, bf16[1,4,2,64,512]{4,3,2,1,0:T(8,128)(2,1)S(1)} %get-tuple-element.210.refs_2_, ...), custom_call_target="tpu_custom_call" | custom-call | flops 26674999296 | bytes 87300000 | tf_op jit(solution)/shard_map/near_backward/pallas_call | solution.py:1182
  245.5 13.1 %weight_grads.3 = (bf16[2,384,1024]{2,1,0:T(8,128)(2,1)}, bf16[2,384,1024]{2,1,0:T(8,128)(2,1)}, bf16[2,384,768]{2,1,0:T(8,128)(2,1)}, bf16[2,384,768]{2,1,0:T(8,128)(2,1)}) custom-call(s32[4]{0:T(128)} %copy-done.1, bf16[768,256]{1,0:T(8,128)(2,1)} %get-tuple-element.191.refs_0_, bf16[768,256]{1,0:T(8,128)(2,1)} %get-tuple-element.192.refs_1_, ...), custom_call_target="tpu_custom_call" | custom-call | flops 32999999488 | bytes 108000000 | tf_op jit(solution)/shard_map/weight_grads/pallas_call | solution.py:1182
  268.6 9.7 %near_backward.4.refs_9_.refs_0_ = bf16[4,2,144,512]{3,2,1,0:T(8,128)(2,1)S(1)} custom-call(s32[4]{0:T(128)S(1)} %copy-done.5, bf16[2,4,2,144,512]{4,3,2,1,0:T(8,128)(2,1)S(1)} %copy-done.66, f32[6,8,512]{2,1,0:T(8,128)S(1)} %reshape.328.refs_1_.refs_4_.refs_8_, bf16[2,4,2,64,512]{4,3,2,1,0:T(8,128)(2,1)S(1)} %get-tuple-element.228.refs_2_, ...), custom_call_target="tpu_custom_call" | custom-call | flops 26674999296 | bytes 87300000 | tf_op jit(solution)/shard_map/near_backward/pallas_call | solution.py:1182
  282.4 23.9 %far_backward.2 = (bf16[2,144,512]{2,1,0:T(8,128)(2,1)S(1)}, bf16[2,144,512]{2,1,0:T(8,128)(2,1)S(1)}, bf16[2,144,512]{2,1,0:T(8,128)(2,1)S(1)}, bf16[2,144,512]{2,1,0:T(8,128)(2,1)S(1)}) custom-call(s32[4]{0:T(128)S(1)} %copy-done.5, bf16[2,144,512]{2,1,0:T(8,128)(2,1)S(1)} %copy-done.79, bf16[2,144,512]{2,1,0:T(8,128)(2,1)S(1)} %copy-done.27, ...), custom_call_target="tpu_custom_call" | custom-call | flops 65999998976 | bytes 216000000 | tf_op jit(solution)/shard_map/far_backward/pallas_call | solution.py:1182
  306.4 3.7 collective-permute-start.38
  315.4 12.2 %far_backward.3 = (bf16[2,1,144,512]{3,2,1,0:T(8,128)(2,1)S(1)}, bf16[2,1,144,512]{3,2,1,0:T(8,128)(2,1)S(1)}) custom-call(s32[4]{0:T(128)S(1)} %copy-done.5, bf16[1,144,512]{2,1,0:T(8,128)(2,1)S(1)} %copy-done.77, bf16[1,144,512]{2,1,0:T(8,128)(2,1)S(1)} %copy-done.34, bf16[1,144,512]{2,1,0:T(8,128)(2,1)S(1)} %copy-done.36, ...), custom_call_target="tpu_custom_call" | custom-call | flops 32999999488 | bytes 108000000 | tf_op jit(solution)/shard_map/far_backward/pallas_call | solution.py:1182
  330.9 9.8 %near_backward.5.refs_2_.refs_1_ = bf16[4,2,144,512]{3,2,1,0:T(8,128)(2,1)S(1)} custom-call(s32[4]{0:T(128)S(1)} %copy-done.5, bf16[2,4,2,144,512]{4,3,2,1,0:T(8,128)(2,1)S(1)} %copy-done.67, f32[6,8,512]{2,1,0:T(8,128)S(1)} %reshape.328.refs_1_.refs_4_.refs_8_, bf16[2,4,2,64,512]{4,3,2,1,0:T(8,128)(2,1)S(1)} %get-tuple-element.228.refs_2_, ...), custom_call_target="tpu_custom_call" | custom-call | flops 26674999296 | bytes 87300000 | tf_op jit(solution)/shard_map/near_backward/pallas_call | solution.py:1182
  344.1 13.0 %collective-permute-done.39.refs_4_ = bf16[2,144,512]{2,1,0:T(8,128)(2,1)S(1)} collective-permute-done((bf16[2,144,512]{2,1,0:T(8,128)(2,1)S(1)}, bf16[2,144,512]{2,1,0:T(8,128)(2,1)S(1)}, u32[]{:S(2)}, u32[]{:S(2)}) %collective-permute-start.39) | collective-permute-done | bytes 294944 | tf_op jit(solution)/shard_map/ppermute | solution.py:1202
  357.2 9.4 %qkv_backward.2 = (f32[576,768]{1,0:T(8,128)}, f32[8,576]{1,0:T(8,128)S(1)}, f32[8,768]{1,0:T(8,128)S(1)}, bf16[2,2,4,64,768]{4,3,2,1,0:T(8,128)(2,1)}, bf16[2,2,4,64,768]{4,3,2,1,0:T(8,128)(2,1)}) custom-call(s32[4]{0:T(128)S(1)} %copy-done.5, bf16[4,2,144,512]{3,2,1,0:T(8,128)(2,1)S(1)} %copy-done.81, ...), custom_call_target="tpu_custom_call" | custom-call | flops 27499999232 | bytes 90000000 | tf_op jit(solution)/shard_map/qkv_backward/pallas_call | solution.py:1182
  376.1 5.6 %qkv_backward.3 = (bf16[384,640]{1,0:T(8,128)(2,1)S(1)}, bf16[384,640]{1,0:T(8,128)(2,1)S(1)}, f32[8,576]{1,0:T(8,128)S(1)}, f32[8,768]{1,0:T(8,128)S(1)}, bf16[...) custom-call(s32[4]{0:T(128)S(1)} %copy-done.5, bf16[4,2,144,512]{3,2,1,0:T(8,128)(2,1)} %copy-done.45, ...), custom_call_target="tpu_custom_call" | custom-call | flops 16499999744 | bytes 54000000 | tf_op jit(solution)/shard_map/qkv_backward/pallas_call | solution.py:1182
  388.7 13.4 %collective-permute-done.49.refs_1_ = bf16[2,2,2,64,768]{4,3,2,1,0:T(8,128)(2,1)S(1)} collective-permute-done((bf16[2,2,2,64,768]{4,3,2,1,0:T(8,128)(2,1)S(1)}, bf16[2,2,2,64,768]{4,3,2,1,0:T(8,128)(2,1)S(1)}, u32[]{:S(2)}, u32[]{:S(2)}) %collective-permute-start.49) | collective-permute-done | bytes 786464 | tf_op jit(solution)/shard_map/ppermute | solution.py:1202
  405.1 5.5 %collective-permute-done.47.refs_1_ = f32[8,768]{1,0:T(8,128)S(1)} collective-permute-done((f32[8,768]{1,0:T(8,128)S(1)}, f32[8,768]{1,0:T(8,128)S(1)}, u32[]{:S(2)}, u32[]{:S(2)}) %collective-permute-start.47) | collective-permute-done | bytes 24608 | tf_op jit(solution)/shard_map/ppermute | solution.py:1202
  412.5 9.0 %collective-permute-done.53.refs_1_ = bf16[192,1792]{1,0:T(8,128)(2,1)S(1)} collective-permute-done((bf16[192,1792]{1,0:T(8,128)(2,1)S(1)}, bf16[192,1792]{1,0:T(8,128)(2,1)S(1)}, u32[]{:S(2)}, u32[]{:S(2)}) %collective-permute-start.53) | collective-permute-done | bytes 688160 | tf_op jit(solution)/shard_map/ppermute | solution.py:1202
  426.2 4.0 leave.2
  (386 shorter events, 140.8 us)
Async XLA Ops:
  7.2 148.2 %all-gather.3.cloned.1.call-start = ((), (), s32[]{:S(2)}) async-start(), calls=%async_computation | async-start | bytes 13393920 | tf_op jit(solution)/shard_map/all_gather | solution.py:1491
  37.4 20.2 %collective-permute-start.7 = (bf16[2,2,2,64,768]{4,3,2,1,0:T(8,128)(2,1)}, bf16[2,2,2,64,768]{4,3,2,1,0:T(8,128)(2,1)S(1)}, u32[]{:S(2)}, u32[]{:S(2)}) collective-permute-start(bf16[2,2,2,64,768]{4,3,2,1,0:T(8,128)(2,1)} %copy-done.18), channel_id=1, source_target_pairs={{0,2},{1,3},{2,0},{3,1},{4,6},{5,7},{6,4},{7,5},{8,10},{9,11},{10,... | collective-permute-start | bytes 2359304 | tf_op jit(solution)/shard_map/ppermute | solution.py:1202
  60.6 23.8 %collective-permute-start.6 = (bf16[1,144,512]{2,1,0:T(8,128)(2,1)S(1)}, bf16[1,144,512]{2,1,0:T(8,128)(2,1)S(1)}, u32[]{:S(2)}, u32[]{:S(2)}) collective-permute-start(bf16[1,144,512]{2,1,0:T(8,128)(2,1)S(1)} %get-tuple-element.155.refs_2_), channel_id=1, source_target_pairs={{0,24},{4,28},{8,16},{12,20},{16,8},{20,12},{24,0},{28,4},{1,25},{... | collective-permute-start | bytes 442376 | tf_op jit(solution)/shard_map/ppermute | solution.py:1202
  64.5 19.9 %collective-permute-start.5 = (bf16[1,144,512]{2,1,0:T(8,128)(2,1)S(1)}, bf16[1,144,512]{2,1,0:T(8,128)(2,1)S(1)}, u32[]{:S(2)}, u32[]{:S(2)}) collective-permute-start(bf16[1,144,512]{2,1,0:T(8,128)(2,1)S(1)} %get-tuple-element.158), channel_id=1, source_target_pairs={{0,16},{4,20},{8,24},{12,28},{16,0},{20,4},{24,8},{28,12},{1,17},{... | collective-permute-start | bytes 442376 | tf_op jit(solution)/shard_map/ppermute | solution.py:1202
  69.1 45.9 %collective-permute-start.14 = (bf16[2,144,512]{2,1,0:T(8,128)(2,1)S(1)}, bf16[2,144,512]{2,1,0:T(8,128)(2,1)S(1)}, u32[]{:S(2)}, u32[]{:S(2)}) collective-permute-start(bf16[2,144,512]{2,1,0:T(8,128)(2,1)S(1)} %get-tuple-element.159.refs_5_), channel_id=1, source_target_pairs={{0,24},{4,28},{8,16},{12,20},{16,8},{20,12},{24,0},{28,4},{1,25},{... | collective-permute-start | bytes 884744 | tf_op jit(solution)/shard_map/ppermute | solution.py:1202
  92.2 22.8 %collective-permute-start.12 = (bf16[2,144,512]{2,1,0:T(8,128)(2,1)S(1)}, bf16[2,144,512]{2,1,0:T(8,128)(2,1)S(1)}, u32[]{:S(2)}, u32[]{:S(2)}) collective-permute-start(bf16[2,144,512]{2,1,0:T(8,128)(2,1)S(1)} %get-tuple-element.166), channel_id=1, source_target_pairs={{0,8},{4,12},{8,0},{12,4},{16,24},{20,28},{24,16},{28,20},{1,9},{5... | collective-permute-start | bytes 884744 | tf_op jit(solution)/shard_map/ppermute | solution.py:1202
  95.2 19.8 %collective-permute-start.13 = (bf16[2,144,512]{2,1,0:T(8,128)(2,1)S(1)}, bf16[2,144,512]{2,1,0:T(8,128)(2,1)S(1)}, u32[]{:S(2)}, u32[]{:S(2)}) collective-permute-start(bf16[2,144,512]{2,1,0:T(8,128)(2,1)S(1)} %get-tuple-element.167), channel_id=1, source_target_pairs={{0,16},{4,20},{8,24},{12,28},{16,0},{20,4},{24,8},{28,12},{1,17},{... | collective-permute-start | bytes 884744 | tf_op jit(solution)/shard_map/ppermute | solution.py:1202
  115.0 15.2 %collective-permute-start.11 = (bf16[1,2,4,64,192]{4,3,2,1,0:T(8,128)(2,1)S(1)}, bf16[1,2,4,64,192]{4,3,2,1,0:T(8,128)(2,1)S(1)}, u32[]{:S(2)}, u32[]{:S(2)}) collective-permute-start(bf16[1,2,4,64,192]{4,3,2,1,0:T(8,128)(2,1)S(1)} %get-tuple-element.164.refs_5_), channel_id=1, source_target_pairs={{0,1},{1,0},{2,3},{3,2},{4,5},{5,4},{6,7},{7,6},{8,9},{9,8},{10,11... | collective-permute-start | bytes 589832 | tf_op jit(solution)/shard_map/ppermute | solution.py:1202
  151.1 19.5 %collective-permute-start.22 = (bf16[2,2,2,64,384]{4,3,2,1,0:T(8,128)(2,1)S(1)}, bf16[2,2,2,64,384]{4,3,2,1,0:T(8,128)(2,1)S(1)}, u32[]{:S(2)}, u32[]{:S(2)}) collective-permute-start(bf16[2,2,2,64,384]{4,3,2,1,0:T(8,128)(2,1)S(1)} %get-tuple-element.179.refs_12_), channel_id=1, source_target_pairs={{0,2},{1,3},{2,0},{3,1},{4,6},{5,7},{6,4},{7,5},{8,10},{9,11},{10,... | collective-permute-start | bytes 1179656 | tf_op jit(solution)/shard_map/ppermute | solution.py:1202
  174.3 35.6 %collective-permute-start.21 = (bf16[1,2,1,64,768]{4,3,2,1,0:T(8,128)(2,1)S(1)}, bf16[1,2,1,64,768]{4,3,2,1,0:T(8,128)(2,1)S(1)}, u32[]{:S(2)}, u32[]{:S(2)}) collective-permute-start(bf16[1,2,1,64,768]{4,3,2,1,0:T(8,128)(2,1)S(1)} %copy-done.97), channel_id=1, source_target_pairs={{0,4},{4,0},{8,12},{12,8},{16,20},{20,16},{24,28},{28,24},{1,5},{5... | collective-permute-start | bytes 589832 | tf_op jit(solution)/shard_map/ppermute | solution.py:1202
  212.1 15.0 %collective-permute-start.26 = (bf16[2,2,1,64,768]{4,3,2,1,0:T(8,128)(2,1)S(1)}, bf16[2,2,1,64,768]{4,3,2,1,0:T(8,128)(2,1)S(1)}, u32[]{:S(2)}, u32[]{:S(2)}) collective-permute-start(bf16[2,2,1,64,768]{4,3,2,1,0:T(8,128)(2,1)S(1)} %copy-done.95), channel_id=1, source_target_pairs={{0,4},{4,0},{8,12},{12,8},{16,20},{20,16},{24,28},{28,24},{1,5},{5... | collective-permute-start | bytes 1179656 | tf_op jit(solution)/shard_map/ppermute | solution.py:1202
  224.0 20.1 %collective-permute-start.30 = (bf16[2,2,384,768]{3,2,1,0:T(8,128)(2,1)}, bf16[2,2,384,768]{3,2,1,0:T(8,128)(2,1)S(1)}, u32[]{:S(2)}, u32[]{:S(2)}) collective-permute-start(bf16[2,2,384,768]{3,2,1,0:T(8,128)(2,1)} %get-tuple-element.203.refs_2_), channel_id=1, source_target_pairs={{0,1},{1,0},{2,3},{3,2},{4,5},{5,4},{6,7},{7,6},{8,9},{9,8},{10,11... | collective-permute-start | bytes 7077896 | tf_op jit(solution)/shard_map/ppermute | solution.py:1202
  224.0 20.0 %collective-permute-start.29 = (bf16[2,2,384,1024]{3,2,1,0:T(8,128)(2,1)}, bf16[2,2,384,1024]{3,2,1,0:T(8,128)(2,1)}, u32[]{:S(2)}, u32[]{:S(2)}) collective-permute-start(bf16[2,2,384,1024]{3,2,1,0:T(8,128)(2,1)} %get-tuple-element.219), channel_id=1, source_target_pairs={{0,1},{1,0},{2,3},{3,2},{4,5},{5,4},{6,7},{7,6},{8,9},{9,8},{10,11... | collective-permute-start | bytes 9437192 | tf_op jit(solution)/shard_map/ppermute | solution.py:1202
  227.8 15.0 %collective-permute-start.27 = (bf16[2,2,2,64,384]{4,3,2,1,0:T(8,128)(2,1)S(1)}, bf16[2,2,2,64,384]{4,3,2,1,0:T(8,128)(2,1)S(1)}, u32[]{:S(2)}, u32[]{:S(2)}) collective-permute-start(bf16[2,2,2,64,384]{4,3,2,1,0:T(8,128)(2,1)S(1)} %get-tuple-element.209.refs_3_), channel_id=1, source_target_pairs={{0,2},{1,3},{2,0},{3,1},{4,6},{5,7},{6,4},{7,5},{8,10},{9,11},{10,... | collective-permute-start | bytes 1179656 | tf_op jit(solution)/shard_map/ppermute | solution.py:1202
  243.9 16.2 %collective-permute-start.28 = (bf16[2,2,4,64,192]{4,3,2,1,0:T(8,128)(2,1)S(1)}, bf16[2,2,4,64,192]{4,3,2,1,0:T(8,128)(2,1)S(1)}, u32[]{:S(2)}, u32[]{:S(2)}) collective-permute-start(bf16[2,2,4,64,192]{4,3,2,1,0:T(8,128)(2,1)S(1)} %get-tuple-element.214.refs_14_), channel_id=1, source_target_pairs={{0,1},{1,0},{2,3},{3,2},{4,5},{5,4},{6,7},{7,6},{8,9},{9,8},{10,11... | collective-permute-start | bytes 1179656 | tf_op jit(solution)/shard_map/ppermute | solution.py:1202
  258.6 53.5 %collective-permute-start.35 = (bf16[2,384,768]{2,1,0:T(8,128)(2,1)}, bf16[2,384,768]{2,1,0:T(8,128)(2,1)S(1)}, u32[]{:S(2)}, u32[]{:S(2)}) collective-permute-start(bf16[2,384,768]{2,1,0:T(8,128)(2,1)} %get-tuple-element.220.refs_7_), channel_id=1, source_target_pairs={{0,2},{1,3},{2,0},{3,1},{4,6},{5,7},{6,4},{7,5},{8,10},{9,11},{10,... | collective-permute-start | bytes 3538952 | tf_op jit(solution)/shard_map/ppermute | solution.py:1202
  265.3 17.1 %collective-permute-start.32 = (bf16[3,64,512]{2,1,0:T(8,128)(2,1)S(1)}, bf16[3,64,512]{2,1,0:T(8,128)(2,1)S(1)}, u32[]{:S(2)}, u32[]{:S(2)}) collective-permute-start(bf16[3,64,512]{2,1,0:T(8,128)(2,1)S(1)} %get-tuple-element.223), channel_id=1, source_target_pairs={{0,16},{4,20},{8,24},{12,28},{16,0},{20,4},{24,8},{28,12},{1,17},{... | collective-permute-start | bytes 589832 | tf_op jit(solution)/shard_map/ppermute | solution.py:1202
  267.4 14.9 %collective-permute-start.33 = (bf16[3,64,512]{2,1,0:T(8,128)(2,1)S(1)}, bf16[3,64,512]{2,1,0:T(8,128)(2,1)S(1)}, u32[]{:S(2)}, u32[]{:S(2)}) collective-permute-start(bf16[3,64,512]{2,1,0:T(8,128)(2,1)S(1)} %get-tuple-element.224.refs_3_), channel_id=1, source_target_pairs={{0,24},{4,28},{8,16},{12,20},{16,8},{20,12},{24,0},{28,4},{1,25},{... | collective-permute-start | bytes 589832 | tf_op jit(solution)/shard_map/ppermute | solution.py:1202
  278.2 35.6 %collective-permute-start.34 = (bf16[2,384,1024]{2,1,0:T(8,128)(2,1)S(1)}, bf16[2,384,1024]{2,1,0:T(8,128)(2,1)S(1)}, u32[]{:S(2)}, u32[]{:S(2)}) collective-permute-start(bf16[2,384,1024]{2,1,0:T(8,128)(2,1)S(1)} %copy-done.94), channel_id=1, source_target_pairs={{0,4},{4,0},{8,12},{12,8},{16,20},{20,16},{24,28},{28,24},{1,5},{5... | collective-permute-start | bytes 4718600 | tf_op jit(solution)/shard_map/ppermute | solution.py:1202
  306.4 37.8 %collective-permute-start.38 = (bf16[2,144,512]{2,1,0:T(8,128)(2,1)S(1)}, bf16[2,144,512]{2,1,0:T(8,128)(2,1)S(1)}, u32[]{:S(2)}, u32[]{:S(2)}) collective-permute-start(bf16[2,144,512]{2,1,0:T(8,128)(2,1)S(1)} %get-tuple-element.235), channel_id=1, source_target_pairs={{0,8},{4,12},{8,0},{12,4},{16,24},{20,28},{24,16},{28,20},{1,9},{5... | collective-permute-start | bytes 884744 | tf_op jit(solution)/shard_map/ppermute | solution.py:1202
  310.1 47.1 %collective-permute-start.40 = (bf16[2,144,512]{2,1,0:T(8,128)(2,1)S(1)}, bf16[2,144,512]{2,1,0:T(8,128)(2,1)S(1)}, u32[]{:S(2)}, u32[]{:S(2)}) collective-permute-start(bf16[2,144,512]{2,1,0:T(8,128)(2,1)S(1)} %get-tuple-element.229.refs_2_), channel_id=1, source_target_pairs={{0,24},{4,28},{8,16},{12,20},{16,8},{20,12},{24,0},{28,4},{1,25},{... | collective-permute-start | bytes 884744 | tf_op jit(solution)/shard_map/ppermute | solution.py:1202
  312.9 29.9 %collective-permute-start.42 = (bf16[384,768]{1,0:T(8,128)(2,1)S(1)}, bf16[384,768]{1,0:T(8,128)(2,1)S(1)}, u32[]{:S(2)}, u32[]{:S(2)}) collective-permute-start(bf16[384,768]{1,0:T(8,128)(2,1)S(1)} %get-tuple-element.230.refs_2_), channel_id=1, source_target_pairs={{0,4},{4,0},{8,12},{12,8},{16,20},{20,16},{24,28},{28,24},{1,5},{5... | collective-permute-start | bytes 1769480 | tf_op jit(solution)/shard_map/ppermute | solution.py:1202
  314.7 28.0 %collective-permute-start.41 = (bf16[384,1024]{1,0:T(8,128)(2,1)S(1)}, bf16[384,1024]{1,0:T(8,128)(2,1)S(1)}, u32[]{:S(2)}, u32[]{:S(2)}) collective-permute-start(bf16[384,1024]{1,0:T(8,128)(2,1)S(1)} %get-tuple-element.231.refs_9_), channel_id=1, source_target_pairs={{0,2},{1,3},{2,0},{3,1},{4,6},{5,7},{6,4},{7,5},{8,10},{9,11},{10,... | collective-permute-start | bytes 2359304 | tf_op jit(solution)/shard_map/ppermute | solution.py:1202
  341.9 15.3 %collective-permute-start.39 = (bf16[2,144,512]{2,1,0:T(8,128)(2,1)S(1)}, bf16[2,144,512]{2,1,0:T(8,128)(2,1)S(1)}, u32[]{:S(2)}, u32[]{:S(2)}) collective-permute-start(bf16[2,144,512]{2,1,0:T(8,128)(2,1)S(1)} %get-tuple-element.236), channel_id=1, source_target_pairs={{0,16},{4,20},{8,24},{12,28},{16,0},{20,4},{24,8},{28,12},{1,17},{... | collective-permute-start | bytes 884744 | tf_op jit(solution)/shard_map/ppermute | solution.py:1202
  381.7 20.4 %collective-permute-start.49 = (bf16[2,2,2,64,768]{4,3,2,1,0:T(8,128)(2,1)S(1)}, bf16[2,2,2,64,768]{4,3,2,1,0:T(8,128)(2,1)S(1)}, u32[]{:S(2)}, u32[]{:S(2)}) collective-permute-start(bf16[2,2,2,64,768]{4,3,2,1,0:T(8,128)(2,1)S(1)} %get-tuple-element.245.refs_12_), channel_id=1, source_target_pairs={{0,2},{1,3},{2,0},{3,1},{4,6},{5,7},{6,4},{7,5},{8,10},{9,11},{10,... | collective-permute-start | bytes 2359304 | tf_op jit(solution)/shard_map/ppermute | solution.py:1202
  383.2 38.2 %collective-permute-start.53 = (bf16[192,1792]{1,0:T(8,128)(2,1)S(1)}, bf16[192,1792]{1,0:T(8,128)(2,1)S(1)}, u32[]{:S(2)}, u32[]{:S(2)}) collective-permute-start(bf16[192,1792]{1,0:T(8,128)(2,1)S(1)} %get-tuple-element.239.refs_10_), channel_id=1, source_target_pairs={{0,16},{4,20},{8,24},{12,28},{16,0},{20,4},{24,8},{28,12},{1,17},{... | collective-permute-start | bytes 2064392 | tf_op jit(solution)/shard_map/ppermute | solution.py:1202
  384.6 18.3 %collective-permute-start.48 = (bf16[384,640]{1,0:T(8,128)(2,1)S(1)}, bf16[384,640]{1,0:T(8,128)(2,1)S(1)}, u32[]{:S(2)}, u32[]{:S(2)}) collective-permute-start(bf16[384,640]{1,0:T(8,128)(2,1)S(1)} %get-tuple-element.260), channel_id=1, source_target_pairs={{0,4},{4,0},{8,12},{12,8},{16,20},{20,16},{24,28},{28,24},{1,5},{5... | collective-permute-start | bytes 1474568 | tf_op jit(solution)/shard_map/ppermute | solution.py:1202
  386.0 25.8 %collective-permute-start.45 = (bf16[1,2,2,64,768]{4,3,2,1,0:T(8,128)(2,1)S(1)}, bf16[1,2,2,64,768]{4,3,2,1,0:T(8,128)(2,1)S(1)}, u32[]{:S(2)}, u32[]{:S(2)}) collective-permute-start(bf16[1,2,2,64,768]{4,3,2,1,0:T(8,128)(2,1)S(1)} %get-tuple-element.254.refs_2_), channel_id=1, source_target_pairs={{0,2},{1,3},{2,0},{3,1},{4,6},{5,7},{6,4},{7,5},{8,10},{9,11},{10,... | collective-permute-start | bytes 1179656 | tf_op jit(solution)/shard_map/ppermute | solution.py:1202
  387.3 23.4 %collective-permute-start.47 = (f32[8,768]{1,0:T(8,128)S(1)}, f32[8,768]{1,0:T(8,128)S(1)}, u32[]{:S(2)}, u32[]{:S(2)}) collective-permute-start(f32[8,768]{1,0:T(8,128)S(1)} %get-tuple-element.258.refs_2_), channel_id=1, source_target_pairs={{0,2},{1,3},{2,0},{3,1},{4,6},{5,7},{6,4},{7,5},{8,10},{9,11},{10,... | collective-permute-start | bytes 73736 | tf_op jit(solution)/shard_map/ppermute | solution.py:1202
  403.7 26.5 %collective-permute-start.55 = (bf16[192,640]{1,0:T(8,128)(2,1)S(1)}, bf16[192,640]{1,0:T(8,128)(2,1)S(1)}, u32[]{:S(2)}, u32[]{:S(2)}) collective-permute-start(bf16[192,640]{1,0:T(8,128)(2,1)S(1)} %get-tuple-element.263.refs_3_), channel_id=1, source_target_pairs={{0,16},{4,20},{8,24},{12,28},{16,0},{20,4},{24,8},{28,12},{1,17},{... | collective-permute-start | bytes 737288 | tf_op jit(solution)/shard_map/ppermute | solution.py:1202
  404.5 21.7 %collective-permute-start.51 = (bf16[2,2,1,64,768]{4,3,1,0,2:T(8,128)(2,1)S(1)}, bf16[2,2,1,64,768]{4,3,1,0,2:T(8,128)(2,1)S(1)}, u32[]{:S(2)}, u32[]{:S(2)}) collective-permute-start(bf16[2,2,1,64,768]{4,3,1,0,2:T(8,128)(2,1)S(1)} %bitcast.56), channel_id=1, source_target_pairs={{0,4},{4,0},{8,12},{12,8},{16,20},{20,16},{24,28},{28,24},{1,5},{5... | collective-permute-start | bytes 1179656 | tf_op jit(solution)/shard_map/ppermute | solution.py:1202
  422.4 14.9 %collective-permute-start.58 = (bf16[96,1792]{1,0:T(8,128)(2,1)S(1)}, bf16[96,1792]{1,0:T(8,128)(2,1)S(1)}, u32[]{:S(2)}, u32[]{:S(2)}) collective-permute-start(bf16[96,1792]{1,0:T(8,128)(2,1)S(1)} %get-tuple-element.272.refs_2_), channel_id=1, source_target_pairs={{0,8},{4,12},{8,0},{12,4},{16,24},{20,28},{24,16},{28,20},{1,9},{5... | collective-permute-start | bytes 1032200 | tf_op jit(solution)/shard_map/ppermute | solution.py:1202
  (127 other events, 1375.2 us)
Sparse Core Ops, SparseCore 0:
  60.7 72.9 all-gather.2

commit v2 on v1

--- a/solution.py
+++ b/solution.py
@@ -420,6 +420,11 @@
 SLOT_ORDER = (0, 2, 1, 3)
 LOG2E = math.log2(math.e)
 COST = 2.5
+NEAR_US = 6.6
+WG_US = 12
+NB_US = 0.2
+FA_US = 3
+SMALL_US = 0.5
 FIRST_COLUMNS = 1024
 BF = jnp.bfloat16
 F32 = jnp.float32
@@ -631,12 +636,19 @@
     send[...] = total[:, :, half:]
 
 
-def z_fold_kernel(place, first, second, stay, send, total, *, bit):
-    half = first.shape[0] // 2
+def z_halves(place, total, stay, send, nearest):
+    piece = total.shape[0] // (4 if nearest else 2)
+    side = place[0] % 2 if nearest else place[0] // 2
+    for lead in range(2 if nearest else 1):
+        rows = slice(lead * piece, (lead + 1) * piece)
+        for ref, here in ((stay, side), (send, 1 - side)):
+            at = pl.multiple_of((2 * lead + here) * piece, 32)
+            ref[rows] = total[pl.ds(at, piece)]
+
+
+def z_fold_kernel(place, first, second, stay, send, total, *, nearest):
     total[...] = (first[...].astype(F32) + second[...].astype(F32)).astype(BF)
-    side = place[0] // 2 if bit else place[0] % 2
-    stay[...] = total[pl.ds(pl.multiple_of(side * half, 32), half)]
-    send[...] = total[pl.ds(pl.multiple_of((1 - side) * half, 32), half)]
+    z_halves(place, total, stay, send, nearest)
 
 
 def weights_out_kernel(place, first, second, fc1, fc2, out):
@@ -656,28 +668,27 @@
             out[:, part, head * HEAD_DIM : (head + 1) * HEAD_DIM] = total[:, at : at + HEAD_DIM]
 
 
-def small_start_kernel(place, sums_a, sums_b, fc1_a, fc1_b, ln_sum, bias_sum, stay, send, last):
+def small_start_kernel(place, sums_a, sums_b, fc1_a, fc1_b, ln_sum, bias_sum, stay, send):
     width = sums_a.shape[1]
     common = [sums_a[index : index + 1] + sums_b[index : index + 1] for index in range(4)]
     common += [ln_sum[0:1], ln_sum[1:2]]
     slots = [fc1_a[slot, 0:1] + fc1_b[slot, 0:1] for slot in range(4)]
-    stay[...] = rows_of((8, width), 0, common + slots[0:2])
+    missing = width - bias_sum.shape[1]
+    last = jnp.concatenate([bias_sum[0:1], jnp.zeros((1, missing), F32)], 1)
+    stay[...] = rows_of((16, width), 0, common + slots[0:2] + [last])
     send[...] = rows_of((8, width), 0, common + slots[2:4])
-    missing = width - bias_sum.shape[1]
-    last[...] = jnp.concatenate([bias_sum[...], jnp.zeros((8, missing), F32)], 1)
+
+
+def small_first_kernel(place, first, second, out):
+    out[0:8] = first[0:8] + second[...]
+    out[8:16] = first[8:16]
 
 
 def small_middle_kernel(place, first, second, stay, send):
     total = first[...] + second[...]
-    row = lax.broadcasted_iota(jnp.int32, total.shape, 0)
-    stay[...] = jnp.where(row == 7, 0.0, total)
-    send[...] = jnp.where(row == 6, total[7:8], jnp.where(row == 7, 0.0, total))
-
-
-def small_last_kernel(place, first, second, last, out):
-    total = first[...] + second[...]
-    row = lax.broadcasted_iota(jnp.int32, total.shape, 0)
-    out[...] = jnp.where(row == 7, last[...], total)
+    row = lax.broadcasted_iota(jnp.int32, stay.shape, 0)
+    stay[...] = jnp.where(row == 7, total[8:9], total[0:8])
+    send[...] = jnp.where(row == 6, total[7:8], jnp.where(row == 7, 0.0, total[0:8]))
 
 
 def add_kernel(place, first, second, out):
@@ -927,7 +938,8 @@
 def qkv_backward_kernel(place, *refs, count, begins, ends):
     refs = list(refs)
     nears = [refs.pop(0) for _ in range(count)]
-    f0, f1, f2, f3, first, second, weight, gains = [refs.pop(0) for _ in range(8)]
+    fars = [[refs.pop(0) for _ in range(4)] for _ in range(count)]
+    first, second, weight, gains = [refs.pop(0) for _ in range(4)]
     before = [] if begins else [refs.pop(0) for _ in range(3)]
     wgrads = [refs.pop(0) for _ in range(2 if ends else 1)]
     bias_sum, ln_sum, stay, send, far = refs[:5]
@@ -944,8 +956,8 @@
     bias_row = jnp.zeros((1, gains.shape[1]), F32)
     ones = jnp.ones((8, 2 * half), BF)
     for slide, near in enumerate(nears):
-        for slot, ref in enumerate((f0, f1, f2, f3)):
-            far[place[0] ^ slot] = ref[slide]
+        for slot, ref in enumerate(fars[slide]):
+            far[place[0] ^ slot] = ref[0]
         for parity in range(2):
             pieces = []
             for head in range(4):
@@ -1144,12 +1156,9 @@
 
 def z_fold_both_kernel(place, first, second, third, fourth, stay, send, total):
     columns = first.shape[1]
-    half = first.shape[0] // 2
     total[:, :columns] = (first[...].astype(F32) + second[...].astype(F32)).astype(BF)
     total[:, columns:] = (third[...].astype(F32) + fourth[...].astype(F32)).astype(BF)
-    side = place[0] // 2
-    stay[...] = total[pl.ds(pl.multiple_of(side * half, 32), half)]
-    send[...] = total[pl.ds(pl.multiple_of((1 - side) * half, 32), half)]
+    z_halves(place, total, stay, send, True)
 
 
 def hold_kernel(place, w1, w2, wo, offset, out):
@@ -1279,7 +1288,7 @@
 
     def over_z_second(pair):
         near, away = pair
-        send = step("pair", pair_kernel, plain(near, away), [(shaped(near.shape, BF), None)], us=0.5)[0]
+        send = step("pair", pair_kernel, plain(near, away), [(shaped(near.shape, BF), None)], us=SMALL_US)[0]
         got = swap(send, "seq", 2)
         return [(near, 0), (got, 0), (away, 0), (got, 1)]
 
@@ -1416,7 +1425,7 @@
             [(f32(4, 2, ACC_ROWS, lanes), each_head(ACC_ROWS))],
             grid=(4,),
             scratch=[vm(2, lanes, AUG), vm(2, OUT_ROWS, lanes), vm(2, lanes, lanes, dtype=F32)],
-            us=6.6,
+            us=NEAR_US,
         )[0]
 
     far_outs, kept, merged = [None, None], [None, None], [None, None]
@@ -1475,6 +1484,7 @@
     spread_columns(0)
     project(0)
     near_forward(0, 0)
+    far_forward(0, True)
     spread_columns(1)
     packed = step(
         "hold",
@@ -1490,7 +1500,6 @@
     )[0]
     packed = lax.all_gather(packed, "head")
     project(1)
-    far_forward(0, True)
     near_forward(1, 0)
     far_outs[0] = over_z_second(far_outs[0])
     near_forward(1, 1)
@@ -1509,6 +1518,7 @@
     last_widen(0)
     merge(1)
     widen(1, "head", 2)
+    last_widen(1)
 
     def head_of(i, p):
         return (p[2] ^ (i % 2)) * 2 + (p[3] ^ (i // 2))
@@ -1575,7 +1585,6 @@
         given[g] = (stay, swap(send, axis, bit))
 
     feed_forward(0)
-    last_widen(1)
     feed_forward(1)
 
     tall = width // 2
@@ -1602,7 +1611,7 @@
             kept_w if partner else sent,
             grid=(2,),
             mib=56,
-            us=12,
+            us=WG_US,
         )
 
     def split_fold(pair, axis, bit):
@@ -1612,7 +1621,7 @@
         )
         return stay, swap(send, axis, bit)
 
-    grad_rows, far_grads, far_backs = [None, None], [None, None], [None, None]
+    grad_rows, far_grads, far_backs = [None, None], [None, None], [None] * group
     backs, sums_so_far = [None, None], []
 
     def rows_of_gradients(g):
@@ -1636,7 +1645,7 @@
         grad_rows[g] = outs[0]
         far_grads[0] = outs[1:] if first == 0 else over_z(outs[1:])
 
-    def near_backward(g, k):
+    def near_backward(g, k, us=9.7):
         slide = parts[g][0] + k
         near_grads[slide] = step(
             "near_backward",
@@ -1653,22 +1662,33 @@
                 vm(2, lanes, OUT_ROWS),
                 vm(2, lanes, OUT_ROWS),
             ],
-            us=9.7,
+            us=us,
         )[0]
 
-    def far_backward(g, two_steps):
-        first = parts[g][0]
+    def far_backward(g, k):
+        slide = parts[g][0] + k
+        blocks_here = []
+        for array, index in far_blocks[g]:
+            shape = array.shape[-2:]
+            if index is None:
+                spec = pl.BlockSpec((1,) + shape, lambda i, p: (k, 0, 0))
+            else:
+                spec = pl.BlockSpec((None, 1) + shape, lambda i, p, n=index: (n, k, 0, 0))
+            blocks_here.append((array, spec))
         grads_here = [
-            (array, pl.BlockSpec((1, OUT_ROWS, lanes), lambda k, p: (first + k, 0, 0)))
+            (array, pl.BlockSpec((1, OUT_ROWS, lanes), lambda i, p: (slide, 0, 0)))
             for array, _ in far_grads[0]
         ]
-        far_backs[g] = far_kernel(
+        ins = blocks_here + grads_here + plain(valid)
+        body = partial(
+            far_backward_kernel, first_slide=slide, half=half, factor=factor, scale=scale
+        )
+        outs = step(
             "far_backward",
-            far_backward_kernel,
-            g,
-            by_slide(far_blocks[g]) + grads_here + plain(valid),
-            TRIPLE,
-            [
+            paired(body, len(ins)),
+            ins,
+            [(bf(2, 1, TRIPLE, lanes), None)] * 2,
+            scratch=[
                 vm(4, lanes, AUG),
                 vm(4, OUT_ROWS, lanes),
                 vm(4, lanes, OUT_ROWS),
@@ -1680,10 +1700,9 @@
                 vm(4, OUT_ROWS, lanes, dtype=F32),
                 vm(4, TRIPLE, lanes),
             ],
-            two_steps,
-            12,
-            scale=scale,
-        )
+            us=FA_US,
+        )
+        far_backs[slide] = over_z_first(outs)
 
     def project_back(g, ends):
         first, count = parts[g]
@@ -1697,7 +1716,7 @@
             "qkv_backward",
             partial(qkv_backward_kernel, count=count, begins=begins, ends=ends),
             plain(*near_grads[first : first + count])
-            + all_slides(far_backs[g])
+            + [slot for slide in range(first, first + count) for slot in all_slides(far_backs[slide])]
             + plain(*blocks[g], weight, gains, *sums_so_far),
             wgrads + [(f32(8, 3 * local), None), (f32(8, width), None), (back, None), (back, None)],
             scratch=[vm(4, TRIPLE, lanes)] + ([vm(3 * local, width, dtype=F32)] if ends else []),
@@ -1710,7 +1729,7 @@
         first, second = backs[g]
         count, _, blocks_here, _, _ = first.shape
         shape = bf(count, 2, blocks_here // 2, half, width)
-        stay, send = step("fold", fold_kernel, plain(first, second), [(shape, None)] * 2, us=1)
+        stay, send = step("fold", fold_kernel, plain(first, second), [(shape, None)] * 2, us=SMALL_US)
         backs[g] = (stay, swap(send, axis, bit))
 
     results = []
@@ -1735,21 +1754,23 @@
             us=1 + 1.3 * count,
         )
 
-    def z_fold(pair, bit):
+    def z_fold(pair, nearest):
         first, second = pair
         shape = bf(first.shape[0] // 2, first.shape[1])
         stay, send = step(
             "z_fold",
-            partial(z_fold_kernel, bit=bit),
+            partial(z_fold_kernel, nearest=nearest),
             plain(first, second),
             [(shape, None)] * 2,
             scratch=[vm(*first.shape)],
-            us=1,
-        )
-        return stay, swap(send, "seq", 4 if bit else 2)
-
-    def small_step(name, body, pair, extra=()):
-        return step(name, body, plain(*pair, *extra), [(f32(8, width), None)], us=0.5)[0]
+            us=SMALL_US,
+        )
+        return stay, swap(send, "seq", 2 if nearest else 4)
+
+    def small_step(name, body, pair, bit=None):
+        height = 8 if bit is None else 16
+        made = step(name, body, plain(*pair), [(f32(height, width), None)], us=SMALL_US)[0]
+        return made if bit is None else (made, swap(made, "seq", bit))
 
     narrow(0, "head", 2)
     sent_w = weight_grads(2, [])
@@ -1758,17 +1779,19 @@
     rows_of_gradients(0)
     near_backward(0, 0)
     narrow(1, "head", 1)
+    rows_of_gradients(1)
     outs = weight_grads(0, [swap(value, "head", 1) for value in sent_w])
     first_w = (outs[0], swap(outs[1], "seq", 1))
     second_w = (outs[2], swap(outs[3], "head", 2))
-    rows_of_gradients(1)
-    near_backward(1, 0)
-    far_backward(1, False)
+    near_backward(1, 0, NB_US)
+    far_backward(1, 0)
+    far_backward(1, 1)
     second_w = split_fold(second_w, "seq", 1)
     first_w = split_fold(first_w, "head", 2)
-    far_backward(0, True)
-    near_backward(1, 1)
-    far_backs[0] = over_z_second(far_backs[0])
+    far_backward(0, 0)
+    far_backs[1] = over_z_second(far_backs[1])
+    far_backs[2] = over_z_second(far_backs[2])
+    near_backward(1, 1, NB_US)
     stay, send = step(
         "z_fold_both",
         z_fold_both_kernel,
@@ -1777,36 +1800,34 @@
         scratch=[vm(tall, FIRST_COLUMNS + width)],
         us=2,
     )
-    folded = (stay, swap(send, "seq", 4))
+    folded = (stay, swap(send, "seq", 2))
+    far_backs[0] = over_z_second(far_backs[0])
     project_back(1, False)
-    fold_back(1, "head", 2)
     project_back(0, True)
     stay, send, bias_sum, ln_sum = sums_so_far
     grad_in = (stay, swap(send, "seq", 1))
-    stay, send, last = step(
+    stay, send = step(
         "small_start",
         small_start_kernel,
         plain(*[owned[g][2] for g in range(2)], *[owned[g][3] for g in range(2)], ln_sum, bias_sum),
-        [(f32(8, width), None)] * 3,
-        us=0.5,
+        [(f32(16, width), None), (f32(8, width), None)],
+        us=SMALL_US,
     )
     common = (stay, swap(send, "head", 1))
+    fold_back(1, "head", 2)
     fold_back(0, "head", 2)
-    stay, send = step("small_middle", small_middle_kernel, plain(*common), [(f32(8, width), None)] * 2, us=0.5)
+    common = small_step("small_first", small_first_kernel, common, 2)
+    common = small_step("add", add_kernel, common, 4)
+    common = small_step("add", add_kernel, common, 1)
+    folded = z_fold(folded, False)
+    grad_in = z_fold(grad_in, True)
+    fold_back(1, "seq", 1)
+    fold_back(0, "seq", 1)
+    grad_in = z_fold(grad_in, False)
+    stay, send = step(
+        "small_middle", small_middle_kernel, plain(*common), [(f32(8, width), None)] * 2, us=SMALL_US
+    )
     common = (stay, swap(send, "head", 2))
-    fold_back(1, "seq", 1)
-    grad_in = z_fold(grad_in, True)
-    common = small_step("small_last", small_last_kernel, common, [last])
-    common = (common, swap(common, "seq", 1))
-    fold_back(0, "seq", 1)
-    folded = z_fold(folded, False)
-    common = small_step("add", add_kernel, common)
-    common = (common, swap(common, "seq", 4))
-    leave(1)
-    grad_in = z_fold(grad_in, False)
-    common = small_step("add", add_kernel, common)
-    common = (common, swap(common, "seq", 2))
-    leave(0)
     w_fc1_grad, w_fc2_grad, w_out_grad = step(
         "weights_out",
         weights_out_kernel,
@@ -1818,10 +1839,16 @@
         ],
         us=1.5,
     )
+    leave(1)
     w_qkv_grad = step(
-        "qkv_out", qkv_out_kernel, plain(*grad_in), [(f32(width // 8, 3, local), None)], us=1.5
+        "qkv_out",
+        qkv_out_kernel,
+        plain(*grad_in),
+        [(f32(width // 8, 3, local), None)],
+        us=1.5,
     )[0]
     common = small_step("add", add_kernel, common)
+    leave(0)
     per_head = common[7, : 3 * local].reshape(4, 3, HEAD_DIM).transpose(1, 0, 2).reshape(3, local)
     tiles_grad, output = results
     return (

time: 457 us -> 435 us (0.952)
  waiting for transfers between devices: 107 us -> 71.8 us
  starting transfers between devices: 62.8 us -> 69.1 us
  local copies, waits for them, and re-layouts: 31.6 us -> 37.2 us
    ppermute x59 -> x60, waiting for transfers between devices: 107 us -> 71.8 us  [swap(): lax.ppermute(value, axis, [(i, i ^ bit) for i in range(lax.axis_size(axis...]
    ppermute x59 -> x60, starting transfers between devices: 62.8 us -> 69.1 us  [swap(): lax.ppermute(value, axis, [(i, i ^ bit) for i in range(lax.axis_size(axis...]
    unnamed x201 -> x191, local copies, waits for them, and re-layouts: 28.3 us -> 33.9 us
    pallas_call x59 -> x62, Pallas kernels: 233 us -> 234 us  [run(): pl.pallas_call(kernel, grid_spec=pltpu.PrefetchScalarGridSpec(num_scalar_...]
  transfers between devices with their start and end apart: 60 -> 61, of which waited for: 20 -> 16; matrix products, arithmetic and copies ran while one was open for 1% -> 2% of each run, Pallas kernels for 47% -> 52%
where the time goes in v2:
time: 435 us; the launch traced here: 431 us
  Pallas kernels  234 us (54%)
  waiting for transfers between devices  71.8 us (17%)
  starting transfers between devices  69.1 us (16%)
  local copies, waits for them, and re-layouts  37.2 us (9%)
  between operations  15.7 us (4%)
    pallas_call x62, Pallas kernels, run(): pl.pallas_call(kernel, grid_spec=pltpu.PrefetchScalarGridSpec(num_scalar_...  234 us
    ppermute x60, waiting for transfers between devices, swap(): lax.ppermute(value, axis, [(i, i ^ bit) for i in range(lax.axis_size(axis...  71.8 us
    ppermute x60, starting transfers between devices, swap(): lax.ppermute(value, axis, [(i, i ^ bit) for i in range(lax.axis_size(axis...  69.1 us
    unnamed x191, local copies, waits for them, and re-layouts  33.9 us
  transfers between devices with their start and end apart: 61, of which 16 were waited for; matrix products, arithmetic and copies ran while one was open for 2% of the time, Pallas kernels for 52%

profile of v2, /device:TPU:0, one launch (start us, length us, event | category | flops | bytes accessed | tf_op | source)
XLA Modules:
  0.0 430.9 jit_solution(15106741574476117722)
XLA Ops:
  17.3 4.5 %entry.3 = (f32[2,2,128,768]{3,2,1,0:T(8,128)}, bf16[2,2,128,768]{3,2,1,0:T(8,128)(2,1)S(1)}, bf16[2,2,64,768]{3,2,1,0:T(8,128)(2,1)S(1)}, bf16[2,2,64,768]{3,2,1,0:T(8,128)(2,1)S(1)}) custom-call(s32[4]{0:T(128)S(1)} %pad_add_fusion.place_ref, bf16[6,128,768]{2,1,0:T(8,128)(2,1)S(1)} %copy-done.11, bf16[6,128,768]{2,1,0:T(8,128)(2,1)S(1)} %copy-done.11, ...), custom_call_target="tpu_custom_call" | custom-call | flops 12099999744 | bytes 39600000 | tf_op jit(solution)/shard_map/entry/pallas_call | solution.py:1191
  25.6 7.7 %collective-permute-done.2 = bf16[2,2,64,768]{3,2,1,0:T(8,128)(2,1)S(1)} collective-permute-done((bf16[2,2,64,768]{3,2,1,0:T(8,128)(2,1)S(1)}, bf16[2,2,64,768]{3,2,1,0:T(8,128)(2,1)S(1)}, u32[]{:S(2)}, u32[]{:S(2)}) %collective-permute-start.2) | collective-permute-done | bytes 393248 | tf_op jit(solution)/shard_map/ppermute | solution.py:1211
  45.5 6.6 %near_forward.3.refs_5_.refs_0_ = f32[4,2,56,512]{3,2,1,0:T(8,128)S(1)} custom-call(s32[4]{0:T(128)S(1)} %pad_add_fusion.place_ref, bf16[1,4,2,144,512]{4,3,2,1,0:T(8,128)(2,1)S(1)} %get-tuple-element.152.refs_0_, f32[6,8,512]{2,1,0:T(8,128)S(1)} %reshape.328.refs_1_.refs_4_.refs_8_, bf16[1,144,512]{2,1,0:T(8,128)(2,1)S(1)} %get-tuple-element.154.refs_2_), custom_call_target="tpu_custom_call" | custom-call | flops 18150000640 | bytes 59400000 | tf_op jit(solution)/shard_map/near_forward/pallas_call | solution.py:1191
  52.1 4.5 %collective-permute-done.5.refs_2_ = bf16[1,144,512]{2,1,0:T(8,128)(2,1)S(1)} collective-permute-done((bf16[1,144,512]{2,1,0:T(8,128)(2,1)S(1)}, bf16[1,144,512]{2,1,0:T(8,128)(2,1)S(1)}, u32[]{:S(2)}, u32[]{:S(2)}) %collective-permute-start.5) | collective-permute-done | bytes 147488 | tf_op jit(solution)/shard_map/ppermute | solution.py:1211
  56.6 7.7 %far_forward.2 = (bf16[2,1,64,512]{3,2,1,0:T(8,128)(2,1)S(1)}, bf16[2,1,64,512]{3,2,1,0:T(8,128)(2,1)S(1)}) custom-call(s32[4]{0:T(128)S(1)} %pad_add_fusion.place_ref, bf16[1,144,512]{2,1,0:T(8,128)(2,1)S(1)} %get-tuple-element.155.refs_0_, bf16[1,144,512]{2,1,0:T(8,128)(2,1)S(1)} %collective-permute-done.4.refs_1_, ...), custom_call_target="tpu_custom_call" | custom-call | flops 22000001024 | bytes 72000000 | tf_op jit(solution)/shard_map/far_forward/pallas_call | solution.py:1191
  68.4 3.8 collective-permute-start.7
  72.2 4.0 qkv.3
  82.8 6.6 %near_forward.4.refs_2_.refs_0_ = f32[4,2,56,512]{3,2,1,0:T(8,128)S(1)} custom-call(s32[4]{0:T(128)S(1)} %pad_add_fusion.place_ref, bf16[2,4,2,144,512]{4,3,2,1,0:T(8,128)(2,1)S(1)} %copy-done, f32[6,8,512]{2,1,0:T(8,128)S(1)} %reshape.328.refs_1_.refs_4_.refs_8_, bf16[2,144,512]{2,1,0:T(8,128)(2,1)S(1)} %get-tuple-element.161.refs_2_), custom_call_target="tpu_custom_call" | custom-call | flops 18150000640 | bytes 59400000 | tf_op jit(solution)/shard_map/near_forward/pallas_call | solution.py:1191
  91.6 6.6 %near_forward.5.refs_5_.refs_1_ = f32[4,2,56,512]{3,2,1,0:T(8,128)S(1)} custom-call(s32[4]{0:T(128)S(1)} %pad_add_fusion.place_ref, bf16[2,4,2,144,512]{4,3,2,1,0:T(8,128)(2,1)S(1)} %copy-done.1, f32[6,8,512]{2,1,0:T(8,128)S(1)} %reshape.328.refs_1_.refs_4_.refs_8_, bf16[2,1,64,512]{3,2,1,0:T(8,128)(2,1)S(1)} %pair.4.refs_2_), custom_call_target="tpu_custom_call" | custom-call | flops 18150000640 | bytes 59400000 | tf_op jit(solution)/shard_map/near_forward/pallas_call | solution.py:1191
  98.3 4.2 collective-permute-done.10.refs_2_.refs_4_
  103.5 15.1 %far_forward.3 = (bf16[2,64,512]{2,1,0:T(8,128)(2,1)S(1)}, bf16[2,64,512]{2,1,0:T(8,128)(2,1)S(1)}, bf16[2,64,512]{2,1,0:T(8,128)(2,1)S(1)}, bf16[2,64,512]{2,1,0:T(8,128)(2,1)S(1)}) custom-call(s32[4]{0:T(128)S(1)} %pad_add_fusion.place_ref, bf16[2,144,512]{2,1,0:T(8,128)(2,1)S(1)} %get-tuple-element.164.refs_0_, ...), custom_call_target="tpu_custom_call" | custom-call | flops 44000002048 | bytes 144000000 | tf_op jit(solution)/shard_map/far_forward/pallas_call | solution.py:1191
  125.7 5.4 %collective-permute-done.15.refs_1_ = bf16[1,2,2,64,384]{4,3,2,1,0:T(8,128)(2,1)S(1)} collective-permute-done((bf16[1,2,2,64,384]{4,3,2,1,0:T(8,128)(2,1)S(1)}, bf16[1,2,2,64,384]{4,3,2,1,0:T(8,128)(2,1)S(1)}, u32[]{:S(2)}, u32[]{:S(2)}) %collective-permute-start.15) | collective-permute-done | bytes 196640 | tf_op jit(solution)/shard_map/ppermute | solution.py:1211
  145.2 7.3 %collective-permute-done.21.refs_1_ = bf16[2,2,2,64,384]{4,3,2,1,0:T(8,128)(2,1)S(1)} collective-permute-done((bf16[2,2,2,64,384]{4,3,2,1,0:T(8,128)(2,1)S(1)}, bf16[2,2,2,64,384]{4,3,2,1,0:T(8,128)(2,1)S(1)}, u32[]{:S(2)}, u32[]{:S(2)}) %collective-permute-start.21) | collective-permute-done | bytes 393248 | tf_op jit(solution)/shard_map/ppermute | solution.py:1211
  157.0 14.4 %mlp.2 = (bf16[2,1,128,768]{3,2,1,0:T(8,128)(2,1)}, f32[2,1,128,768]{3,2,1,0:T(8,128)}, bf16[1,2,1,64,768]{4,3,2,1,0:T(8,128)(2,1)}, bf16[1,2,1,64,768]{4,3,2,1,...) custom-call(s32[4]{0:T(128)} %copy-done.4, ...), custom_call_target="tpu_custom_call" | custom-call | flops 41250000896 | bytes 135000000 | tf_op jit(solution)/shard_map/mlp/pallas_call | solution.py:1191
  172.8 24.3 %mlp.3 = (bf16[2,2,128,768]{3,2,1,0:T(8,128)(2,1)}, f32[2,2,128,768]{3,2,1,0:T(8,128)}, bf16[2,2,1,64,768]{4,3,2,1,0:T(8,128)(2,1)}, bf16[2,2,1,64,768]{4,3,2,1,...) custom-call(s32[4]{0:T(128)} %copy-done.4, ...), custom_call_target="tpu_custom_call" | custom-call | flops 68750000128 | bytes 225000000 | tf_op jit(solution)/shard_map/mlp/pallas_call | solution.py:1191
  201.9 10.4 %weight_grads.2 = (bf16[2,2,384,1024]{3,2,1,0:T(8,128)(2,1)}, bf16[2,2,384,768]{3,2,1,0:T(8,128)(2,1)}) custom-call(s32[4]{0:T(128)} %copy-done.4, bf16[768,256]{1,0:T(8,128)(2,1)} %get-tuple-element.190.refs_0_, bf16[768,256]{1,0:T(8,128)(2,1)} %get-tuple-element.191.refs_1_, bf16[768,256]{1,0:T(8,128)(2,1)} %get-tuple-element.192.refs_2_, ...), custom_call_target="tpu_custom_call" | custom-call | flops 32999999488 | bytes 108000000 | tf_op jit(solution)/shard_map/weight_grads/pallas_call | solution.py:1191
  216.7 3.4 collective-permute-done.25
  221.4 9.7 %near_backward.3.refs_2_.refs_0_ = bf16[4,2,144,512]{3,2,1,0:T(8,128)(2,1)S(1)} custom-call(s32[4]{0:T(128)S(1)} %copy-done.6, bf16[1,4,2,144,512]{4,3,2,1,0:T(8,128)(2,1)S(1)} %copy-done.56, f32[6,8,512]{2,1,0:T(8,128)S(1)} %reshape.328.refs_1_.refs_4_.refs_8_, bf16[1,4,2,64,512]{4,3,2,1,0:T(8,128)(2,1)S(1)} %get-tuple-element.209.refs_2_, ...), custom_call_target="tpu_custom_call" | custom-call | flops 26674999296 | bytes 87300000 | tf_op jit(solution)/shard_map/near_backward/pallas_call | solution.py:1191
  241.3 13.0 %weight_grads.3 = (bf16[2,384,1024]{2,1,0:T(8,128)(2,1)}, bf16[2,384,1024]{2,1,0:T(8,128)(2,1)}, bf16[2,384,768]{2,1,0:T(8,128)(2,1)}, bf16[2,384,768]{2,1,0:T(8,128)(2,1)}) custom-call(s32[4]{0:T(128)} %copy-done.4, bf16[768,256]{1,0:T(8,128)(2,1)} %get-tuple-element.190.refs_0_, bf16[768,256]{1,0:T(8,128)(2,1)} %get-tuple-element.191.refs_1_, ...), custom_call_target="tpu_custom_call" | custom-call | flops 32999999488 | bytes 108000000 | tf_op jit(solution)/shard_map/weight_grads/pallas_call | solution.py:1191
  256.7 9.6 %near_backward.4.refs_9_.refs_0_ = bf16[4,2,144,512]{3,2,1,0:T(8,128)(2,1)S(1)} custom-call(s32[4]{0:T(128)S(1)} %copy-done.7, bf16[2,4,2,144,512]{4,3,2,1,0:T(8,128)(2,1)S(1)} %copy-done.2, f32[6,8,512]{2,1,0:T(8,128)S(1)} %reshape.328.refs_1_.refs_4_.refs_8_, bf16[2,4,2,64,512]{4,3,2,1,0:T(8,128)(2,1)S(1)} %get-tuple-element.227.refs_2_, ...), custom_call_target="tpu_custom_call" | custom-call | flops 550000000 | bytes 1800000 | tf_op jit(solution)/shard_map/near_backward/pallas_call | solution.py:1191
  266.5 12.2 %far_backward.3 = (bf16[2,1,144,512]{3,2,1,0:T(8,128)(2,1)S(1)}, bf16[2,1,144,512]{3,2,1,0:T(8,128)(2,1)S(1)}) custom-call(s32[4]{0:T(128)S(1)} %copy-done.7, bf16[2,144,512]{2,1,0:T(8,128)(2,1)S(1)} %copy-done.79, bf16[2,144,512]{2,1,0:T(8,128)(2,1)S(1)} %copy-done.24, bf16[2,144,512]{2,1,0:T(8,128)(2,1)S(1)} %copy-done.26, ...), custom_call_target="tpu_custom_call" | custom-call | flops 8249999872 | bytes 27000000 | tf_op jit(solution)/shard_map/far_backward/pallas_call | solution.py:1191
  280.3 12.2 %far_backward.4 = (bf16[2,1,144,512]{3,2,1,0:T(8,128)(2,1)S(1)}, bf16[2,1,144,512]{3,2,1,0:T(8,128)(2,1)S(1)}) custom-call(s32[4]{0:T(128)S(1)} %copy-done.7, bf16[2,144,512]{2,1,0:T(8,128)(2,1)S(1)} %copy-done.79, bf16[2,144,512]{2,1,0:T(8,128)(2,1)S(1)} %copy-done.24, bf16[2,144,512]{2,1,0:T(8,128)(2,1)S(1)} %copy-done.26, ...), custom_call_target="tpu_custom_call" | custom-call | flops 8249999872 | bytes 27000000 | tf_op jit(solution)/shard_map/far_backward/pallas_call | solution.py:1191
  302.8 12.2 %far_backward.5 = (bf16[2,1,144,512]{3,2,1,0:T(8,128)(2,1)S(1)}, bf16[2,1,144,512]{3,2,1,0:T(8,128)(2,1)S(1)}) custom-call(s32[4]{0:T(128)S(1)} %copy-done.7, bf16[1,144,512]{2,1,0:T(8,128)(2,1)S(1)} %copy-done.77, bf16[1,144,512]{2,1,0:T(8,128)(2,1)S(1)} %copy-done.32, bf16[1,144,512]{2,1,0:T(8,128)(2,1)S(1)} %copy-done.34, ...), custom_call_target="tpu_custom_call" | custom-call | flops 8249999872 | bytes 27000000 | tf_op jit(solution)/shard_map/far_backward/pallas_call | solution.py:1191
  319.5 9.9 %near_backward.5.refs_4_.refs_1_ = bf16[4,2,144,512]{3,2,1,0:T(8,128)(2,1)S(1)} custom-call(s32[4]{0:T(128)S(1)} %copy-done.7, bf16[2,4,2,144,512]{4,3,2,1,0:T(8,128)(2,1)S(1)} %copy-done.2, f32[6,8,512]{2,1,0:T(8,128)S(1)} %reshape.328.refs_1_.refs_4_.refs_8_, bf16[2,4,2,64,512]{4,3,2,1,0:T(8,128)(2,1)S(1)} %get-tuple-element.227.refs_2_, ...), custom_call_target="tpu_custom_call" | custom-call | flops 550000000 | bytes 1800000 | tf_op jit(solution)/shard_map/near_backward/pallas_call | solution.py:1191
  334.5 4.4 %collective-permute-done.43.refs_7_.refs_9_ = bf16[2,1,144,512]{3,2,1,0:T(8,128)(2,1)S(1)} collective-permute-done((bf16[2,1,144,512]{3,2,1,0:T(8,128)(2,1)S(1)}, bf16[2,1,144,512]{3,2,1,0:T(8,128)(2,1)S(1)}, u32[]{:S(2)}, u32[]{:S(2)}) %collective-permute-start.43) | collective-permute-done | bytes 294944 | tf_op jit(solution)/shard_map/ppermute | solution.py:1211
  338.8 9.4 %qkv_backward.2 = (f32[576,768]{1,0:T(8,128)}, f32[8,576]{1,0:T(8,128)S(1)}, f32[8,768]{1,0:T(8,128)S(1)}, bf16[2,2,4,64,768]{4,3,2,1,0:T(8,128)(2,1)}, bf16[2,2,4,64,768]{4,3,2,1,0:T(8,128)(2,1)}) custom-call(s32[4]{0:T(128)S(1)} %copy-done.7, bf16[4,2,144,512]{3,2,1,0:T(8,128)(2,1)S(1)} %near_backward.4.refs_9_.refs_0_, ...), custom_call_target="tpu_custom_call" | custom-call | flops 27499999232 | bytes 90000000 | tf_op jit(solution)/shard_map/qkv_backward/pallas_call | solution.py:1191
  348.3 5.3 %qkv_backward.3 = (bf16[384,640]{1,0:T(8,128)(2,1)S(1)}, bf16[384,640]{1,0:T(8,128)(2,1)S(1)}, f32[8,576]{1,0:T(8,128)S(1)}, f32[8,768]{1,0:T(8,128)S(1)}, bf16[...) custom-call(s32[4]{0:T(128)S(1)} %copy-done.7, bf16[4,2,144,512]{3,2,1,0:T(8,128)(2,1)} %copy-done.42, ...), custom_call_target="tpu_custom_call" | custom-call | flops 16499999744 | bytes 54000000 | tf_op jit(solution)/shard_map/qkv_backward/pallas_call | solution.py:1191
  360.6 12.1 %collective-permute-done.51.refs_1_ = f32[16,768]{1,0:T(8,128)S(1)} collective-permute-done((f32[16,768]{1,0:T(8,128)S(1)}, f32[16,768]{1,0:T(8,128)S(1)}, u32[]{:S(2)}, u32[]{:S(2)}) %collective-permute-start.51) | collective-permute-done | bytes 49184 | tf_op jit(solution)/shard_map/ppermute | solution.py:1211
  374.3 4.2 collective-permute-done.52.refs_1_
  385.2 6.6 %collective-permute-done.57.refs_1_ = bf16[192,640]{1,0:T(8,128)(2,1)S(1)} collective-permute-done((bf16[192,640]{1,0:T(8,128)(2,1)S(1)}, bf16[192,640]{1,0:T(8,128)(2,1)S(1)}, u32[]{:S(2)}, u32[]{:S(2)}) %collective-permute-start.57) | collective-permute-done | bytes 245792 | tf_op jit(solution)/shard_map/ppermute | solution.py:1211
  401.4 4.6 %collective-permute-done.54 = bf16[2,2,1,64,768]{4,3,1,0,2:T(8,128)(2,1)S(1)} collective-permute-done((bf16[2,2,1,64,768]{4,3,1,0,2:T(8,128)(2,1)S(1)}, bf16[2,2,1,64,768]{4,3,1,0,2:T(8,128)(2,1)S(1)}, u32[]{:S(2)}, u32[]{:S(2)}) %collective-permute-start.54) | collective-permute-done | bytes 393248 | tf_op jit(solution)/shard_map/ppermute | solution.py:1211
  410.9 3.7 leave.2
  (381 shorter events, 149.8 us)
Async XLA Ops:
  7.2 149.2 %all-gather.3.cloned.1.call-start = ((), (), s32[]{:S(2)}) async-start(), calls=%async_computation | async-start | bytes 13393920 | tf_op jit(solution)/shard_map/all_gather | solution.py:1501
  37.5 26.8 %collective-permute-start.8 = (bf16[2,2,2,64,768]{4,3,2,1,0:T(8,128)(2,1)}, bf16[2,2,2,64,768]{4,3,2,1,0:T(8,128)(2,1)S(1)}, u32[]{:S(2)}, u32[]{:S(2)}) collective-permute-start(bf16[2,2,2,64,768]{4,3,2,1,0:T(8,128)(2,1)} %copy-done.19), channel_id=1, source_target_pairs={{0,2},{1,3},{2,0},{3,1},{4,6},{5,7},{6,4},{7,5},{8,10},{9,11},{10,... | collective-permute-start | bytes 2359304 | tf_op jit(solution)/shard_map/ppermute | solution.py:1211
  68.4 21.1 %collective-permute-start.7 = (bf16[2,1,64,512]{3,2,1,0:T(8,128)(2,1)S(1)}, bf16[2,1,64,512]{3,2,1,0:T(8,128)(2,1)S(1)}, u32[]{:S(2)}, u32[]{:S(2)}) collective-permute-start(bf16[2,1,64,512]{3,2,1,0:T(8,128)(2,1)S(1)} %get-tuple-element.159.refs_2_), channel_id=1, source_target_pairs={{0,16},{4,20},{8,24},{12,28},{16,0},{20,4},{24,8},{28,12},{1,17},{... | collective-permute-start | bytes 393224 | tf_op jit(solution)/shard_map/ppermute | solution.py:1211
  76.2 27.3 %collective-permute-start.12 = (bf16[2,144,512]{2,1,0:T(8,128)(2,1)S(1)}, bf16[2,144,512]{2,1,0:T(8,128)(2,1)S(1)}, u32[]{:S(2)}, u32[]{:S(2)}) collective-permute-start(bf16[2,144,512]{2,1,0:T(8,128)(2,1)S(1)} %get-tuple-element.165), channel_id=1, source_target_pairs={{0,8},{4,12},{8,0},{12,4},{16,24},{20,28},{24,16},{28,20},{1,9},{5... | collective-permute-start | bytes 884744 | tf_op jit(solution)/shard_map/ppermute | solution.py:1211
  78.5 25.0 %collective-permute-start.13 = (bf16[2,144,512]{2,1,0:T(8,128)(2,1)S(1)}, bf16[2,144,512]{2,1,0:T(8,128)(2,1)S(1)}, u32[]{:S(2)}, u32[]{:S(2)}) collective-permute-start(bf16[2,144,512]{2,1,0:T(8,128)(2,1)S(1)} %get-tuple-element.166), channel_id=1, source_target_pairs={{0,16},{4,20},{8,24},{12,28},{16,0},{20,4},{24,8},{28,12},{1,17},{... | collective-permute-start | bytes 884744 | tf_op jit(solution)/shard_map/ppermute | solution.py:1211
  79.5 23.9 %collective-permute-start.14 = (bf16[2,144,512]{2,1,0:T(8,128)(2,1)S(1)}, bf16[2,144,512]{2,1,0:T(8,128)(2,1)S(1)}, u32[]{:S(2)}, u32[]{:S(2)}) collective-permute-start(bf16[2,144,512]{2,1,0:T(8,128)(2,1)S(1)} %get-tuple-element.161.refs_2_), channel_id=1, source_target_pairs={{0,24},{4,28},{8,16},{12,20},{16,8},{20,12},{24,0},{28,4},{1,25},{... | collective-permute-start | bytes 884744 | tf_op jit(solution)/shard_map/ppermute | solution.py:1211
  119.5 16.1 %collective-permute-start.19 = (bf16[2,64,512]{2,1,0:T(8,128)(2,1)S(1)}, bf16[2,64,512]{2,1,0:T(8,128)(2,1)S(1)}, u32[]{:S(2)}, u32[]{:S(2)}) collective-permute-start(bf16[2,64,512]{2,1,0:T(8,128)(2,1)S(1)} %get-tuple-element.167.refs_2_), channel_id=1, source_target_pairs={{0,24},{4,28},{8,16},{12,20},{16,8},{20,12},{24,0},{28,4},{1,25},{... | collective-permute-start | bytes 393224 | tf_op jit(solution)/shard_map/ppermute | solution.py:1211
  154.8 17.2 %collective-permute-start.23 = (bf16[2,2,1,64,768]{4,3,1,0,2:T(8,128)(2,1)S(1)}, bf16[2,2,1,64,768]{4,3,1,0,2:T(8,128)(2,1)S(1)}, u32[]{:S(2)}, u32[]{:S(2)}) collective-permute-start(bf16[2,2,1,64,768]{4,3,1,0,2:T(8,128)(2,1)S(1)} %bitcast.58), channel_id=1, source_target_pairs={{0,4},{4,0},{8,12},{12,8},{16,20},{20,16},{24,28},{28,24},{1,5},{5... | collective-permute-start | bytes 1179656 | tf_op jit(solution)/shard_map/ppermute | solution.py:1211
  171.4 27.2 %collective-permute-start.22 = (bf16[1,2,1,64,768]{4,3,2,1,0:T(8,128)(2,1)}, bf16[1,2,1,64,768]{4,3,2,1,0:T(8,128)(2,1)S(1)}, u32[]{:S(2)}, u32[]{:S(2)}) collective-permute-start(bf16[1,2,1,64,768]{4,3,2,1,0:T(8,128)(2,1)} %get-tuple-element.182), channel_id=1, source_target_pairs={{0,4},{4,0},{8,12},{12,8},{16,20},{20,16},{24,28},{28,24},{1,5},{5... | collective-permute-start | bytes 589832 | tf_op jit(solution)/shard_map/ppermute | solution.py:1211
  197.1 18.2 %collective-permute-start.26 = (bf16[2,2,1,64,768]{4,3,2,1,0:T(8,128)(2,1)}, bf16[2,2,1,64,768]{4,3,2,1,0:T(8,128)(2,1)S(1)}, u32[]{:S(2)}, u32[]{:S(2)}) collective-permute-start(bf16[2,2,1,64,768]{4,3,2,1,0:T(8,128)(2,1)} %get-tuple-element.207), channel_id=1, source_target_pairs={{0,4},{4,0},{8,12},{12,8},{16,20},{20,16},{24,28},{28,24},{1,5},{5... | collective-permute-start | bytes 1179656 | tf_op jit(solution)/shard_map/ppermute | solution.py:1211
  212.2 27.6 %collective-permute-start.33 = (bf16[2,2,384,768]{3,2,1,0:T(8,128)(2,1)}, bf16[2,2,384,768]{3,2,1,0:T(8,128)(2,1)S(1)}, u32[]{:S(2)}, u32[]{:S(2)}) collective-permute-start(bf16[2,2,384,768]{3,2,1,0:T(8,128)(2,1)} %get-tuple-element.202.refs_2_), channel_id=1, source_target_pairs={{0,1},{1,0},{2,3},{3,2},{4,5},{5,4},{6,7},{7,6},{8,9},{9,8},{10,11... | collective-permute-start | bytes 7077896 | tf_op jit(solution)/shard_map/ppermute | solution.py:1211
  212.3 29.0 %collective-permute-start.32 = (bf16[2,2,384,1024]{3,2,1,0:T(8,128)(2,1)}, bf16[2,2,384,1024]{3,2,1,0:T(8,128)(2,1)}, u32[]{:S(2)}, u32[]{:S(2)}) collective-permute-start(bf16[2,2,384,1024]{3,2,1,0:T(8,128)(2,1)} %get-tuple-element.222), channel_id=1, source_target_pairs={{0,1},{1,0},{2,3},{3,2},{4,5},{5,4},{6,7},{7,6},{8,9},{9,8},{10,11... | collective-permute-start | bytes 9437192 | tf_op jit(solution)/shard_map/ppermute | solution.py:1211
  235.4 31.0 %collective-permute-start.29 = (bf16[3,64,512]{2,1,0:T(8,128)(2,1)S(1)}, bf16[3,64,512]{2,1,0:T(8,128)(2,1)S(1)}, u32[]{:S(2)}, u32[]{:S(2)}) collective-permute-start(bf16[3,64,512]{2,1,0:T(8,128)(2,1)S(1)} %get-tuple-element.219), channel_id=1, source_target_pairs={{0,8},{4,12},{8,0},{12,4},{16,24},{20,28},{24,16},{28,20},{1,9},{5... | collective-permute-start | bytes 589832 | tf_op jit(solution)/shard_map/ppermute | solution.py:1211
  235.5 30.9 %collective-permute-start.30 = (bf16[3,64,512]{2,1,0:T(8,128)(2,1)S(1)}, bf16[3,64,512]{2,1,0:T(8,128)(2,1)S(1)}, u32[]{:S(2)}, u32[]{:S(2)}) collective-permute-start(bf16[3,64,512]{2,1,0:T(8,128)(2,1)S(1)} %get-tuple-element.220), channel_id=1, source_target_pairs={{0,16},{4,20},{8,24},{12,28},{16,0},{20,4},{24,8},{28,12},{1,17},{... | collective-permute-start | bytes 589832 | tf_op jit(solution)/shard_map/ppermute | solution.py:1211
  238.7 27.7 %collective-permute-start.31 = (bf16[3,64,512]{2,1,0:T(8,128)(2,1)S(1)}, bf16[3,64,512]{2,1,0:T(8,128)(2,1)S(1)}, u32[]{:S(2)}, u32[]{:S(2)}) collective-permute-start(bf16[3,64,512]{2,1,0:T(8,128)(2,1)S(1)} %get-tuple-element.221.refs_14_), channel_id=1, source_target_pairs={{0,24},{4,28},{8,16},{12,20},{16,8},{20,12},{24,0},{28,4},{1,25},{... | collective-permute-start | bytes 589832 | tf_op jit(solution)/shard_map/ppermute | solution.py:1211
  254.3 40.6 %collective-permute-start.35 = (bf16[2,384,768]{2,1,0:T(8,128)(2,1)}, bf16[2,384,768]{2,1,0:T(8,128)(2,1)S(1)}, u32[]{:S(2)}, u32[]{:S(2)}) collective-permute-start(bf16[2,384,768]{2,1,0:T(8,128)(2,1)} %get-tuple-element.226.refs_3_), channel_id=1, source_target_pairs={{0,2},{1,3},{2,0},{3,1},{4,6},{5,7},{6,4},{7,5},{8,10},{9,11},{10,... | collective-permute-start | bytes 3538952 | tf_op jit(solution)/shard_map/ppermute | solution.py:1211
  254.9 43.1 %collective-permute-start.34 = (bf16[2,384,1024]{2,1,0:T(8,128)(2,1)}, bf16[2,384,1024]{2,1,0:T(8,128)(2,1)S(1)}, u32[]{:S(2)}, u32[]{:S(2)}) collective-permute-start(bf16[2,384,1024]{2,1,0:T(8,128)(2,1)} %get-tuple-element.224), channel_id=1, source_target_pairs={{0,4},{4,0},{8,12},{12,8},{16,20},{20,16},{24,28},{28,24},{1,5},{5... | collective-permute-start | bytes 4718600 | tf_op jit(solution)/shard_map/ppermute | solution.py:1211
  278.7 36.7 %collective-permute-start.40 = (bf16[2,1,144,512]{3,2,1,0:T(8,128)(2,1)S(1)}, bf16[2,1,144,512]{3,2,1,0:T(8,128)(2,1)S(1)}, u32[]{:S(2)}, u32[]{:S(2)}) collective-permute-start(bf16[2,1,144,512]{3,2,1,0:T(8,128)(2,1)S(1)} %get-tuple-element.228.refs_9_), channel_id=1, source_target_pairs={{0,16},{4,20},{8,24},{12,28},{16,0},{20,4},{24,8},{28,12},{1,17},{... | collective-permute-start | bytes 884744 | tf_op jit(solution)/shard_map/ppermute | solution.py:1211
  292.5 26.4 %collective-permute-start.39 = (bf16[2,1,144,512]{3,2,1,0:T(8,128)(2,1)S(1)}, bf16[2,1,144,512]{3,2,1,0:T(8,128)(2,1)S(1)}, u32[]{:S(2)}, u32[]{:S(2)}) collective-permute-start(bf16[2,1,144,512]{3,2,1,0:T(8,128)(2,1)S(1)} %get-tuple-element.229.refs_2_), channel_id=1, source_target_pairs={{0,16},{4,20},{8,24},{12,28},{16,0},{20,4},{24,8},{28,12},{1,17},{... | collective-permute-start | bytes 884744 | tf_op jit(solution)/shard_map/ppermute | solution.py:1211
  296.5 32.8 %collective-permute-start.38 = (bf16[384,768]{1,0:T(8,128)(2,1)S(1)}, bf16[384,768]{1,0:T(8,128)(2,1)S(1)}, u32[]{:S(2)}, u32[]{:S(2)}) collective-permute-start(bf16[384,768]{1,0:T(8,128)(2,1)S(1)} %get-tuple-element.230.refs_2_), channel_id=1, source_target_pairs={{0,4},{4,0},{8,12},{12,8},{16,20},{20,16},{24,28},{28,24},{1,5},{5... | collective-permute-start | bytes 1769480 | tf_op jit(solution)/shard_map/ppermute | solution.py:1211
  301.3 28.1 %collective-permute-start.37 = (bf16[384,1024]{1,0:T(8,128)(2,1)S(1)}, bf16[384,1024]{1,0:T(8,128)(2,1)S(1)}, u32[]{:S(2)}, u32[]{:S(2)}) collective-permute-start(bf16[384,1024]{1,0:T(8,128)(2,1)S(1)} %get-tuple-element.231.refs_9_), channel_id=1, source_target_pairs={{0,2},{1,3},{2,0},{3,1},{4,6},{5,7},{6,4},{7,5},{8,10},{9,11},{10,... | collective-permute-start | bytes 2359304 | tf_op jit(solution)/shard_map/ppermute | solution.py:1211
  315.0 16.9 %collective-permute-start.36 = (bf16[2,1,144,512]{3,2,1,0:T(8,128)(2,1)S(1)}, bf16[2,1,144,512]{3,2,1,0:T(8,128)(2,1)S(1)}, u32[]{:S(2)}, u32[]{:S(2)}) collective-permute-start(bf16[2,1,144,512]{3,2,1,0:T(8,128)(2,1)S(1)} %get-tuple-element.233.refs_2_), channel_id=1, source_target_pairs={{0,16},{4,20},{8,24},{12,28},{16,0},{20,4},{24,8},{28,12},{1,17},{... | collective-permute-start | bytes 884744 | tf_op jit(solution)/shard_map/ppermute | solution.py:1211
  315.9 22.9 %collective-permute-start.42 = (bf16[2,1,144,512]{3,2,1,0:T(8,128)(2,1)S(1)}, bf16[2,1,144,512]{3,2,1,0:T(8,128)(2,1)S(1)}, u32[]{:S(2)}, u32[]{:S(2)}) collective-permute-start(bf16[2,1,144,512]{3,2,1,0:T(8,128)(2,1)S(1)} %pair.5.refs_2_), channel_id=1, source_target_pairs={{0,8},{4,12},{8,0},{12,4},{16,24},{20,28},{24,16},{28,20},{1,9},{5... | collective-permute-start | bytes 884744 | tf_op jit(solution)/shard_map/ppermute | solution.py:1211
  319.4 19.4 %collective-permute-start.43 = (bf16[2,1,144,512]{3,2,1,0:T(8,128)(2,1)S(1)}, bf16[2,1,144,512]{3,2,1,0:T(8,128)(2,1)S(1)}, u32[]{:S(2)}, u32[]{:S(2)}) collective-permute-start(bf16[2,1,144,512]{3,2,1,0:T(8,128)(2,1)S(1)} %pair.6.refs_3_), channel_id=1, source_target_pairs={{0,8},{4,12},{8,0},{12,4},{16,24},{20,28},{24,16},{28,20},{1,9},{5... | collective-permute-start | bytes 884744 | tf_op jit(solution)/shard_map/ppermute | solution.py:1211
  354.2 25.5 %collective-permute-start.49 = (bf16[192,1792]{1,0:T(8,128)(2,1)S(1)}, bf16[192,1792]{1,0:T(8,128)(2,1)S(1)}, u32[]{:S(2)}, u32[]{:S(2)}) collective-permute-start(bf16[192,1792]{1,0:T(8,128)(2,1)S(1)} %get-tuple-element.238.refs_2_), channel_id=1, source_target_pairs={{0,8},{4,12},{8,0},{12,4},{16,24},{20,28},{24,16},{28,20},{1,9},{5... | collective-permute-start | bytes 2064392 | tf_op jit(solution)/shard_map/ppermute | solution.py:1211
  355.0 25.8 %collective-permute-start.48 = (bf16[384,640]{1,0:T(8,128)(2,1)S(1)}, bf16[384,640]{1,0:T(8,128)(2,1)S(1)}, u32[]{:S(2)}, u32[]{:S(2)}) collective-permute-start(bf16[384,640]{1,0:T(8,128)(2,1)S(1)} %get-tuple-element.256), channel_id=1, source_target_pairs={{0,4},{4,0},{8,12},{12,8},{16,20},{20,16},{24,28},{28,24},{1,5},{5... | collective-permute-start | bytes 1474568 | tf_op jit(solution)/shard_map/ppermute | solution.py:1211
  356.5 27.1 %collective-permute-start.47 = (bf16[2,2,2,64,768]{4,3,2,1,0:T(8,128)(2,1)S(1)}, bf16[2,2,2,64,768]{4,3,2,1,0:T(8,128)(2,1)S(1)}, u32[]{:S(2)}, u32[]{:S(2)}) collective-permute-start(bf16[2,2,2,64,768]{4,3,2,1,0:T(8,128)(2,1)S(1)} %get-tuple-element.251.refs_2_), channel_id=1, source_target_pairs={{0,2},{1,3},{2,0},{3,1},{4,6},{5,7},{6,4},{7,5},{8,10},{9,11},{10,... | collective-permute-start | bytes 2359304 | tf_op jit(solution)/shard_map/ppermute | solution.py:1211
  379.1 18.3 %collective-permute-start.56 = (f32[16,768]{1,0:T(8,128)S(1)}, f32[16,768]{1,0:T(8,128)S(1)}, u32[]{:S(2)}, u32[]{:S(2)}) collective-permute-start(f32[16,768]{1,0:T(8,128)S(1)} %add.141.refs_2_.refs_0_), channel_id=1, source_target_pairs={{0,4},{4,0},{8,12},{12,8},{16,20},{20,16},{24,28},{28,24},{1,5},{5... | collective-permute-start | bytes 147464 | tf_op jit(solution)/shard_map/ppermute | solution.py:1211
  380.6 18.5 %collective-permute-start.55 = (bf16[96,1792]{1,0:T(8,128)(2,1)S(1)}, bf16[96,1792]{1,0:T(8,128)(2,1)S(1)}, u32[]{:S(2)}, u32[]{:S(2)}) collective-permute-start(bf16[96,1792]{1,0:T(8,128)(2,1)S(1)} %get-tuple-element.259.refs_2_), channel_id=1, source_target_pairs={{0,16},{4,20},{8,24},{12,28},{16,0},{20,4},{24,8},{28,12},{1,17},{... | collective-permute-start | bytes 1032200 | tf_op jit(solution)/shard_map/ppermute | solution.py:1211
  392.5 22.1 %collective-permute-start.59 = (bf16[96,640]{1,0:T(8,128)(2,1)S(1)}, bf16[96,640]{1,0:T(8,128)(2,1)S(1)}, u32[]{:S(2)}, u32[]{:S(2)}) collective-permute-start(bf16[96,640]{1,0:T(8,128)(2,1)S(1)} %get-tuple-element.271.refs_2_), channel_id=1, source_target_pairs={{0,16},{4,20},{8,24},{12,28},{16,0},{20,4},{24,8},{28,12},{1,17},{... | collective-permute-start | bytes 368648 | tf_op jit(solution)/shard_map/ppermute | solution.py:1211
  397.9 20.2 %collective-permute-start.58 = (f32[8,768]{1,0:T(8,128)S(1)}, f32[8,768]{1,0:T(8,128)S(1)}, u32[]{:S(2)}, u32[]{:S(2)}) collective-permute-start(f32[8,768]{1,0:T(8,128)S(1)} %get-tuple-element.272.refs_2_), channel_id=1, source_target_pairs={{0,2},{1,3},{2,0},{3,1},{4,6},{5,7},{6,4},{7,5},{8,10},{9,11},{10,... | collective-permute-start | bytes 73736 | tf_op jit(solution)/shard_map/ppermute | solution.py:1211
  398.6 21.6 %collective-permute-start.53 = (bf16[1,2,1,64,768]{4,3,1,2,0:T(8,128)(2,1)S(1)}, bf16[1,2,1,64,768]{4,3,1,2,0:T(8,128)(2,1)S(1)}, u32[]{:S(2)}, u32[]{:S(2)}) collective-permute-start(bf16[1,2,1,64,768]{4,3,1,2,0:T(8,128)(2,1)S(1)} %bitcast.61), channel_id=1, source_target_pairs={{0,4},{4,0},{8,12},{12,8},{16,20},{20,16},{24,28},{28,24},{1,5},{5... | collective-permute-start | bytes 589832 | tf_op jit(solution)/shard_map/ppermute | solution.py:1211
  (123 other events, 949.4 us)
Sparse Core Ops, SparseCore 0:
  68.4 76.1 all-gather.2

commit v3 on v2

--- a/solution.py
+++ b/solution.py
@@ -424,6 +424,7 @@
 WG_US = 12
 NB_US = 0.2
 FA_US = 3
+QB_US = 4
 SMALL_US = 0.5
 FIRST_COLUMNS = 1024
 BF = jnp.bfloat16
@@ -1518,7 +1519,6 @@
     last_widen(0)
     merge(1)
     widen(1, "head", 2)
-    last_widen(1)
 
     def head_of(i, p):
         return (p[2] ^ (i % 2)) * 2 + (p[3] ^ (i // 2))
@@ -1585,6 +1585,7 @@
         given[g] = (stay, swap(send, axis, bit))
 
     feed_forward(0)
+    last_widen(1)
     feed_forward(1)
 
     tall = width // 2
@@ -1720,7 +1721,7 @@
             + plain(*blocks[g], weight, gains, *sums_so_far),
             wgrads + [(f32(8, 3 * local), None), (f32(8, width), None), (back, None), (back, None)],
             scratch=[vm(4, TRIPLE, lanes)] + ([vm(3 * local, width, dtype=F32)] if ends else []),
-            us=2 + 4 * count,
+            us=QB_US * count,
         )
         sums_so_far[:] = outs[:-2]
         backs[g] = (outs[-2], swap(outs[-1], "head", 1))
@@ -1803,6 +1804,7 @@
     folded = (stay, swap(send, "seq", 2))
     far_backs[0] = over_z_second(far_backs[0])
     project_back(1, False)
+    fold_back(1, "head", 2)
     project_back(0, True)
     stay, send, bias_sum, ln_sum = sums_so_far
     grad_in = (stay, swap(send, "seq", 1))
@@ -1814,20 +1816,21 @@
         us=SMALL_US,
     )
     common = (stay, swap(send, "head", 1))
-    fold_back(1, "head", 2)
     fold_back(0, "head", 2)
     common = small_step("small_first", small_first_kernel, common, 2)
+    fold_back(1, "seq", 1)
     common = small_step("add", add_kernel, common, 4)
+    fold_back(0, "seq", 1)
+    grad_in = z_fold(grad_in, True)
     common = small_step("add", add_kernel, common, 1)
     folded = z_fold(folded, False)
-    grad_in = z_fold(grad_in, True)
-    fold_back(1, "seq", 1)
-    fold_back(0, "seq", 1)
+    leave(1)
     grad_in = z_fold(grad_in, False)
     stay, send = step(
         "small_middle", small_middle_kernel, plain(*common), [(f32(8, width), None)] * 2, us=SMALL_US
     )
     common = (stay, swap(send, "head", 2))
+    leave(0)
     w_fc1_grad, w_fc2_grad, w_out_grad = step(
         "weights_out",
         weights_out_kernel,
@@ -1839,7 +1842,6 @@
         ],
         us=1.5,
     )
-    leave(1)
     w_qkv_grad = step(
         "qkv_out",
         qkv_out_kernel,
@@ -1848,7 +1850,6 @@
         us=1.5,
     )[0]
     common = small_step("add", add_kernel, common)
-    leave(0)
     per_head = common[7, : 3 * local].reshape(4, 3, HEAD_DIM).transpose(1, 0, 2).reshape(3, local)
     tiles_grad, output = results
     return (

time: 435 us -> 438 us (level)
  waiting for transfers between devices: 71.8 us -> 83.8 us
  starting transfers between devices: 69.1 us -> 64.1 us
    ppermute x60, waiting for transfers between devices: 71.8 us -> 83.8 us  [swap(): lax.ppermute(value, axis, [(i, i ^ bit) for i in range(lax.axis_size(axis...]
    ppermute x60, starting transfers between devices: 69.1 us -> 64 us  [swap(): lax.ppermute(value, axis, [(i, i ^ bit) for i in range(lax.axis_size(axis...]
    unnamed x191 -> x199, local copies, waits for them, and re-layouts: 33.9 us -> 29.6 us
  transfers between devices with their start and end apart: 61 -> 61, of which waited for: 16 -> 18; matrix products, arithmetic and copies ran while one was open for 2% -> 1% of each run, Pallas kernels for 52% -> 49%
where the time goes in v3:
time: 438 us; the launch traced here: 434 us
  Pallas kernels  235 us (54%)
  waiting for transfers between devices  83.8 us (19%)
  starting transfers between devices  64.1 us (15%)
  local copies, waits for them, and re-layouts  32.9 us (8%)
  between operations  15.8 us (4%)
    pallas_call x62, Pallas kernels, run(): pl.pallas_call(kernel, grid_spec=pltpu.PrefetchScalarGridSpec(num_scalar_...  235 us
    ppermute x60, waiting for transfers between devices, swap(): lax.ppermute(value, axis, [(i, i ^ bit) for i in range(lax.axis_size(axis...  83.8 us
    ppermute x60, starting transfers between devices, swap(): lax.ppermute(value, axis, [(i, i ^ bit) for i in range(lax.axis_size(axis...  64 us
    unnamed x199, local copies, waits for them, and re-layouts  29.6 us
  transfers between devices with their start and end apart: 61, of which 18 were waited for; matrix products, arithmetic and copies ran while one was open for 1% of the time, Pallas kernels for 49%

profile of v3, /device:TPU:0, one launch (start us, length us, event | category | flops | bytes accessed | tf_op | source)
XLA Modules:
  0.0 434.2 jit_solution(17695893143474492172)
XLA Ops:
  17.3 4.5 %entry.3 = (f32[2,2,128,768]{3,2,1,0:T(8,128)}, bf16[2,2,128,768]{3,2,1,0:T(8,128)(2,1)S(1)}, bf16[2,2,64,768]{3,2,1,0:T(8,128)(2,1)S(1)}, bf16[2,2,64,768]{3,2,1,0:T(8,128)(2,1)S(1)}) custom-call(s32[4]{0:T(128)S(1)} %pad_add_fusion.place_ref, bf16[6,128,768]{2,1,0:T(8,128)(2,1)S(1)} %copy-done.13, bf16[6,128,768]{2,1,0:T(8,128)(2,1)S(1)} %copy-done.13, ...), custom_call_target="tpu_custom_call" | custom-call | flops 12099999744 | bytes 39600000 | tf_op jit(solution)/shard_map/entry/pallas_call | solution.py:1192
  25.5 7.7 %collective-permute-done.2 = bf16[2,2,64,768]{3,2,1,0:T(8,128)(2,1)S(1)} collective-permute-done((bf16[2,2,64,768]{3,2,1,0:T(8,128)(2,1)S(1)}, bf16[2,2,64,768]{3,2,1,0:T(8,128)(2,1)S(1)}, u32[]{:S(2)}, u32[]{:S(2)}) %collective-permute-start.2) | collective-permute-done | bytes 393248 | tf_op jit(solution)/shard_map/ppermute | solution.py:1212
  45.4 6.6 %near_forward.3.refs_5_.refs_0_ = f32[4,2,56,512]{3,2,1,0:T(8,128)S(1)} custom-call(s32[4]{0:T(128)S(1)} %pad_add_fusion.place_ref, bf16[1,4,2,144,512]{4,3,2,1,0:T(8,128)(2,1)S(1)} %get-tuple-element.152.refs_0_, f32[6,8,512]{2,1,0:T(8,128)S(1)} %reshape.328.refs_1_.refs_4_.refs_8_, bf16[1,144,512]{2,1,0:T(8,128)(2,1)S(1)} %get-tuple-element.154.refs_2_), custom_call_target="tpu_custom_call" | custom-call | flops 18150000640 | bytes 59400000 | tf_op jit(solution)/shard_map/near_forward/pallas_call | solution.py:1192
  52.1 4.4 %collective-permute-done.5.refs_2_ = bf16[1,144,512]{2,1,0:T(8,128)(2,1)S(1)} collective-permute-done((bf16[1,144,512]{2,1,0:T(8,128)(2,1)S(1)}, bf16[1,144,512]{2,1,0:T(8,128)(2,1)S(1)}, u32[]{:S(2)}, u32[]{:S(2)}) %collective-permute-start.5) | collective-permute-done | bytes 147488 | tf_op jit(solution)/shard_map/ppermute | solution.py:1212
  56.6 7.7 %far_forward.2 = (bf16[2,1,64,512]{3,2,1,0:T(8,128)(2,1)S(1)}, bf16[2,1,64,512]{3,2,1,0:T(8,128)(2,1)S(1)}) custom-call(s32[4]{0:T(128)S(1)} %pad_add_fusion.place_ref, bf16[1,144,512]{2,1,0:T(8,128)(2,1)S(1)} %get-tuple-element.155.refs_0_, bf16[1,144,512]{2,1,0:T(8,128)(2,1)S(1)} %collective-permute-done.4.refs_1_, ...), custom_call_target="tpu_custom_call" | custom-call | flops 22000001024 | bytes 72000000 | tf_op jit(solution)/shard_map/far_forward/pallas_call | solution.py:1192
  68.3 3.8 collective-permute-start.7
  72.1 4.0 qkv.3
  82.8 6.6 %near_forward.4.refs_2_.refs_0_ = f32[4,2,56,512]{3,2,1,0:T(8,128)S(1)} custom-call(s32[4]{0:T(128)S(1)} %pad_add_fusion.place_ref, bf16[2,4,2,144,512]{4,3,2,1,0:T(8,128)(2,1)S(1)} %copy-done, f32[6,8,512]{2,1,0:T(8,128)S(1)} %reshape.328.refs_1_.refs_4_.refs_8_, bf16[2,144,512]{2,1,0:T(8,128)(2,1)S(1)} %get-tuple-element.161.refs_2_), custom_call_target="tpu_custom_call" | custom-call | flops 18150000640 | bytes 59400000 | tf_op jit(solution)/shard_map/near_forward/pallas_call | solution.py:1192
  91.6 6.6 %near_forward.5.refs_5_.refs_1_ = f32[4,2,56,512]{3,2,1,0:T(8,128)S(1)} custom-call(s32[4]{0:T(128)S(1)} %pad_add_fusion.place_ref, bf16[2,4,2,144,512]{4,3,2,1,0:T(8,128)(2,1)S(1)} %copy-done.1, f32[6,8,512]{2,1,0:T(8,128)S(1)} %reshape.328.refs_1_.refs_4_.refs_8_, bf16[2,1,64,512]{3,2,1,0:T(8,128)(2,1)S(1)} %pair.4.refs_2_), custom_call_target="tpu_custom_call" | custom-call | flops 18150000640 | bytes 59400000 | tf_op jit(solution)/shard_map/near_forward/pallas_call | solution.py:1192
  98.2 4.3 collective-permute-done.10.refs_2_.refs_4_
  103.4 15.1 %far_forward.3 = (bf16[2,64,512]{2,1,0:T(8,128)(2,1)S(1)}, bf16[2,64,512]{2,1,0:T(8,128)(2,1)S(1)}, bf16[2,64,512]{2,1,0:T(8,128)(2,1)S(1)}, bf16[2,64,512]{2,1,0:T(8,128)(2,1)S(1)}) custom-call(s32[4]{0:T(128)S(1)} %pad_add_fusion.place_ref, bf16[2,144,512]{2,1,0:T(8,128)(2,1)S(1)} %get-tuple-element.164.refs_0_, ...), custom_call_target="tpu_custom_call" | custom-call | flops 44000002048 | bytes 144000000 | tf_op jit(solution)/shard_map/far_forward/pallas_call | solution.py:1192
  125.7 5.4 %collective-permute-done.15.refs_1_ = bf16[1,2,2,64,384]{4,3,2,1,0:T(8,128)(2,1)S(1)} collective-permute-done((bf16[1,2,2,64,384]{4,3,2,1,0:T(8,128)(2,1)S(1)}, bf16[1,2,2,64,384]{4,3,2,1,0:T(8,128)(2,1)S(1)}, u32[]{:S(2)}, u32[]{:S(2)}) %collective-permute-start.15) | collective-permute-done | bytes 196640 | tf_op jit(solution)/shard_map/ppermute | solution.py:1212
  146.6 14.5 %mlp.2 = (bf16[2,1,128,768]{3,2,1,0:T(8,128)(2,1)}, f32[2,1,128,768]{3,2,1,0:T(8,128)}, bf16[1,2,1,64,768]{4,3,2,1,0:T(8,128)(2,1)}, bf16[1,2,1,64,768]{4,3,2,1,...) custom-call(s32[4]{0:T(128)} %copy-done.5, ...), custom_call_target="tpu_custom_call" | custom-call | flops 41250000896 | bytes 135000000 | tf_op jit(solution)/shard_map/mlp/pallas_call | solution.py:1192
  165.5 10.0 %collective-permute-done.23 = bf16[2,2,1,64,768]{4,3,1,0,2:T(8,128)(2,1)S(1)} collective-permute-done((bf16[2,2,1,64,768]{4,3,1,0,2:T(8,128)(2,1)S(1)}, bf16[2,2,1,64,768]{4,3,1,0,2:T(8,128)(2,1)S(1)}, u32[]{:S(2)}, u32[]{:S(2)}) %collective-permute-start.23) | collective-permute-done | bytes 393248 | tf_op jit(solution)/shard_map/ppermute | solution.py:1212
  176.2 24.4 %mlp.3 = (bf16[2,2,128,768]{3,2,1,0:T(8,128)(2,1)}, f32[2,2,128,768]{3,2,1,0:T(8,128)}, bf16[2,2,1,64,768]{4,3,2,1,0:T(8,128)(2,1)}, bf16[2,2,1,64,768]{4,3,2,1,...) custom-call(s32[4]{0:T(128)} %copy-done.5, ...), custom_call_target="tpu_custom_call" | custom-call | flops 68750000128 | bytes 225000000 | tf_op jit(solution)/shard_map/mlp/pallas_call | solution.py:1192
  205.4 10.4 %weight_grads.2 = (bf16[2,2,384,1024]{3,2,1,0:T(8,128)(2,1)}, bf16[2,2,384,768]{3,2,1,0:T(8,128)(2,1)}) custom-call(s32[4]{0:T(128)} %copy-done.5, bf16[768,256]{1,0:T(8,128)(2,1)} %get-tuple-element.190.refs_0_, bf16[768,256]{1,0:T(8,128)(2,1)} %get-tuple-element.191.refs_1_, bf16[768,256]{1,0:T(8,128)(2,1)} %get-tuple-element.192.refs_2_, ...), custom_call_target="tpu_custom_call" | custom-call | flops 32999999488 | bytes 108000000 | tf_op jit(solution)/shard_map/weight_grads/pallas_call | solution.py:1192
  220.0 3.7 collective-permute-done.25
  225.0 9.7 %near_backward.3.refs_2_.refs_0_ = bf16[4,2,144,512]{3,2,1,0:T(8,128)(2,1)S(1)} custom-call(s32[4]{0:T(128)S(1)} %copy-done.8, bf16[1,4,2,144,512]{4,3,2,1,0:T(8,128)(2,1)S(1)} %copy-done.63, f32[6,8,512]{2,1,0:T(8,128)S(1)} %reshape.328.refs_1_.refs_4_.refs_8_, bf16[1,4,2,64,512]{4,3,2,1,0:T(8,128)(2,1)S(1)} %get-tuple-element.209.refs_2_, ...), custom_call_target="tpu_custom_call" | custom-call | flops 26674999296 | bytes 87300000 | tf_op jit(solution)/shard_map/near_backward/pallas_call | solution.py:1192
  244.8 13.0 %weight_grads.3 = (bf16[2,384,1024]{2,1,0:T(8,128)(2,1)}, bf16[2,384,1024]{2,1,0:T(8,128)(2,1)}, bf16[2,384,768]{2,1,0:T(8,128)(2,1)}, bf16[2,384,768]{2,1,0:T(8,128)(2,1)}) custom-call(s32[4]{0:T(128)} %copy-done.5, bf16[768,256]{1,0:T(8,128)(2,1)} %get-tuple-element.190.refs_0_, bf16[768,256]{1,0:T(8,128)(2,1)} %get-tuple-element.191.refs_1_, ...), custom_call_target="tpu_custom_call" | custom-call | flops 32999999488 | bytes 108000000 | tf_op jit(solution)/shard_map/weight_grads/pallas_call | solution.py:1192
  260.0 9.7 %near_backward.4.refs_9_.refs_0_ = bf16[4,2,144,512]{3,2,1,0:T(8,128)(2,1)S(1)} custom-call(s32[4]{0:T(128)S(1)} %copy-done.9, bf16[2,4,2,144,512]{4,3,2,1,0:T(8,128)(2,1)S(1)} %copy-done.2, f32[6,8,512]{2,1,0:T(8,128)S(1)} %reshape.328.refs_1_.refs_4_.refs_8_, bf16[2,4,2,64,512]{4,3,2,1,0:T(8,128)(2,1)S(1)} %get-tuple-element.227.refs_2_, ...), custom_call_target="tpu_custom_call" | custom-call | flops 550000000 | bytes 1800000 | tf_op jit(solution)/shard_map/near_backward/pallas_call | solution.py:1192
  269.7 12.2 %far_backward.3 = (bf16[2,1,144,512]{3,2,1,0:T(8,128)(2,1)S(1)}, bf16[2,1,144,512]{3,2,1,0:T(8,128)(2,1)S(1)}) custom-call(s32[4]{0:T(128)S(1)} %copy-done.9, bf16[2,144,512]{2,1,0:T(8,128)(2,1)S(1)} %copy-done.81, bf16[2,144,512]{2,1,0:T(8,128)(2,1)S(1)} %copy-done.27, bf16[2,144,512]{2,1,0:T(8,128)(2,1)S(1)} %copy-done.29, ...), custom_call_target="tpu_custom_call" | custom-call | flops 8249999872 | bytes 27000000 | tf_op jit(solution)/shard_map/far_backward/pallas_call | solution.py:1192
  282.8 12.2 %far_backward.4 = (bf16[2,1,144,512]{3,2,1,0:T(8,128)(2,1)S(1)}, bf16[2,1,144,512]{3,2,1,0:T(8,128)(2,1)S(1)}) custom-call(s32[4]{0:T(128)S(1)} %copy-done.9, bf16[2,144,512]{2,1,0:T(8,128)(2,1)S(1)} %copy-done.81, bf16[2,144,512]{2,1,0:T(8,128)(2,1)S(1)} %copy-done.27, bf16[2,144,512]{2,1,0:T(8,128)(2,1)S(1)} %copy-done.29, ...), custom_call_target="tpu_custom_call" | custom-call | flops 8249999872 | bytes 27000000 | tf_op jit(solution)/shard_map/far_backward/pallas_call | solution.py:1192
  305.7 12.2 %far_backward.5 = (bf16[2,1,144,512]{3,2,1,0:T(8,128)(2,1)S(1)}, bf16[2,1,144,512]{3,2,1,0:T(8,128)(2,1)S(1)}) custom-call(s32[4]{0:T(128)S(1)} %copy-done.9, bf16[1,144,512]{2,1,0:T(8,128)(2,1)S(1)} %copy-done.79, bf16[1,144,512]{2,1,0:T(8,128)(2,1)S(1)} %copy-done.35, bf16[1,144,512]{2,1,0:T(8,128)(2,1)S(1)} %copy-done.37, ...), custom_call_target="tpu_custom_call" | custom-call | flops 8249999872 | bytes 27000000 | tf_op jit(solution)/shard_map/far_backward/pallas_call | solution.py:1192
  322.5 9.9 %near_backward.5.refs_4_.refs_1_ = bf16[4,2,144,512]{3,2,1,0:T(8,128)(2,1)S(1)} custom-call(s32[4]{0:T(128)S(1)} %copy-done.9, bf16[2,4,2,144,512]{4,3,2,1,0:T(8,128)(2,1)S(1)} %copy-done.2, f32[6,8,512]{2,1,0:T(8,128)S(1)} %reshape.328.refs_1_.refs_4_.refs_8_, bf16[2,4,2,64,512]{4,3,2,1,0:T(8,128)(2,1)S(1)} %get-tuple-element.227.refs_2_, ...), custom_call_target="tpu_custom_call" | custom-call | flops 550000000 | bytes 1800000 | tf_op jit(solution)/shard_map/near_backward/pallas_call | solution.py:1192
  334.3 4.6 %collective-permute-done.43.refs_7_.refs_9_ = bf16[2,1,144,512]{3,2,1,0:T(8,128)(2,1)S(1)} collective-permute-done((bf16[2,1,144,512]{3,2,1,0:T(8,128)(2,1)S(1)}, bf16[2,1,144,512]{3,2,1,0:T(8,128)(2,1)S(1)}, u32[]{:S(2)}, u32[]{:S(2)}) %collective-permute-start.43) | collective-permute-done | bytes 294944 | tf_op jit(solution)/shard_map/ppermute | solution.py:1212
  338.9 9.4 %qkv_backward.2 = (f32[576,768]{1,0:T(8,128)}, f32[8,576]{1,0:T(8,128)S(1)}, f32[8,768]{1,0:T(8,128)S(1)}, bf16[2,2,4,64,768]{4,3,2,1,0:T(8,128)(2,1)}, bf16[2,2,4,64,768]{4,3,2,1,0:T(8,128)(2,1)}) custom-call(s32[4]{0:T(128)S(1)} %copy-done.9, bf16[4,2,144,512]{3,2,1,0:T(8,128)(2,1)S(1)} %near_backward.4.refs_9_.refs_0_, ...), custom_call_target="tpu_custom_call" | custom-call | flops 22000001024 | bytes 72000000 | tf_op jit(solution)/shard_map/qkv_backward/pallas_call | solution.py:1192
  348.3 3.6 collective-permute-done.44.refs_1_
  357.7 5.6 %qkv_backward.3 = (bf16[384,640]{1,0:T(8,128)(2,1)S(1)}, bf16[384,640]{1,0:T(8,128)(2,1)S(1)}, f32[8,576]{1,0:T(8,128)S(1)}, f32[8,768]{1,0:T(8,128)S(1)}, bf16[...) custom-call(s32[4]{0:T(128)S(1)} %copy-done.9, bf16[4,2,144,512]{3,2,1,0:T(8,128)(2,1)} %copy-done.46, ...), custom_call_target="tpu_custom_call" | custom-call | flops 11000000512 | bytes 36000000 | tf_op jit(solution)/shard_map/qkv_backward/pallas_call | solution.py:1192
  370.2 13.5 %collective-permute-done.49.refs_1_ = bf16[2,2,2,64,768]{4,3,2,1,0:T(8,128)(2,1)S(1)} collective-permute-done((bf16[2,2,2,64,768]{4,3,2,1,0:T(8,128)(2,1)S(1)}, bf16[2,2,2,64,768]{4,3,2,1,0:T(8,128)(2,1)S(1)}, u32[]{:S(2)}, u32[]{:S(2)}) %collective-permute-start.49) | collective-permute-done | bytes 786464 | tf_op jit(solution)/shard_map/ppermute | solution.py:1212
  386.5 5.2 %collective-permute-done.46.refs_1_ = bf16[1,2,2,64,768]{4,3,2,1,0:T(8,128)(2,1)S(1)} collective-permute-done((bf16[1,2,2,64,768]{4,3,2,1,0:T(8,128)(2,1)S(1)}, bf16[1,2,2,64,768]{4,3,2,1,0:T(8,128)(2,1)S(1)}, u32[]{:S(2)}, u32[]{:S(2)}) %collective-permute-start.46) | collective-permute-done | bytes 393248 | tf_op jit(solution)/shard_map/ppermute | solution.py:1212
  399.1 3.9 leave.2
  409.8 8.4 %collective-permute-done.59.refs_1_ = bf16[96,1792]{1,0:T(8,128)(2,1)S(1)} collective-permute-done((bf16[96,1792]{1,0:T(8,128)(2,1)S(1)}, bf16[96,1792]{1,0:T(8,128)(2,1)S(1)}, u32[]{:S(2)}, u32[]{:S(2)}) %collective-permute-start.59) | collective-permute-done | bytes 344096 | tf_op jit(solution)/shard_map/ppermute | solution.py:1212
  (389 shorter events, 145.8 us)
Async XLA Ops:
  7.2 138.7 %all-gather.3.cloned.1.call-start = ((), (), s32[]{:S(2)}) async-start(), calls=%async_computation | async-start | bytes 13393920 | tf_op jit(solution)/shard_map/all_gather | solution.py:1502
  37.4 26.8 %collective-permute-start.8 = (bf16[2,2,2,64,768]{4,3,2,1,0:T(8,128)(2,1)}, bf16[2,2,2,64,768]{4,3,2,1,0:T(8,128)(2,1)S(1)}, u32[]{:S(2)}, u32[]{:S(2)}) collective-permute-start(bf16[2,2,2,64,768]{4,3,2,1,0:T(8,128)(2,1)} %copy-done.21), channel_id=1, source_target_pairs={{0,2},{1,3},{2,0},{3,1},{4,6},{5,7},{6,4},{7,5},{8,10},{9,11},{10,... | collective-permute-start | bytes 2359304 | tf_op jit(solution)/shard_map/ppermute | solution.py:1212
  68.3 21.1 %collective-permute-start.7 = (bf16[2,1,64,512]{3,2,1,0:T(8,128)(2,1)S(1)}, bf16[2,1,64,512]{3,2,1,0:T(8,128)(2,1)S(1)}, u32[]{:S(2)}, u32[]{:S(2)}) collective-permute-start(bf16[2,1,64,512]{3,2,1,0:T(8,128)(2,1)S(1)} %get-tuple-element.159.refs_2_), channel_id=1, source_target_pairs={{0,16},{4,20},{8,24},{12,28},{16,0},{20,4},{24,8},{28,12},{1,17},{... | collective-permute-start | bytes 393224 | tf_op jit(solution)/shard_map/ppermute | solution.py:1212
  76.1 27.3 %collective-permute-start.12 = (bf16[2,144,512]{2,1,0:T(8,128)(2,1)S(1)}, bf16[2,144,512]{2,1,0:T(8,128)(2,1)S(1)}, u32[]{:S(2)}, u32[]{:S(2)}) collective-permute-start(bf16[2,144,512]{2,1,0:T(8,128)(2,1)S(1)} %get-tuple-element.165), channel_id=1, source_target_pairs={{0,8},{4,12},{8,0},{12,4},{16,24},{20,28},{24,16},{28,20},{1,9},{5... | collective-permute-start | bytes 884744 | tf_op jit(solution)/shard_map/ppermute | solution.py:1212
  78.4 25.0 %collective-permute-start.13 = (bf16[2,144,512]{2,1,0:T(8,128)(2,1)S(1)}, bf16[2,144,512]{2,1,0:T(8,128)(2,1)S(1)}, u32[]{:S(2)}, u32[]{:S(2)}) collective-permute-start(bf16[2,144,512]{2,1,0:T(8,128)(2,1)S(1)} %get-tuple-element.166), channel_id=1, source_target_pairs={{0,16},{4,20},{8,24},{12,28},{16,0},{20,4},{24,8},{28,12},{1,17},{... | collective-permute-start | bytes 884744 | tf_op jit(solution)/shard_map/ppermute | solution.py:1212
  79.5 23.9 %collective-permute-start.14 = (bf16[2,144,512]{2,1,0:T(8,128)(2,1)S(1)}, bf16[2,144,512]{2,1,0:T(8,128)(2,1)S(1)}, u32[]{:S(2)}, u32[]{:S(2)}) collective-permute-start(bf16[2,144,512]{2,1,0:T(8,128)(2,1)S(1)} %get-tuple-element.161.refs_2_), channel_id=1, source_target_pairs={{0,24},{4,28},{8,16},{12,20},{16,8},{20,12},{24,0},{28,4},{1,25},{... | collective-permute-start | bytes 884744 | tf_op jit(solution)/shard_map/ppermute | solution.py:1212
  103.3 15.3 %collective-permute-start.11 = (bf16[1,2,4,64,192]{4,3,2,1,0:T(8,128)(2,1)S(1)}, bf16[1,2,4,64,192]{4,3,2,1,0:T(8,128)(2,1)S(1)}, u32[]{:S(2)}, u32[]{:S(2)}) collective-permute-start(bf16[1,2,4,64,192]{4,3,2,1,0:T(8,128)(2,1)S(1)} %get-tuple-element.163.refs_5_), channel_id=1, source_target_pairs={{0,1},{1,0},{2,3},{3,2},{4,5},{5,4},{6,7},{7,6},{8,9},{9,8},{10,11... | collective-permute-start | bytes 589832 | tf_op jit(solution)/shard_map/ppermute | solution.py:1212
  119.5 16.1 %collective-permute-start.19 = (bf16[2,64,512]{2,1,0:T(8,128)(2,1)S(1)}, bf16[2,64,512]{2,1,0:T(8,128)(2,1)S(1)}, u32[]{:S(2)}, u32[]{:S(2)}) collective-permute-start(bf16[2,64,512]{2,1,0:T(8,128)(2,1)S(1)} %get-tuple-element.167.refs_2_), channel_id=1, source_target_pairs={{0,24},{4,28},{8,16},{12,20},{16,8},{20,12},{24,0},{28,4},{1,25},{... | collective-permute-start | bytes 393224 | tf_op jit(solution)/shard_map/ppermute | solution.py:1212
  141.6 19.5 %collective-permute-start.22 = (bf16[2,2,2,64,384]{4,3,2,1,0:T(8,128)(2,1)S(1)}, bf16[2,2,2,64,384]{4,3,2,1,0:T(8,128)(2,1)S(1)}, u32[]{:S(2)}, u32[]{:S(2)}) collective-permute-start(bf16[2,2,2,64,384]{4,3,2,1,0:T(8,128)(2,1)S(1)} %get-tuple-element.178.refs_12_), channel_id=1, source_target_pairs={{0,2},{1,3},{2,0},{3,1},{4,6},{5,7},{6,4},{7,5},{8,10},{9,11},{10,... | collective-permute-start | bytes 1179656 | tf_op jit(solution)/shard_map/ppermute | solution.py:1212
  164.9 35.7 %collective-permute-start.21 = (bf16[1,2,1,64,768]{4,3,2,1,0:T(8,128)(2,1)S(1)}, bf16[1,2,1,64,768]{4,3,2,1,0:T(8,128)(2,1)S(1)}, u32[]{:S(2)}, u32[]{:S(2)}) collective-permute-start(bf16[1,2,1,64,768]{4,3,2,1,0:T(8,128)(2,1)S(1)} %copy-done.96), channel_id=1, source_target_pairs={{0,4},{4,0},{8,12},{12,8},{16,20},{20,16},{24,28},{28,24},{1,5},{5... | collective-permute-start | bytes 589832 | tf_op jit(solution)/shard_map/ppermute | solution.py:1212
  215.8 27.6 %collective-permute-start.33 = (bf16[2,2,384,768]{3,2,1,0:T(8,128)(2,1)}, bf16[2,2,384,768]{3,2,1,0:T(8,128)(2,1)S(1)}, u32[]{:S(2)}, u32[]{:S(2)}) collective-permute-start(bf16[2,2,384,768]{3,2,1,0:T(8,128)(2,1)} %get-tuple-element.202.refs_2_), channel_id=1, source_target_pairs={{0,1},{1,0},{2,3},{3,2},{4,5},{5,4},{6,7},{7,6},{8,9},{9,8},{10,11... | collective-permute-start | bytes 7077896 | tf_op jit(solution)/shard_map/ppermute | solution.py:1212
  215.9 29.0 %collective-permute-start.32 = (bf16[2,2,384,1024]{3,2,1,0:T(8,128)(2,1)}, bf16[2,2,384,1024]{3,2,1,0:T(8,128)(2,1)}, u32[]{:S(2)}, u32[]{:S(2)}) collective-permute-start(bf16[2,2,384,1024]{3,2,1,0:T(8,128)(2,1)} %get-tuple-element.222), channel_id=1, source_target_pairs={{0,1},{1,0},{2,3},{3,2},{4,5},{5,4},{6,7},{7,6},{8,9},{9,8},{10,11... | collective-permute-start | bytes 9437192 | tf_op jit(solution)/shard_map/ppermute | solution.py:1212
  238.9 30.7 %collective-permute-start.29 = (bf16[3,64,512]{2,1,0:T(8,128)(2,1)S(1)}, bf16[3,64,512]{2,1,0:T(8,128)(2,1)S(1)}, u32[]{:S(2)}, u32[]{:S(2)}) collective-permute-start(bf16[3,64,512]{2,1,0:T(8,128)(2,1)S(1)} %get-tuple-element.219), channel_id=1, source_target_pairs={{0,8},{4,12},{8,0},{12,4},{16,24},{20,28},{24,16},{28,20},{1,9},{5... | collective-permute-start | bytes 589832 | tf_op jit(solution)/shard_map/ppermute | solution.py:1212
  239.0 30.7 %collective-permute-start.30 = (bf16[3,64,512]{2,1,0:T(8,128)(2,1)S(1)}, bf16[3,64,512]{2,1,0:T(8,128)(2,1)S(1)}, u32[]{:S(2)}, u32[]{:S(2)}) collective-permute-start(bf16[3,64,512]{2,1,0:T(8,128)(2,1)S(1)} %get-tuple-element.220), channel_id=1, source_target_pairs={{0,16},{4,20},{8,24},{12,28},{16,0},{20,4},{24,8},{28,12},{1,17},{... | collective-permute-start | bytes 589832 | tf_op jit(solution)/shard_map/ppermute | solution.py:1212
  242.2 27.5 %collective-permute-start.31 = (bf16[3,64,512]{2,1,0:T(8,128)(2,1)S(1)}, bf16[3,64,512]{2,1,0:T(8,128)(2,1)S(1)}, u32[]{:S(2)}, u32[]{:S(2)}) collective-permute-start(bf16[3,64,512]{2,1,0:T(8,128)(2,1)S(1)} %get-tuple-element.221.refs_14_), channel_id=1, source_target_pairs={{0,24},{4,28},{8,16},{12,20},{16,8},{20,12},{24,0},{28,4},{1,25},{... | collective-permute-start | bytes 589832 | tf_op jit(solution)/shard_map/ppermute | solution.py:1212
  257.8 39.4 %collective-permute-start.35 = (bf16[2,384,768]{2,1,0:T(8,128)(2,1)}, bf16[2,384,768]{2,1,0:T(8,128)(2,1)S(1)}, u32[]{:S(2)}, u32[]{:S(2)}) collective-permute-start(bf16[2,384,768]{2,1,0:T(8,128)(2,1)} %get-tuple-element.226.refs_3_), channel_id=1, source_target_pairs={{0,2},{1,3},{2,0},{3,1},{4,6},{5,7},{6,4},{7,5},{8,10},{9,11},{10,... | collective-permute-start | bytes 3538952 | tf_op jit(solution)/shard_map/ppermute | solution.py:1212
  258.2 43.4 %collective-permute-start.34 = (bf16[2,384,1024]{2,1,0:T(8,128)(2,1)}, bf16[2,384,1024]{2,1,0:T(8,128)(2,1)S(1)}, u32[]{:S(2)}, u32[]{:S(2)}) collective-permute-start(bf16[2,384,1024]{2,1,0:T(8,128)(2,1)} %get-tuple-element.224), channel_id=1, source_target_pairs={{0,4},{4,0},{8,12},{12,8},{16,20},{20,16},{24,28},{28,24},{1,5},{5... | collective-permute-start | bytes 4718600 | tf_op jit(solution)/shard_map/ppermute | solution.py:1212
  281.9 36.4 %collective-permute-start.40 = (bf16[2,1,144,512]{3,2,1,0:T(8,128)(2,1)S(1)}, bf16[2,1,144,512]{3,2,1,0:T(8,128)(2,1)S(1)}, u32[]{:S(2)}, u32[]{:S(2)}) collective-permute-start(bf16[2,1,144,512]{3,2,1,0:T(8,128)(2,1)S(1)} %get-tuple-element.228.refs_9_), channel_id=1, source_target_pairs={{0,16},{4,20},{8,24},{12,28},{16,0},{20,4},{24,8},{28,12},{1,17},{... | collective-permute-start | bytes 884744 | tf_op jit(solution)/shard_map/ppermute | solution.py:1212
  295.0 26.9 %collective-permute-start.39 = (bf16[2,1,144,512]{3,2,1,0:T(8,128)(2,1)S(1)}, bf16[2,1,144,512]{3,2,1,0:T(8,128)(2,1)S(1)}, u32[]{:S(2)}, u32[]{:S(2)}) collective-permute-start(bf16[2,1,144,512]{3,2,1,0:T(8,128)(2,1)S(1)} %get-tuple-element.229.refs_2_), channel_id=1, source_target_pairs={{0,16},{4,20},{8,24},{12,28},{16,0},{20,4},{24,8},{28,12},{1,17},{... | collective-permute-start | bytes 884744 | tf_op jit(solution)/shard_map/ppermute | solution.py:1212
  300.1 32.2 %collective-permute-start.38 = (bf16[384,768]{1,0:T(8,128)(2,1)S(1)}, bf16[384,768]{1,0:T(8,128)(2,1)S(1)}, u32[]{:S(2)}, u32[]{:S(2)}) collective-permute-start(bf16[384,768]{1,0:T(8,128)(2,1)S(1)} %get-tuple-element.230.refs_2_), channel_id=1, source_target_pairs={{0,4},{4,0},{8,12},{12,8},{16,20},{20,16},{24,28},{28,24},{1,5},{5... | collective-permute-start | bytes 1769480 | tf_op jit(solution)/shard_map/ppermute | solution.py:1212
  304.0 28.4 %collective-permute-start.37 = (bf16[384,1024]{1,0:T(8,128)(2,1)S(1)}, bf16[384,1024]{1,0:T(8,128)(2,1)S(1)}, u32[]{:S(2)}, u32[]{:S(2)}) collective-permute-start(bf16[384,1024]{1,0:T(8,128)(2,1)S(1)} %get-tuple-element.231.refs_9_), channel_id=1, source_target_pairs={{0,2},{1,3},{2,0},{3,1},{4,6},{5,7},{6,4},{7,5},{8,10},{9,11},{10,... | collective-permute-start | bytes 2359304 | tf_op jit(solution)/shard_map/ppermute | solution.py:1212
  318.0 15.7 %collective-permute-start.36 = (bf16[2,1,144,512]{3,2,1,0:T(8,128)(2,1)S(1)}, bf16[2,1,144,512]{3,2,1,0:T(8,128)(2,1)S(1)}, u32[]{:S(2)}, u32[]{:S(2)}) collective-permute-start(bf16[2,1,144,512]{3,2,1,0:T(8,128)(2,1)S(1)} %get-tuple-element.233.refs_2_), channel_id=1, source_target_pairs={{0,16},{4,20},{8,24},{12,28},{16,0},{20,4},{24,8},{28,12},{1,17},{... | collective-permute-start | bytes 884744 | tf_op jit(solution)/shard_map/ppermute | solution.py:1212
  318.9 20.0 %collective-permute-start.42 = (bf16[2,1,144,512]{3,2,1,0:T(8,128)(2,1)S(1)}, bf16[2,1,144,512]{3,2,1,0:T(8,128)(2,1)S(1)}, u32[]{:S(2)}, u32[]{:S(2)}) collective-permute-start(bf16[2,1,144,512]{3,2,1,0:T(8,128)(2,1)S(1)} %pair.5.refs_2_), channel_id=1, source_target_pairs={{0,8},{4,12},{8,0},{12,4},{16,24},{20,28},{24,16},{28,20},{1,9},{5... | collective-permute-start | bytes 884744 | tf_op jit(solution)/shard_map/ppermute | solution.py:1212
  322.4 16.5 %collective-permute-start.43 = (bf16[2,1,144,512]{3,2,1,0:T(8,128)(2,1)S(1)}, bf16[2,1,144,512]{3,2,1,0:T(8,128)(2,1)S(1)}, u32[]{:S(2)}, u32[]{:S(2)}) collective-permute-start(bf16[2,1,144,512]{3,2,1,0:T(8,128)(2,1)S(1)} %pair.6.refs_3_), channel_id=1, source_target_pairs={{0,8},{4,12},{8,0},{12,4},{16,24},{20,28},{24,16},{28,20},{1,9},{5... | collective-permute-start | bytes 884744 | tf_op jit(solution)/shard_map/ppermute | solution.py:1212
  363.4 20.4 %collective-permute-start.49 = (bf16[2,2,2,64,768]{4,3,2,1,0:T(8,128)(2,1)S(1)}, bf16[2,2,2,64,768]{4,3,2,1,0:T(8,128)(2,1)S(1)}, u32[]{:S(2)}, u32[]{:S(2)}) collective-permute-start(bf16[2,2,2,64,768]{4,3,2,1,0:T(8,128)(2,1)S(1)} %get-tuple-element.244.refs_12_), channel_id=1, source_target_pairs={{0,2},{1,3},{2,0},{3,1},{4,6},{5,7},{6,4},{7,5},{8,10},{9,11},{10,... | collective-permute-start | bytes 2359304 | tf_op jit(solution)/shard_map/ppermute | solution.py:1212
  366.3 25.4 %collective-permute-start.46 = (bf16[1,2,2,64,768]{4,3,2,1,0:T(8,128)(2,1)S(1)}, bf16[1,2,2,64,768]{4,3,2,1,0:T(8,128)(2,1)S(1)}, u32[]{:S(2)}, u32[]{:S(2)}) collective-permute-start(bf16[1,2,2,64,768]{4,3,2,1,0:T(8,128)(2,1)S(1)} %get-tuple-element.253.refs_2_), channel_id=1, source_target_pairs={{0,2},{1,3},{2,0},{3,1},{4,6},{5,7},{6,4},{7,5},{8,10},{9,11},{10,... | collective-permute-start | bytes 1179656 | tf_op jit(solution)/shard_map/ppermute | solution.py:1212
  367.1 29.1 %collective-permute-start.52 = (bf16[192,1792]{1,0:T(8,128)(2,1)S(1)}, bf16[192,1792]{1,0:T(8,128)(2,1)S(1)}, u32[]{:S(2)}, u32[]{:S(2)}) collective-permute-start(bf16[192,1792]{1,0:T(8,128)(2,1)S(1)} %get-tuple-element.238.refs_2_), channel_id=1, source_target_pairs={{0,8},{4,12},{8,0},{12,4},{16,24},{20,28},{24,16},{28,20},{1,9},{5... | collective-permute-start | bytes 2064392 | tf_op jit(solution)/shard_map/ppermute | solution.py:1212
  367.3 25.0 %collective-permute-start.54 = (bf16[384,640]{1,0:T(8,128)(2,1)S(1)}, bf16[384,640]{1,0:T(8,128)(2,1)S(1)}, u32[]{:S(2)}, u32[]{:S(2)}) collective-permute-start(bf16[384,640]{1,0:T(8,128)(2,1)S(1)} %get-tuple-element.266), channel_id=1, source_target_pairs={{0,4},{4,0},{8,12},{12,8},{16,20},{20,16},{24,28},{28,24},{1,5},{5... | collective-permute-start | bytes 1474568 | tf_op jit(solution)/shard_map/ppermute | solution.py:1212
  368.4 17.1 %collective-permute-start.48 = (f32[16,768]{1,0:T(8,128)S(1)}, f32[16,768]{1,0:T(8,128)S(1)}, u32[]{:S(2)}, u32[]{:S(2)}) collective-permute-start(f32[16,768]{1,0:T(8,128)S(1)} %small_first.1.refs_2_.refs_0_), channel_id=1, source_target_pairs={{0,8},{4,12},{8,0},{12,4},{16,24},{20,28},{24,16},{28,20},{1,9},{5... | collective-permute-start | bytes 147464 | tf_op jit(solution)/shard_map/ppermute | solution.py:1212
  397.1 21.1 %collective-permute-start.59 = (bf16[96,1792]{1,0:T(8,128)(2,1)S(1)}, bf16[96,1792]{1,0:T(8,128)(2,1)S(1)}, u32[]{:S(2)}, u32[]{:S(2)}) collective-permute-start(bf16[96,1792]{1,0:T(8,128)(2,1)S(1)} %get-tuple-element.268.refs_6_), channel_id=1, source_target_pairs={{0,16},{4,20},{8,24},{12,28},{16,0},{20,4},{24,8},{28,12},{1,17},{... | collective-permute-start | bytes 1032200 | tf_op jit(solution)/shard_map/ppermute | solution.py:1212
  405.0 16.8 %collective-permute-start.58 = (bf16[96,640]{1,0:T(8,128)(2,1)S(1)}, bf16[96,640]{1,0:T(8,128)(2,1)S(1)}, u32[]{:S(2)}, u32[]{:S(2)}) collective-permute-start(bf16[96,640]{1,0:T(8,128)(2,1)S(1)} %get-tuple-element.272.refs_2_), channel_id=1, source_target_pairs={{0,16},{4,20},{8,24},{12,28},{16,0},{20,4},{24,8},{28,12},{1,17},{... | collective-permute-start | bytes 368648 | tf_op jit(solution)/shard_map/ppermute | solution.py:1212
  406.7 18.3 %collective-permute-start.57 = (f32[8,768]{1,0:T(8,128)S(1)}, f32[8,768]{1,0:T(8,128)S(1)}, u32[]{:S(2)}, u32[]{:S(2)}) collective-permute-start(f32[8,768]{1,0:T(8,128)S(1)} %get-tuple-element.273.refs_8_), channel_id=1, source_target_pairs={{0,2},{1,3},{2,0},{3,1},{4,6},{5,7},{6,4},{7,5},{8,10},{9,11},{10,... | collective-permute-start | bytes 73736 | tf_op jit(solution)/shard_map/ppermute | solution.py:1212
  (127 other events, 1225.8 us)
Sparse Core Ops, SparseCore 0:
  68.3 76.1 all-gather.2
